TPU v7x, 512 devices: a whole 4x4x16 slice. The times are simulated.
512 devices in a mesh: seq: 32 (over x, z_lo, core), head: 16 (over y, z_hi).
Axes of the slice: x: 4, y: 4, z: 16 (z_hi: 4, z_lo: 4; z = z_hi * 4 + z_lo), core: 2. Of those that a mesh axis runs over, the one named last changes fastest.
Arguments:
- head_inputs: bfloat16 [2, 4096, 8192], P(None, 'seq', 'head'), may hold values from -6 to 6
- gate_inputs: bfloat16 [2, 4096, 8192], P(None, 'seq', 'head'), may hold values from -400 to 400
- write_vectors: bfloat16 [2, 4096, 8, 128], P(None, 'seq'), may hold values from -0.5 to 0.5
- read_vectors: bfloat16 [2, 4096, 8, 128], P(None, 'seq'), may hold values from -6 to 6
- step_sizes: float32 [2, 128, 4096], P(None, 'head', 'seq'), may hold values from 0.03 to 1, as said below
- decay_logs: float32 [128], P('head'), may hold values from -12 to 0
- skip_scale: float32 [128], P('head'), may hold values from 0.5 to 2
- norm_gain: float32 [8192], P('head'), may hold values from 0.1 to 1.9
- out_weight: bfloat16 [8192, 8192], P('head', 'seq'), may hold values from -0.0625 to 0.0625
- boundary: int32 [2], replicated, may hold values from 1024 to 3071
Outputs:
- mixed: bfloat16 [2, 4096, 8192], P(None, 'seq', 'head')
Inputs may be any that keep to these rules, and one draw needn't show every extreme that they name: `boundary`: the first position of trajectory B; positions before it belong to trajectory A. `step_sizes`: positive.
All inputs are finite; a program needn't handle non-finite values.
Results may differ from a plain program's by a relative error of at most 0.024.
Values may be sent and summed in bfloat16 or wider, within the bound.
No kernel may reach another device: no remote copies, remote signals or barrier semaphores. Data moves between devices by JAX's collectives and lax.ppermute only.
A program may use at most 128 MiB of HBM per device.

v0:
```python
import jax
import jax.numpy as jnp
from jax import lax
from jax.sharding import PartitionSpec as P

HEADS = 128
GROUPS = 8
INNER = 8192


epsilon = 1e-05


def prefix(value, axis, combine, identity):
    devices, mine = (lax.axis_size(axis), lax.axis_index(axis))
    everything = jax.tree.map(
        lambda part, kind: lax.all_gather(part.astype(kind), axis),
        value,
        (jnp.bfloat16, jnp.bfloat16),
    )
    start = jax.tree.map(
        lambda part, zero: jnp.broadcast_to(jnp.asarray(zero, part.dtype), part.shape),
        value,
        identity,
    )

    def lap(k, before):
        reached = k < mine
        new = combine(
            before, jax.tree.map(lambda part, own: part[k].astype(own.dtype), everything, value)
        )
        return jax.tree.map(lambda a, b: jnp.where(reached, a, b), new, before)

    return lax.fori_loop(0, devices, lap, start)


def combine(earlier, later):
    return (earlier[0] * later[0], later[0][..., None, None] * earlier[1] + later[1])


def finish(
    intra, skip_part, block_state, passing, factor, reads_wide, gates, norm_gain, whole_weight
):
    identity = (jnp.ones_like(passing), jnp.zeros_like(block_state))
    _, incoming = prefix((passing, block_state), "seq", combine, identity)
    carry = jnp.einsum("pign,pglnd->pigld", reads_wide, incoming, precision=lax.Precision.HIGHEST)
    ssm = intra + carry * factor + skip_part
    pair_count, block_len = (ssm.shape[0], ssm.shape[1])
    gated = ssm.reshape(pair_count, block_len, -1) * jax.nn.silu(gates.astype(jnp.float32))
    squares = lax.psum(jnp.sum(gated * gated, axis=-1), "head")
    hidden = (gated * lax.rsqrt(squares / INNER + epsilon)[..., None] * norm_gain).astype(
        jnp.bfloat16
    )
    flat = hidden.reshape(pair_count * block_len, -1)
    share = whole_weight.shape[1] // lax.axis_size("head")
    summed = lax.psum_scatter(
        lax.dot_general(
            whole_weight, flat, (((0,), (1,)), ((), ())), preferred_element_type=jnp.float32
        ).astype(jnp.bfloat16),
        "head",
        scatter_dimension=0,
        tiled=True,
    ).astype(jnp.float32)
    return summed.T.astype(jnp.bfloat16).reshape(pair_count, block_len, share)


def shards(
    head_inputs,
    gate_inputs,
    write_vectors,
    read_vectors,
    step_sizes,
    decay_logs,
    skip_scale,
    norm_gain,
    out_weight,
    boundary,
):
    pair_count, block_len, inner_local = head_inputs.shape
    heads_local = step_sizes.shape[1]
    per_group_all = HEADS // GROUPS
    local_groups = max(1, heads_local // per_group_all)
    per_group = heads_local // local_groups
    channels = inner_local // heads_local
    whole_weight = lax.all_gather(out_weight, "seq", axis=1, tiled=True)
    first = lax.axis_index("seq") * block_len
    first_group = lax.axis_index("head") * heads_local // per_group_all
    reads = lax.dynamic_slice_in_dim(read_vectors, first_group, local_groups, 2)
    writes = lax.dynamic_slice_in_dim(write_vectors, first_group, local_groups, 2)
    position = first + jnp.arange(block_len, dtype=jnp.int32)
    parts = (position[None, :] >= boundary[:, None]).astype(jnp.float32)
    previous = (first - 1 >= boundary).astype(jnp.float32)
    rates = jnp.exp(decay_logs)
    cumul = jnp.cumsum(-rates[None, :, None] * step_sizes, axis=-1)
    lower = jnp.arange(block_len)[:, None] >= jnp.arange(block_len)[None, :]
    same = (parts[:, :, None] == parts[:, None, :]) & lower
    diffs = cumul[..., :, None] - cumul[..., None, :]
    decay = jnp.where(same[:, None], jnp.exp(jnp.minimum(diffs, 0.0)), 0.0)
    decay = decay.reshape(pair_count, local_groups, per_group, block_len, block_len)
    inputs = head_inputs.reshape(pair_count, block_len, local_groups, per_group, channels)
    scores = jnp.einsum("pign,pjgn->pgij", reads, writes, preferred_element_type=jnp.float32)
    step_group = step_sizes.reshape(pair_count, local_groups, per_group, 1, block_len)
    mixing = (scores[:, :, None] * decay * step_group).astype(jnp.bfloat16)
    intra = jnp.einsum("pglij,pjgld->pigld", mixing, inputs, preferred_element_type=jnp.float32)
    ends = jnp.where(parts[:, -1:] == parts, 1.0, 0.0)
    end_weights = jnp.exp(cumul[..., -1:] - cumul) * ends[:, None] * step_sizes
    end_weights = end_weights.reshape(pair_count, local_groups, per_group, block_len).transpose(
        0, 3, 1, 2
    )
    weighted = (writes[:, :, :, None, :] * end_weights[..., None]).astype(jnp.bfloat16)
    block_state = jnp.einsum(
        "pjgln,pjgld->pglnd", weighted, inputs, preferred_element_type=jnp.float32
    )
    passing = jnp.exp(cumul[..., -1]) * (parts[:, -1] == previous).astype(jnp.float32)[:, None]
    passing = passing.reshape(pair_count, local_groups, per_group)
    factor = jnp.exp(cumul) * (parts == previous[:, None]).astype(jnp.float32)[:, None]
    factor = factor.reshape(pair_count, local_groups, per_group, block_len).transpose(0, 3, 1, 2)[
        ..., None
    ]
    skip_part = skip_scale.reshape(local_groups, per_group)[:, :, None] * inputs
    reads_wide = reads.astype(jnp.float32)
    return finish(
        intra,
        skip_part,
        block_state,
        passing,
        factor,
        reads_wide,
        gate_inputs,
        norm_gain,
        whole_weight,
    )


def solution(mesh):
    return jax.shard_map(
        shards,
        mesh=mesh,
        in_specs=(
            P(None, "seq", "head"),
            P(None, "seq", "head"),
            P(None, "seq", None, None),
            P(None, "seq", None, None),
            P(None, "head", "seq"),
            P("head"),
            P("head"),
            P("head"),
            P("head", "seq"),
            P(),
        ),
        out_specs=P(None, "seq", "head"),
        check_vma=False,
    )
```

profile of v0, /device:TPU:1, one launch (start us, length us, event | category | flops | bytes accessed | tf_op | source)
XLA Modules:
  0.0 366.8 jit_solution(14442289711344321184)
XLA Ops:
  6.5 1.5 constant_dynamic-slice_fusion.1
  8.0 0.7 compare_convert_fusion.3
  9.0 0.7 compare_select_fusion
  9.7 0.7 exponential_negate_fusion
  10.3 0.8 broadcast_multiply_fusion
  11.1 0.6 reduce_window_sum.11
  11.9 1.1 copy.52
  13.0 0.8 multiply_bitcast_fusion
  13.8 1.2 convolution_convert_fusion.1
  15.1 0.7 all-gather.4.cloned.1.call-update
  15.9 1.1 copy.55
  16.9 0.7 compare_convert_fusion.1
  17.7 45.5 %all_gather.13 = bf16[32,2,1,8]{3,1,2,0:T(2,128)(2,1)S(1)} all-gather(bf16[1,2,1,8]{3,1,2,0:T(2,128)(2,1)S(1)} %fusion.25), channel_id=1, replica_groups=mesh['seq'=32,'head'=16] {'seq'}, dimensions={0}, use_global_device_ids=true | all-gather | bytes 1056 | tf_op jit(solution)/shard_map/all_gather | solution.py:17
  63.2 0.7 compare_convert_fusion
  64.2 30.9 %all-gather.6.cloned.1.call-done = bf16[64,8,128,64]{2,3,1,0:T(8,128)(2,1)} async-done(((bf16[2,8,128,64]{2,3,1,0:T(8,128)(2,1)}), bf16[64,8,128,64]{2,3,1,0:T(8,128)(2,1)}) %all-gather.6.cloned.1.call-update) | async-done | bytes 8388624 | tf_op jit(solution)/shard_map/all_gather | solution.py:17
  95.2 54.9 %while.14 = (s32[]{:T(128)}, f32[2,1,8,128,64]{4,3,2,1,0:T(8,128)S(1)}, s32[]{:T(128)}, bf16[32,2,1,8]{3,1,2,0:T(2,128)(2,1)S(1)}, bf16[32,2,1,8,128,64]{4,5,3,1,0,2:T(8,128)(2,1)}, /*index=5*/s32[]{:T(128)}, s32[]{:T(128)}) while((s32[]{:T(128)}, f32[2,1,8,128,64]{4,3,2,1,0:T(8,128)S(1)}, s32[]{:T(128)}, ...), condition=%wide.region_2.3_spmd.clone, body=%wide.region_1.2_spmd.clone.sunk | while | flops 655380 | bytes 2359561 | solution.py:34
  95.2 1.0 constant_dynamic-slice_fusion.4
  96.5 0.4 fusion.32
  96.9 1.0 constant_dynamic-slice_fusion.4
  98.2 0.4 fusion.32
  98.6 1.0 constant_dynamic-slice_fusion.4
  99.9 0.4 fusion.32
  100.3 1.0 constant_dynamic-slice_fusion.4
  101.6 0.4 fusion.32
  102.1 1.0 constant_dynamic-slice_fusion.4
  103.3 0.4 fusion.32
  103.8 1.0 constant_dynamic-slice_fusion.4
  105.1 0.4 fusion.32
  105.5 1.0 constant_dynamic-slice_fusion.4
  106.8 0.4 fusion.32
  107.2 1.0 constant_dynamic-slice_fusion.4
  108.5 0.4 fusion.32
  108.9 1.0 constant_dynamic-slice_fusion.4
  110.2 0.4 fusion.32
  110.6 1.0 constant_dynamic-slice_fusion.4
  112.3 1.0 constant_dynamic-slice_fusion.4
  114.1 1.0 constant_dynamic-slice_fusion.4
  115.8 1.0 constant_dynamic-slice_fusion.4
  117.5 1.0 constant_dynamic-slice_fusion.4
  119.2 1.0 constant_dynamic-slice_fusion.4
  120.9 1.0 constant_dynamic-slice_fusion.4
  122.2 0.4 fusion.32
  122.6 1.0 constant_dynamic-slice_fusion.4
  124.4 1.0 constant_dynamic-slice_fusion.4
  126.1 1.0 constant_dynamic-slice_fusion.4
  127.8 1.0 constant_dynamic-slice_fusion.4
  129.5 1.0 constant_dynamic-slice_fusion.4
  131.2 1.0 constant_dynamic-slice_fusion.4
  132.9 1.0 constant_dynamic-slice_fusion.4
  134.6 1.0 constant_dynamic-slice_fusion.4
  136.3 1.0 constant_dynamic-slice_fusion.4
  138.1 1.0 constant_dynamic-slice_fusion.4
  139.8 1.0 constant_dynamic-slice_fusion.4
  141.5 1.0 constant_dynamic-slice_fusion.4
  142.8 0.4 fusion.32
  143.2 1.0 constant_dynamic-slice_fusion.4
  144.9 1.0 constant_dynamic-slice_fusion.4
  146.6 1.0 constant_dynamic-slice_fusion.4
  148.3 1.0 constant_dynamic-slice_fusion.4
  150.1 1.0 fusion.4
  151.1 0.6 fusion.3
  152.1 46.9 %psum.7 = f32[2,128]{1,0:T(2,128)S(1)} all-reduce(f32[2,128]{1,0:T(2,128)S(1)} %multiply_reduce_fusion), channel_id=1, replica_groups=mesh['seq'=32,'head'=16] {'head'}, use_global_device_ids=true, to_apply=%region_4.5 | all-reduce | flops 256 | bytes 2048 | tf_op jit(solution)/shard_map/psum | solution.py:50
  199.2 7.7 %fusion.1 = bf16[8192,256]{0,1:T(8,128)(2,1)} fusion(bf16[256,512]{1,0:T(8,128)(2,1)S(1)} %bitcast.78, bf16[512,8192]{1,0:T(8,128)(2,1)} %all-gather.4.cloned.1.call-done), kind=kOutput, calls=%fused_computation.5 | convolution fusion | flops 2149580800 | bytes 12845056 | tf_op jit(solution)/shard_map/dot_general | solution.py:57
  206.9 153.4 %reduce-scatter.2.cloned.1.call-done = bf16[512,256]{0,1:T(8,128)(2,1)} async-done(((bf16[8192,256]{0,1:T(8,128)(2,1)}), bf16[512,256]{0,1:T(8,128)(2,1)}) %reduce-scatter.2.cloned.1.call-update) | async-done | bytes 262160 | tf_op jit(solution)/shard_map/reduce_scatter | solution.py:56
  (113 shorter events, 19.4 us)
Async XLA Ops:
  6.5 88.6 %all-gather.6.cloned.1.call-start = ((), (), s32[]{:S(2)}) async-start(), calls=%async_computation.3 | async-start | bytes 8650752 | tf_op jit(solution)/shard_map/all_gather | solution.py:17
  15.0 184.2 %all-gather.4.cloned.1.call-start = ((), (), s32[]{:S(2)}) async-start(), calls=%async_computation.1 | async-start | bytes 8650752 | tf_op jit(solution)/shard_map/all_gather | solution.py:85
  15.8 344.5 %reduce-scatter.2.cloned.1.call-start = ((), (), s32[]{:S(2)}) async-start(), calls=%async_computation.2 | async-start | bytes 4456448 | tf_op jit(solution)/shard_map/reduce_scatter | solution.py:56
  95.1 55.9 %copy-start.1 = (f32[2,8,128]{2,1,0:T(8,128)S(1)}, f32[2,8,128]{2,1,0:T(8,128)}, u32[]{:S(2)}) copy-start(f32[2,8,128]{2,1,0:T(8,128)} %param.16) | copy-start | bytes 24580
  95.1 55.9 %copy-start.3 = (f32[8]{0:T(128)S(1)}, f32[8]{0:T(128)}, u32[]{:S(2)}) copy-start(f32[8]{0:T(128)} %param.18) | copy-start | bytes 100
  95.2 56.7 %copy-start = (bf16[2,128,512]{2,1,0:T(8,128)(2,1)S(1)}, bf16[2,128,512]{2,1,0:T(8,128)(2,1)}, u32[]{:S(2)}) copy-start(bf16[2,128,512]{2,1,0:T(8,128)(2,1)} %param.13) | copy-start | bytes 786436
  95.2 103.8 %copy-start.2 = (f32[512]{0:T(512)S(1)}, f32[512]{0:T(512)}, u32[]{:S(2)}) copy-start(f32[512]{0:T(512)} %param.19) | copy-start | bytes 6148
Sparse Core Ops, SparseCore 0:
  15.1 79.9 all-gather.5
  97.2 93.0 all-gather.3
  207.1 153.2 reduce-scatter.1
where the time goes:
time: 368 us; the launch traced here: 367 us
  waiting for transfers between devices  185 us (50%)
  blocking collectives  92.3 us (25%)
  local copies, waits for them, and re-layouts  44.6 us (12%)
  other arithmetic  19.4 us (5%)
  between operations  13.3 us (4%)
  matrix products  10.7 us (3%)
    reduce_scatter x1, waiting for transfers between devices, finish(): lax.psum_scatter(lax.dot_general(whole_weight, flat, (((0,), (1,)), ((),...  153 us
    psum x1, blocking collectives, finish(): squares = lax.psum(jnp.sum(gated * gated, axis=-1), 'head')  46.9 us
    all_gather x1, blocking collectives, prefix(): lax.all_gather(part.astype(kind), axis)  45.5 us
    dynamic_slice x64, local copies, waits for them, and re-layouts, lap(): part[k].astype(own.dtype)  40.4 us
    all_gather x1, waiting for transfers between devices, prefix(): lax.all_gather(part.astype(kind), axis)  30.9 us
    select_n x32, other arithmetic, lap(): return jax.tree.map(lambda a, b: jnp.where(reached, a, b), new, before)  12.8 us
    dot_general x1, matrix products, finish(): lax.dot_general(whole_weight, flat, (((0,), (1,)), ((), ())), preferred_e...  7.71 us
  transfers between devices with their start and end apart: 3, of which 2 were waited for; matrix products, arithmetic and copies ran while one was open for 16% of the time, Pallas kernels for 0%

commit v1 on v0

v1 whole, which is shorter than its diff:
```python
import jax
import jax.numpy as jnp
from jax import lax
from jax.experimental import pallas as pl
from jax.experimental.pallas import tpu as pltpu
from jax.sharding import PartitionSpec as P

INNER = 8192
EPSILON = 1e-05
PAIRS = 2
SPAN = 128
HEADS_LOCAL = 8
HALF = 4
CHANNELS = 64
STATE = 128
WIDTH = 512
TOKENS = PAIRS * SPAN
STATE_ROWS = PAIRS * HALF * CHANNELS
PAYLOAD_ROWS = STATE_ROWS + 16
TOKEN_ROWS = TOKENS + 16
NX = NZL = NCORE = NY = NZH = 4
NCORE = 2
EXACT = lax.Precision.HIGHEST
f32 = jnp.float32
bf16 = jnp.bfloat16


def seq_index(x, zl, core):
    return (x * NZL + zl) * NCORE + core


def head_index(y, zh):
    return y * NZH + zh


def route(move):
    pairs = []
    for x in range(NX):
        for zl in range(NZL):
            for core in range(NCORE):
                for y in range(NY):
                    for zh in range(NZH):
                        to = move(x, zl, core, y, zh)
                        if to is None:
                            continue
                        source = seq_index(x, zl, core) * NY * NZH + head_index(y, zh)
                        target = seq_index(*to[:3]) * NY * NZH + head_index(*to[3:])
                        pairs.append((source, target))
    return pairs


def send(value, move):
    return lax.ppermute(value, ("seq", "head"), route(move))


def to_core(value):
    return send(value, lambda x, zl, c, y, zh: (x, zl, 1 - c, y, zh))


def to_zl(value, d):
    return send(value, lambda x, zl, c, y, zh: (x, (zl + d) % NZL, c, y, zh))


def to_x(value, d):
    return send(value, lambda x, zl, c, y, zh: (x + d, zl, c, y, zh) if x + d < NX else None)


def to_y(value, d):
    return send(value, lambda x, zl, c, y, zh: (x, zl, c, (y + d) % NY, zh))


def to_zh(value, d):
    return send(value, lambda x, zl, c, y, zh: (x, zl, c, y, (zh + d) % NZH))


def swap_z(value):
    return send(value, lambda x, zl, c, y, zh: (x, zh, c, y, zl))


VMEM = pl.BlockSpec(memory_space=pltpu.VMEM)
SMEM = pl.BlockSpec(memory_space=pltpu.SMEM)


def call(kernel, outs, specs, args, flops, moved, limit=None):
    return pl.pallas_call(
        kernel,
        out_shape=outs,
        in_specs=specs,
        out_specs=jax.tree.map(lambda _: VMEM, outs),
        cost_estimate=pl.CostEstimate(flops=flops, bytes_accessed=moved, transcendentals=0),
        compiler_params=pltpu.CompilerParams(vmem_limit_bytes=limit or 16 * 2**20),
    )(*args)


def shape(dims, kind):
    return jax.ShapeDtypeStruct(dims, kind)


def head_rows(scalars):
    rows = lax.broadcasted_iota(jnp.int32, (HEADS_LOCAL, SPAN), 0)
    out = jnp.zeros((HEADS_LOCAL, SPAN), f32)
    for h in range(HEADS_LOCAL):
        out = jnp.where(rows == h, scalars[h], out)
    return out


def split(value):
    high = value.astype(bf16)
    low = (value - high.astype(f32)).astype(bf16)
    return high, low


def flag(condition):
    return jnp.where(condition, 1.0, 0.0).astype(f32)


def states_kernel(meta, decay_logs, x, writes, steps, out, mine, decay_mine):
    first, core = meta[0], meta[1]
    rates = jnp.exp(head_rows(decay_logs))
    row = lax.broadcasted_iota(jnp.int32, (SPAN, SPAN), 0)
    col = lax.broadcasted_iota(jnp.int32, (SPAN, SPAN), 1)
    upto = jnp.where(row <= col, 1.0, 0.0).astype(f32)
    position = first + lax.broadcasted_iota(jnp.int32, (HEADS_LOCAL, SPAN), 1)
    send_decay, keep_decay = [], []
    rows = HALF * CHANNELS
    for p in range(PAIRS):
        limit = meta[2 + p]
        step = steps[p]
        cumul = jnp.dot(-rates * step, upto, precision=EXACT, preferred_element_type=f32)
        last = cumul[:, SPAN - 1 :]
        last_part = jnp.where(first + SPAN - 1 >= limit, 1, 0)
        previous = jnp.where(first - 1 >= limit, 1, 0)
        part = jnp.where(position >= limit, 1, 0)
        ends = jnp.exp(last - cumul) * step
        ends = jnp.where(part == last_part, ends, 0.0)
        spread = jnp.broadcast_to(ends[:, None, :], (HEADS_LOCAL, CHANNELS, SPAN))
        spread = spread.reshape(HEADS_LOCAL * CHANNELS, SPAN)
        turned = x[p].astype(f32).T
        state = jnp.dot(
            (turned * spread).astype(bf16), writes[p], preferred_element_type=f32
        )
        passing = jnp.broadcast_to(jnp.exp(last), (HEADS_LOCAL, SPAN))
        passing = jnp.where(last_part == previous, passing, 0.0)
        here = pl.ds(p * rows, rows)
        lower, upper = state[:rows], state[rows:]
        out[here, :] = jnp.where(core == 0, upper, lower).astype(bf16)
        mine[here, :] = jnp.where(core == 0, lower, upper)
        send_decay.append(jnp.where(core == 0, passing[HALF:], passing[:HALF]))
        keep_decay.append(jnp.where(core == 0, passing[:HALF], passing[HALF:]))
    leaving = jnp.concatenate(send_decay, axis=0)
    high = leaving.astype(bf16).astype(f32)
    out[pl.ds(STATE_ROWS, 16), :] = jnp.concatenate([high, leaving - high], axis=0).astype(bf16)
    decay_mine[...] = jnp.concatenate(keep_decay, axis=0)


def unpack(ref):
    tail = ref[pl.ds(STATE_ROWS, 16), :].astype(f32)
    return tail[:8] + tail[8:], ref[pl.ds(0, STATE_ROWS), :].astype(f32)


def scale(decay, state):
    groups = PAIRS * HALF
    return (state.reshape(groups, CHANNELS, STATE) * decay[:, None, :]).reshape(STATE_ROWS, STATE)


def pack(out, decay, state):
    out[pl.ds(0, STATE_ROWS), :] = state.astype(bf16)
    high = decay.astype(bf16).astype(f32)
    out[pl.ds(STATE_ROWS, 16), :] = jnp.concatenate([high, decay - high], axis=0).astype(bf16)


def chip_kernel(meta, got, mine, decay_mine, total, state_first, decay_first):
    core = meta[1]
    decay_got, state_got = unpack(got)
    decay_own, state_own = decay_mine[...], mine[...]
    decay0 = jnp.where(core == 0, decay_own, decay_got)
    decay1 = jnp.where(core == 0, decay_got, decay_own)
    state0 = jnp.where(core == 0, state_own, state_got)
    state1 = jnp.where(core == 0, state_got, state_own)
    state_first[...] = state0
    decay_first[...] = decay0
    pack(total, decay0 * decay1, scale(decay1, state0) + state1)


def line_kernel(meta, own, from1, from2, from3, total, state_before, decay_before):
    zl = meta[4]
    state = jnp.zeros((STATE_ROWS, STATE), f32)
    decay = jnp.ones((PAIRS * HALF, STATE), f32)

    def follow(decay, state, ref, valid):
        factor, fresh = unpack(ref)
        factor = jnp.where(valid, factor, 1.0)
        fresh = jnp.where(valid, fresh, 0.0)
        return decay * factor, scale(factor, state) + fresh

    apart = ((3, from3), (2, from2), (1, from1))
    for d, ref in apart:
        decay, state = follow(decay, state, ref, zl >= d)
    state_before[...] = state
    decay_before[...] = decay
    factor, fresh = unpack(own)
    decay, state = decay * factor, scale(factor, state) + fresh
    for d, ref in apart:
        decay, state = follow(decay, state, ref, zl < d)
    pack(total, decay, state)


def whole_kernel(
    meta, from1, from2, from3, state_before, decay_before, state_first, decay_first, out, keep
):
    core = meta[1]
    state = jnp.zeros((STATE_ROWS, STATE), f32)
    for ref in (from3, from2, from1):
        factor, fresh = unpack(ref)
        state = scale(factor, state) + fresh
    entering = scale(decay_before[...], state) + state_before[...]
    second = scale(decay_first[...], entering) + state_first[...]
    out[...] = jnp.where(core == 0, second, entering).astype(bf16)
    keep[...] = jnp.where(core == 0, entering, second).astype(bf16)


def inside_kernel(
    meta, decay_logs, skip_scale, x, writes, reads, steps, gates, early, late
):
    first = meta[0]
    rates = jnp.exp(head_rows(decay_logs))
    row = lax.broadcasted_iota(jnp.int32, (SPAN, SPAN), 0)
    col = lax.broadcasted_iota(jnp.int32, (SPAN, SPAN), 1)
    upto = jnp.where(row <= col, 1.0, 0.0).astype(f32)
    below = jnp.where(row >= col, 1.0, 0.0).astype(f32)
    for p in range(PAIRS):
        limit = meta[2 + p]
        step = steps[p]
        drop = -rates * step
        cumul = jnp.dot(drop, upto, precision=EXACT, preferred_element_type=f32)
        turned = lax.dot_general(
            below, drop, (((1,), (1,)), ((), ())), precision=EXACT, preferred_element_type=f32
        )
        part_row = jnp.where(first + row >= limit, 1, 0)
        part_col = jnp.where(first + col >= limit, 1, 0)
        previous = jnp.where(first - 1 >= limit, 1, 0)
        allowed = (part_row == part_col) & (row >= col)
        scores = lax.dot_general(
            reads[p], writes[p], (((1,), (1,)), ((), ())), preferred_element_type=f32
        )
        scores = jnp.where(allowed, scores, 0.0)
        reached = jnp.where(part_row[:, :CHANNELS] == previous, 1.0, 0.0)
        for h in range(HEADS_LOCAL):
            here = slice(h * CHANNELS, (h + 1) * CHANNELS)
            column = turned[:, h : h + 1]
            decay = jnp.exp(jnp.minimum(column - cumul[h : h + 1, :], 0.0))
            weights = (scores * decay * step[h : h + 1, :]).astype(bf16)
            inputs = x[p, :, here]
            intra = jnp.dot(weights, inputs, preferred_element_type=f32)
            ssm = intra + skip_scale[h] * inputs.astype(f32)
            gate = gates[p, :, here].astype(f32)
            opened = gate / (1.0 + jnp.exp(-gate))
            early[p, :, here] = ssm * opened
            late[p, :, here] = opened * reached * jnp.exp(column)


def hidden_kernel(meta, keep, got, reads, early, late, gain, out):
    core = meta[1]
    rows = HALF * CHANNELS
    ones = jnp.ones((8, WIDTH), f32)
    highs, lows = [], []
    for p in range(PAIRS):
        here = pl.ds(p * rows, rows)
        own, other = keep[here, :], got[here, :]
        total = jnp.zeros((8, SPAN), f32)
        for half in range(2):
            state = jnp.where(core == half, own, other)
            columns = slice(half * rows, (half + 1) * rows)
            carry = lax.dot_general(
                reads[p], state, (((1,), (1,)), ((), ())), preferred_element_type=f32
            )
            gated = early[p, :, columns] + late[p, :, columns] * carry
            out[pl.ds(p * SPAN, SPAN), columns] = (gated * gain[:, columns]).astype(bf16)
            total += lax.dot_general(
                ones[:, columns],
                gated * gated,
                (((1,), (1,)), ((), ())),
                precision=EXACT,
                preferred_element_type=f32,
            )
        high = total.astype(bf16).astype(f32)
        highs.append(high)
        lows.append(total - high)
    squares = jnp.concatenate(highs + lows, axis=1)
    out[pl.ds(TOKENS, 16), :] = jnp.concatenate([squares, squares], axis=0).astype(bf16)


def project_kernel(index, own, up, down, far, weight, out):
    half = pl.program_id(0)
    total = jnp.zeros((TOKENS, WIDTH // 2), f32)
    squares = jnp.zeros((16, TOKENS), f32)
    for k, ref in enumerate((own, up, down, far)):
        total += jnp.dot(
            ref[pl.ds(0, TOKENS), :], weight[0, index[1 + k], 0], preferred_element_type=f32
        )
        tail = ref[pl.ds(TOKENS, 16), :].astype(f32)
        squares += tail[:, :TOKENS] + tail[:, TOKENS:]
    out[pl.ds(0, TOKENS), :] = total.astype(bf16)
    high = squares.astype(bf16).astype(f32)
    out[pl.ds(TOKENS, 16), :] = jnp.where(half == 0, high, squares - high).astype(bf16)


def project(index, parts, weight):
    whole = pl.BlockSpec((TOKEN_ROWS, WIDTH), lambda half, index: (0, 0))
    return pl.pallas_call(
        project_kernel,
        out_shape=shape((TOKEN_ROWS, WIDTH), bf16),
        grid_spec=pltpu.PrefetchScalarGridSpec(
            num_scalar_prefetch=1,
            grid=(2,),
            in_specs=[whole] * 4
            + [
                pl.BlockSpec(
                    (1, NZH, 1, WIDTH, WIDTH // 2),
                    lambda half, index: (index[0], 0, half, 0, 0),
                )
            ],
            out_specs=pl.BlockSpec((TOKEN_ROWS, WIDTH // 2), lambda half, index: (0, half)),
        ),
        cost_estimate=pl.CostEstimate(
            flops=2 * TOKENS * WIDTH * 4 * WIDTH, bytes_accessed=3 * 2**20, transcendentals=0
        ),
        compiler_params=pltpu.CompilerParams(vmem_limit_bytes=16 * 2**20),
    )(index, *parts, weight)


def finish_kernel(own, got1, got2, got3, out):
    refs = (own, got1, got2, got3)
    squares = jnp.zeros((16, TOKENS), f32)
    for ref in refs:
        tail = ref[pl.ds(TOKENS, 16), :].astype(f32)
        squares += tail[:, :TOKENS] + tail[:, TOKENS:]
    factor = lax.rsqrt(squares[:8] / INNER + EPSILON)
    row = lax.broadcasted_iota(jnp.int32, (SPAN, SPAN), 0)
    col = lax.broadcasted_iota(jnp.int32, (SPAN, SPAN), 1)
    same = jnp.where(row == col, 1.0, 0.0).astype(f32)
    for p in range(PAIRS):
        here = pl.ds(p * SPAN, SPAN)
        turned = lax.dot_general(
            same,
            factor[:, p * SPAN : (p + 1) * SPAN],
            (((1,), (1,)), ((), ())),
            precision=EXACT,
            preferred_element_type=f32,
        )
        total = sum(ref[here, :].astype(f32) for ref in refs)
        out[p] = (total * turned[:, :1]).astype(bf16)


def shards(
    head_inputs,
    gate_inputs,
    write_vectors,
    read_vectors,
    step_sizes,
    decay_logs,
    skip_scale,
    norm_gain,
    out_weight,
    boundary,
):
    seq, head = lax.axis_index("seq"), lax.axis_index("head")
    zl, core = (seq // NCORE) % NZL, seq % NCORE
    y, zh = head // NZH, head % NZH
    first = seq * SPAN
    meta = jnp.concatenate(
        [jnp.stack([first, core]).astype(jnp.int32), boundary, jnp.stack([zl, zh]).astype(jnp.int32)]
    )

    weight = lax.all_gather(swap_z(out_weight), "seq", axis=0, tiled=True)
    weight = weight.reshape(NY, NZH, NCORE, WIDTH, WIDTH // 2)

    group = head // 2
    writes = lax.dynamic_index_in_dim(write_vectors, group, 2, keepdims=False)
    reads = lax.dynamic_index_in_dim(read_vectors, group, 2, keepdims=False)

    payload = shape((PAYLOAD_ROWS, STATE), bf16)
    wide = shape((STATE_ROWS, STATE), f32)
    small = shape((PAIRS * HALF, STATE), f32)
    leaving, mine, decay_mine = call(
        states_kernel,
        (payload, wide, small),
        [SMEM, SMEM, VMEM, VMEM, VMEM],
        (meta, decay_logs, head_inputs, writes, step_sizes),
        2 * 2**24,
        2**20,
    )
    total, state_first, decay_first = call(
        chip_kernel,
        (payload, wide, small),
        [SMEM, VMEM, VMEM, VMEM],
        (meta, to_core(leaving), mine, decay_mine),
        2**18,
        2**19,
    )
    line, state_before, decay_before = call(
        line_kernel,
        (payload, wide, small),
        [SMEM] + [VMEM] * 4,
        (meta, total, to_zl(total, 1), to_zl(total, 2), to_zl(total, 3)),
        2**18,
        2**19,
    )
    half_state = shape((STATE_ROWS, STATE), bf16)
    crossing, keep = call(
        whole_kernel,
        (half_state, half_state),
        [SMEM] + [VMEM] * 7,
        (meta, to_x(line, 1), to_x(line, 2), to_x(line, 3))
        + (state_before, decay_before, state_first, decay_first),
        2**18,
        2**19,
    )
    got = to_core(crossing)

    local = shape((PAIRS, SPAN, WIDTH), f32)
    early, late = call(
        inside_kernel,
        (local, local),
        [SMEM, SMEM, SMEM] + [VMEM] * 5,
        (meta, decay_logs, skip_scale, head_inputs, writes, reads, step_sizes, gate_inputs),
        2**26,
        2**21,
    )
    hidden = call(
        hidden_kernel,
        shape((TOKEN_ROWS, WIDTH), bf16),
        [SMEM] + [VMEM] * 6,
        (meta, keep, got, reads, early, late, norm_gain.reshape(1, WIDTH)),
        2**25,
        2**21,
    )
    parts = (hidden, to_zh(hidden, 1), to_zh(hidden, NZH - 1), to_zh(hidden, 2))
    blocks = [zh, (zh + NZH - 1) % NZH, (zh + 1) % NZH, (zh + 2) % NZH]

    def partial(d):
        index = jnp.stack([(y + d) % NY] + blocks).astype(jnp.int32)
        return project(index, parts, weight)

    arrived = [to_y(partial(d), d) for d in (2, 1, 3)]
    return call(
        finish_kernel,
        shape((PAIRS, SPAN, WIDTH), bf16),
        [VMEM] * 4,
        (partial(0), *arrived),
        2**20,
        2**20,
    )


def solution(mesh):
    return jax.shard_map(
        shards,
        mesh=mesh,
        in_specs=(
            P(None, "seq", "head"),
            P(None, "seq", "head"),
            P(None, "seq", None, None),
            P(None, "seq", None, None),
            P(None, "head", "seq"),
            P("head"),
            P("head"),
            P("head"),
            P("head", "seq"),
            P(),
        ),
        out_specs=P(None, "seq", "head"),
        check_vma=False,
    )
```

time: 368 us -> 204 us (0.55)
  the two profiles are of different devices: /device:TPU:1 before, /device:TPU:158 now
where the time goes in v1:
time: 204 us
  waiting for transfers between devices  98.2 us (48%)
  starting transfers between devices  59.7 us (29%)
  local copies, waits for them, and re-layouts  16.8 us (8%)
  Pallas kernels  15 us (7%)
  between operations  13.9 us (7%)
    ppermute x15, waiting for transfers between devices, send(): return lax.ppermute(value, ('seq', 'head'), route(move))  84.3 us
    ppermute x15, starting transfers between devices, send(): return lax.ppermute(value, ('seq', 'head'), route(move))  59.7 us
    unnamed x28, local copies, waits for them, and re-layouts  14.4 us
    all_gather x1, waiting for transfers between devices, shards(): weight = lax.all_gather(swap_z(out_weight), 'seq', axis=0, tiled=True)  13.9 us
    pallas_call x7, Pallas kernels, call(): pl.pallas_call(kernel, out_shape=outs, in_specs=specs, out_specs=jax.tree...  8.41 us
    pallas_call x4, Pallas kernels, project(): pl.pallas_call(project_kernel, out_shape=shape((TOKEN_ROWS, WIDTH), bf16)...  6.6 us
  transfers between devices with their start and end apart: 16, of which 11 were waited for; matrix products, arithmetic and copies ran while one was open for 1% of the time, Pallas kernels for 6%

profile of v1, /device:TPU:158, one launch (start us, length us, event | category | flops | bytes accessed | tf_op | source)
XLA Modules:
  0.0 203.6 jit_solution(3569950681502000238)
XLA Ops:
  6.5 2.0 %collective-permute-start.11 = (bf16[512,256]{1,0:T(8,128)(2,1)}, bf16[512,256]{1,0:T(8,128)(2,1)S(1)}, u32[]{:S(2)}, u32[]{:S(2)}) collective-permute-start(bf16[512,256]{1,0:T(8,128)(2,1)} %param.18), channel_id=1, source_target_pairs={{0,0},{1,32},{2,64},{3,96},{4,4},{5,36},{6,68},{7,100},{8,8},{9,40... | collective-permute-start | bytes 786440 | tf_op jit(solution)/shard_map/ppermute | solution.py:53
  8.6 14.7 %collective-permute-done.11 = bf16[512,256]{1,0:T(8,128)(2,1)S(1)} collective-permute-done((bf16[512,256]{1,0:T(8,128)(2,1)}, bf16[512,256]{1,0:T(8,128)(2,1)S(1)}, u32[]{:S(2)}, u32[]{:S(2)}) %collective-permute-start.11) | collective-permute-done | bytes 262176 | tf_op jit(solution)/shard_map/ppermute | solution.py:53
  23.3 0.7 copy-done.12
  24.0 0.0 all-gather.2.cloned.1.call-update
  24.1 0.1 constant_dynamic-slice_fusion.1
  24.3 0.7 concatenate.3.meta
  25.0 0.9 copy-done.3
  26.0 0.7 copy-done.6
  26.7 0.7 copy-done.9
  27.3 1.4 shard_map.100
  28.8 1.9 collective-permute-start
  30.7 1.3 collective-permute-done.got
  32.0 0.6 shard_map.101
  32.6 18.2 %collective-permute-start.3 = (bf16[528,128]{1,0:T(8,128)(2,1)S(1)}, bf16[528,128]{1,0:T(8,128)(2,1)S(1)}, u32[]{:S(2)}, u32[]{:S(2)}) collective-permute-start(bf16[528,128]{1,0:T(8,128)(2,1)S(1)} %get-tuple-element.21.own), channel_id=1, source_target_pairs={{0,96},{1,97},{2,98},{3,99},{4,100},{5,101},{6,102},{7,103},{8,104... | collective-permute-start | bytes 405512 | tf_op jit(solution)/shard_map/ppermute | solution.py:53
  50.8 1.9 collective-permute-start.2
  52.8 2.5 %collective-permute-start.1 = (bf16[528,128]{1,0:T(8,128)(2,1)S(1)}, bf16[528,128]{1,0:T(8,128)(2,1)S(1)}, u32[]{:S(2)}, u32[]{:S(2)}) collective-permute-start(bf16[528,128]{1,0:T(8,128)(2,1)S(1)} %get-tuple-element.21.own), channel_id=1, source_target_pairs={{0,32},{1,33},{2,34},{3,35},{4,36},{5,37},{6,38},{7,39},{8,40},{9,... | collective-permute-start | bytes 405512 | tf_op jit(solution)/shard_map/ppermute | solution.py:53
  55.2 1.6 collective-permute-done.3.from3
  56.8 6.3 %collective-permute-done.2.from2 = bf16[528,128]{1,0:T(8,128)(2,1)S(1)} collective-permute-done((bf16[528,128]{1,0:T(8,128)(2,1)S(1)}, bf16[528,128]{1,0:T(8,128)(2,1)S(1)}, u32[]{:S(2)}, u32[]{:S(2)}) %collective-permute-start.2) | collective-permute-done | bytes 135200 | tf_op jit(solution)/shard_map/ppermute | solution.py:53
  63.1 4.2 %collective-permute-done.1.from1 = bf16[528,128]{1,0:T(8,128)(2,1)S(1)} collective-permute-done((bf16[528,128]{1,0:T(8,128)(2,1)S(1)}, bf16[528,128]{1,0:T(8,128)(2,1)S(1)}, u32[]{:S(2)}, u32[]{:S(2)}) %collective-permute-start.1) | collective-permute-done | bytes 135200 | tf_op jit(solution)/shard_map/ppermute | solution.py:53
  67.3 0.8 shard_map.102
  68.1 1.3 collective-permute-start.6
  69.4 1.3 collective-permute-start.5
  70.7 1.3 collective-permute-start.4
  72.0 4.9 %collective-permute-done.6.from3 = bf16[528,128]{1,0:T(8,128)(2,1)S(1)} collective-permute-done((bf16[528,128]{1,0:T(8,128)(2,1)S(1)}, bf16[528,128]{1,0:T(8,128)(2,1)S(1)}, u32[]{:S(2)}, u32[]{:S(2)}) %collective-permute-start.6) | collective-permute-done | bytes 135200 | tf_op jit(solution)/shard_map/ppermute | solution.py:53
  76.9 3.1 %collective-permute-done.5.from2 = bf16[528,128]{1,0:T(8,128)(2,1)S(1)} collective-permute-done((bf16[528,128]{1,0:T(8,128)(2,1)S(1)}, bf16[528,128]{1,0:T(8,128)(2,1)S(1)}, u32[]{:S(2)}, u32[]{:S(2)}) %collective-permute-start.5) | collective-permute-done | bytes 135200 | tf_op jit(solution)/shard_map/ppermute | solution.py:53
  80.0 0.0 collective-permute-done.4.from1
  80.0 0.7 shard_map.103
  80.7 1.9 collective-permute-start.7
  82.6 1.2 constant_dynamic-slice_fusion
  83.8 0.0 copy-start.4
  83.8 0.9 copy-done.4
  84.8 0.9 copy-done.5
  85.7 0.7 copy-done.7
  86.4 0.7 copy-done.10
  87.1 0.7 copy-done.11
  87.7 2.4 %shard_map.104 = (f32[2,128,512]{2,1,0:T(8,128)S(1)}, f32[2,128,512]{2,1,0:T(8,128)S(1)}) custom-call(s32[6]{0:T(128)S(1)} %concatenate.3.meta, f32[8]{0:T(128)S(1)} %copy-done.10, f32[8]{0:T(128)S(1)} %copy-done.11, bf16[2,128,512]{2,1,0:T(8,128)(2,1)S(1)} %copy-done.4, bf16[2,128,128]{2,1,0:T(8,128)(2,1)S(1)} %bitcast.26, ...), custom_call_target="tpu_custom_call" | custom-call | flops 67108864 | bytes 2097152 | tf_op jit(solution)/shard_map/pallas_call | solution.py:85
  90.2 0.0 collective-permute-done.7.got
  90.2 0.0 copy-start.8
  90.2 0.7 copy-done.8
  90.9 1.4 shard_map.105.own
  92.2 7.9 %collective-permute-start.10 = (bf16[272,512]{1,0:T(8,128)(2,1)S(1)}, bf16[272,512]{1,0:T(8,128)(2,1)S(1)}, u32[]{:S(2)}, u32[]{:S(2)}) collective-permute-start(bf16[272,512]{1,0:T(8,128)(2,1)S(1)} %shard_map.105.own), channel_id=1, source_target_pairs={{0,2},{1,3},{2,0},{3,1},{4,6},{5,7},{6,4},{7,5},{8,10},{9,11},{10,... | collective-permute-start | bytes 835592 | tf_op jit(solution)/shard_map/ppermute | solution.py:53
  100.1 1.9 collective-permute-start.9
  102.1 7.8 %collective-permute-start.8 = (bf16[272,512]{1,0:T(8,128)(2,1)S(1)}, bf16[272,512]{1,0:T(8,128)(2,1)S(1)}, u32[]{:S(2)}, u32[]{:S(2)}) collective-permute-start(bf16[272,512]{1,0:T(8,128)(2,1)S(1)} %shard_map.105.own), channel_id=1, source_target_pairs={{0,1},{1,2},{2,3},{3,0},{4,5},{5,6},{6,7},{7,4},{8,9},{9,10},{10,1... | collective-permute-start | bytes 835592 | tf_op jit(solution)/shard_map/ppermute | solution.py:53
  110.0 0.1 stack.68.index
  110.1 0.1 stack.70.index
  110.2 0.1 stack.72.index
  110.3 31.1 %collective-permute-done.10.far = bf16[272,512]{1,0:T(8,128)(2,1)S(1)} collective-permute-done((bf16[272,512]{1,0:T(8,128)(2,1)S(1)}, bf16[272,512]{1,0:T(8,128)(2,1)S(1)}, u32[]{:S(2)}, u32[]{:S(2)}) %collective-permute-start.10) | collective-permute-done | bytes 278560 | tf_op jit(solution)/shard_map/ppermute | solution.py:53
  141.4 0.0 collective-permute-done.9.down
  141.4 12.9 %collective-permute-done.8.up = bf16[272,512]{1,0:T(8,128)(2,1)S(1)} collective-permute-done((bf16[272,512]{1,0:T(8,128)(2,1)S(1)}, bf16[272,512]{1,0:T(8,128)(2,1)S(1)}, u32[]{:S(2)}, u32[]{:S(2)}) %collective-permute-start.8) | collective-permute-done | bytes 278560 | tf_op jit(solution)/shard_map/ppermute | solution.py:53
  154.3 13.9 %all-gather.2.cloned.1.call-done = bf16[16384,256]{1,0:T(8,128)(2,1)} async-done(((bf16[512,256]{1,0:T(8,128)(2,1)}), bf16[16384,256]{1,0:T(8,128)(2,1)}) %all-gather.2.cloned.1.call-update) | async-done | bytes 8388624 | tf_op jit(solution)/shard_map/all_gather | solution.py:375
  168.1 3.4 %copy-done.1 = bf16[16384,256]{1,0:T(8,128)(2,1)S(1)} copy-done((bf16[16384,256]{1,0:T(8,128)(2,1)S(1)}, bf16[16384,256]{1,0:T(8,128)(2,1)}, u32[]{:S(2)}) %copy-start.1) | copy-done | bytes 8388632
  171.5 1.6 shard_map.107
  173.2 3.7 %collective-permute-start.12 = (bf16[272,512]{1,0:T(8,128)(2,1)S(1)}, bf16[272,512]{1,0:T(8,128)(2,1)S(1)}, u32[]{:S(2)}, u32[]{:S(2)}) collective-permute-start(bf16[272,512]{1,0:T(8,128)(2,1)S(1)} %shard_map.107), channel_id=1, source_target_pairs={{0,8},{1,9},{2,10},{3,11},{4,12},{5,13},{6,14},{7,15},{8,0},{9,1},... | collective-permute-start | bytes 835592 | tf_op jit(solution)/shard_map/ppermute | solution.py:53
  176.9 1.7 shard_map.108
  178.6 4.1 %collective-permute-start.13 = (bf16[272,512]{1,0:T(8,128)(2,1)S(1)}, bf16[272,512]{1,0:T(8,128)(2,1)S(1)}, u32[]{:S(2)}, u32[]{:S(2)}) collective-permute-start(bf16[272,512]{1,0:T(8,128)(2,1)S(1)} %shard_map.108), channel_id=1, source_target_pairs={{0,4},{1,5},{2,6},{3,7},{4,8},{5,9},{6,10},{7,11},{8,12},{9,13},{1... | collective-permute-start | bytes 835592 | tf_op jit(solution)/shard_map/ppermute | solution.py:53
  182.6 1.7 shard_map.109
  184.3 1.9 collective-permute-start.14
  186.3 0.1 stack.63.index
  186.3 3.4 %copy-done.2 = bf16[16384,256]{1,0:T(8,128)(2,1)S(1)} copy-done((bf16[16384,256]{1,0:T(8,128)(2,1)S(1)}, bf16[16384,256]{1,0:T(8,128)(2,1)}, u32[]{:S(2)}) %copy-start.2) | copy-done | bytes 8388632
  189.7 1.6 shard_map.106.own
  191.4 0.0 collective-permute-done.12.got1
  191.4 0.0 collective-permute-done.13.got2
  191.4 4.2 %collective-permute-done.14.got3 = bf16[272,512]{1,0:T(8,128)(2,1)S(1)} collective-permute-done((bf16[272,512]{1,0:T(8,128)(2,1)S(1)}, bf16[272,512]{1,0:T(8,128)(2,1)S(1)}, u32[]{:S(2)}, u32[]{:S(2)}) %collective-permute-start.14) | collective-permute-done | bytes 278560 | tf_op jit(solution)/shard_map/ppermute | solution.py:53
  195.6 1.1 shard_map.110
  (15 shorter events, 0.0 us)
Async XLA Ops:
  6.5 17.6 %copy-start = (bf16[2,128,8,128]{3,2,1,0:T(8,128)(2,1)S(1)}, bf16[2,128,8,128]{3,2,1,0:T(8,128)(2,1)}, u32[]{:S(2)}) copy-start(bf16[2,128,8,128]{3,2,1,0:T(8,128)(2,1)} %param.12) | copy-start | bytes 1572868
  6.5 161.6 %all-gather.2.cloned.1.call-start = ((), (), s32[]{:S(2)}) async-start(), calls=%async_computation | async-start | bytes 8650752 | tf_op jit(solution)/shard_map/all_gather | solution.py:375
  6.5 16.8 %collective-permute-start.11 = (bf16[512,256]{1,0:T(8,128)(2,1)}, bf16[512,256]{1,0:T(8,128)(2,1)S(1)}, u32[]{:S(2)}, u32[]{:S(2)}) collective-permute-start(bf16[512,256]{1,0:T(8,128)(2,1)} %param.18), channel_id=1, source_target_pairs={{0,0},{1,32},{2,64},{3,96},{4,4},{5,36},{6,68},{7,100},{8,8},{9,40... | collective-permute-start | bytes 786440 | tf_op jit(solution)/shard_map/ppermute | solution.py:53
  23.3 0.7 copy-start.12
  25.0 1.0 copy-start.3
  26.0 0.7 copy-start.6
  26.7 0.7 copy-start.9
  28.8 3.2 %collective-permute-start = (bf16[528,128]{1,0:T(8,128)(2,1)S(1)}, bf16[528,128]{1,0:T(8,128)(2,1)S(1)}, u32[]{:S(2)}, u32[]{:S(2)}) collective-permute-start(bf16[528,128]{1,0:T(8,128)(2,1)S(1)} %get-tuple-element.18), channel_id=1, source_target_pairs={{0,16},{1,17},{2,18},{3,19},{4,20},{5,21},{6,22},{7,23},{8,24},{9,... | collective-permute-start | bytes 405512 | tf_op jit(solution)/shard_map/ppermute | solution.py:53
  32.6 24.2 %collective-permute-start.3 = (bf16[528,128]{1,0:T(8,128)(2,1)S(1)}, bf16[528,128]{1,0:T(8,128)(2,1)S(1)}, u32[]{:S(2)}, u32[]{:S(2)}) collective-permute-start(bf16[528,128]{1,0:T(8,128)(2,1)S(1)} %get-tuple-element.21.own), channel_id=1, source_target_pairs={{0,96},{1,97},{2,98},{3,99},{4,100},{5,101},{6,102},{7,103},{8,104... | collective-permute-start | bytes 405512 | tf_op jit(solution)/shard_map/ppermute | solution.py:53
  50.8 12.3 %collective-permute-start.2 = (bf16[528,128]{1,0:T(8,128)(2,1)S(1)}, bf16[528,128]{1,0:T(8,128)(2,1)S(1)}, u32[]{:S(2)}, u32[]{:S(2)}) collective-permute-start(bf16[528,128]{1,0:T(8,128)(2,1)S(1)} %get-tuple-element.21.own), channel_id=1, source_target_pairs={{0,64},{1,65},{2,66},{3,67},{4,68},{5,69},{6,70},{7,71},{8,72},{9,... | collective-permute-start | bytes 405512 | tf_op jit(solution)/shard_map/ppermute | solution.py:53
  52.8 14.5 %collective-permute-start.1 = (bf16[528,128]{1,0:T(8,128)(2,1)S(1)}, bf16[528,128]{1,0:T(8,128)(2,1)S(1)}, u32[]{:S(2)}, u32[]{:S(2)}) collective-permute-start(bf16[528,128]{1,0:T(8,128)(2,1)S(1)} %get-tuple-element.21.own), channel_id=1, source_target_pairs={{0,32},{1,33},{2,34},{3,35},{4,36},{5,37},{6,38},{7,39},{8,40},{9,... | collective-permute-start | bytes 405512 | tf_op jit(solution)/shard_map/ppermute | solution.py:53
  68.1 8.8 %collective-permute-start.6 = (bf16[528,128]{1,0:T(8,128)(2,1)S(1)}, bf16[528,128]{1,0:T(8,128)(2,1)S(1)}, u32[]{:S(2)}, u32[]{:S(2)}) collective-permute-start(bf16[528,128]{1,0:T(8,128)(2,1)S(1)} %get-tuple-element.22), channel_id=1, source_target_pairs={{0,384},{1,385},{2,386},{3,387},{4,388},{5,389},{6,390},{7,391},{8... | collective-permute-start | bytes 405512 | tf_op jit(solution)/shard_map/ppermute | solution.py:53
  69.4 10.6 %collective-permute-start.5 = (bf16[528,128]{1,0:T(8,128)(2,1)S(1)}, bf16[528,128]{1,0:T(8,128)(2,1)S(1)}, u32[]{:S(2)}, u32[]{:S(2)}) collective-permute-start(bf16[528,128]{1,0:T(8,128)(2,1)S(1)} %get-tuple-element.22), channel_id=1, source_target_pairs={{0,256},{1,257},{2,258},{3,259},{4,260},{5,261},{6,262},{7,263},{8... | collective-permute-start | bytes 405512 | tf_op jit(solution)/shard_map/ppermute | solution.py:53
  70.7 9.3 %collective-permute-start.4 = (bf16[528,128]{1,0:T(8,128)(2,1)S(1)}, bf16[528,128]{1,0:T(8,128)(2,1)S(1)}, u32[]{:S(2)}, u32[]{:S(2)}) collective-permute-start(bf16[528,128]{1,0:T(8,128)(2,1)S(1)} %get-tuple-element.22), channel_id=1, source_target_pairs={{0,128},{1,129},{2,130},{3,131},{4,132},{5,133},{6,134},{7,135},{8... | collective-permute-start | bytes 405512 | tf_op jit(solution)/shard_map/ppermute | solution.py:53
  80.7 9.5 %collective-permute-start.7 = (bf16[512,128]{1,0:T(8,128)(2,1)S(1)}, bf16[512,128]{1,0:T(8,128)(2,1)S(1)}, u32[]{:S(2)}, u32[]{:S(2)}) collective-permute-start(bf16[512,128]{1,0:T(8,128)(2,1)S(1)} %get-tuple-element.28), channel_id=1, source_target_pairs={{0,16},{1,17},{2,18},{3,19},{4,20},{5,21},{6,22},{7,23},{8,24},{9,... | collective-permute-start | bytes 393224 | tf_op jit(solution)/shard_map/ppermute | solution.py:53
  83.8 1.0 copy-start.4
  84.8 0.9 copy-start.5
  85.7 0.7 copy-start.7
  86.4 0.7 copy-start.10
  87.1 0.7 copy-start.11
  90.2 0.7 copy-start.8
  92.2 49.2 %collective-permute-start.10 = (bf16[272,512]{1,0:T(8,128)(2,1)S(1)}, bf16[272,512]{1,0:T(8,128)(2,1)S(1)}, u32[]{:S(2)}, u32[]{:S(2)}) collective-permute-start(bf16[272,512]{1,0:T(8,128)(2,1)S(1)} %shard_map.105.own), channel_id=1, source_target_pairs={{0,2},{1,3},{2,0},{3,1},{4,6},{5,7},{6,4},{7,5},{8,10},{9,11},{10,... | collective-permute-start | bytes 835592 | tf_op jit(solution)/shard_map/ppermute | solution.py:53
  100.1 41.3 %collective-permute-start.9 = (bf16[272,512]{1,0:T(8,128)(2,1)S(1)}, bf16[272,512]{1,0:T(8,128)(2,1)S(1)}, u32[]{:S(2)}, u32[]{:S(2)}) collective-permute-start(bf16[272,512]{1,0:T(8,128)(2,1)S(1)} %shard_map.105.own), channel_id=1, source_target_pairs={{0,3},{1,0},{2,1},{3,2},{4,7},{5,4},{6,5},{7,6},{8,11},{9,8},{10,9... | collective-permute-start | bytes 835592 | tf_op jit(solution)/shard_map/ppermute | solution.py:53
  102.1 52.2 %collective-permute-start.8 = (bf16[272,512]{1,0:T(8,128)(2,1)S(1)}, bf16[272,512]{1,0:T(8,128)(2,1)S(1)}, u32[]{:S(2)}, u32[]{:S(2)}) collective-permute-start(bf16[272,512]{1,0:T(8,128)(2,1)S(1)} %shard_map.105.own), channel_id=1, source_target_pairs={{0,1},{1,2},{2,3},{3,0},{4,5},{5,6},{6,7},{7,4},{8,9},{9,10},{10,1... | collective-permute-start | bytes 835592 | tf_op jit(solution)/shard_map/ppermute | solution.py:53
  168.1 3.4 %copy-start.1 = (bf16[16384,256]{1,0:T(8,128)(2,1)S(1)}, bf16[16384,256]{1,0:T(8,128)(2,1)}, u32[]{:S(2)}) copy-start(bf16[16384,256]{1,0:T(8,128)(2,1)} %all-gather.2.cloned.1.call-done) | copy-start | bytes 25165828
  173.2 18.2 %collective-permute-start.12 = (bf16[272,512]{1,0:T(8,128)(2,1)S(1)}, bf16[272,512]{1,0:T(8,128)(2,1)S(1)}, u32[]{:S(2)}, u32[]{:S(2)}) collective-permute-start(bf16[272,512]{1,0:T(8,128)(2,1)S(1)} %shard_map.107), channel_id=1, source_target_pairs={{0,8},{1,9},{2,10},{3,11},{4,12},{5,13},{6,14},{7,15},{8,0},{9,1},... | collective-permute-start | bytes 835592 | tf_op jit(solution)/shard_map/ppermute | solution.py:53
  178.6 12.8 %collective-permute-start.13 = (bf16[272,512]{1,0:T(8,128)(2,1)S(1)}, bf16[272,512]{1,0:T(8,128)(2,1)S(1)}, u32[]{:S(2)}, u32[]{:S(2)}) collective-permute-start(bf16[272,512]{1,0:T(8,128)(2,1)S(1)} %shard_map.108), channel_id=1, source_target_pairs={{0,4},{1,5},{2,6},{3,7},{4,8},{5,9},{6,10},{7,11},{8,12},{9,13},{1... | collective-permute-start | bytes 835592 | tf_op jit(solution)/shard_map/ppermute | solution.py:53
  184.3 11.3 %collective-permute-start.14 = (bf16[272,512]{1,0:T(8,128)(2,1)S(1)}, bf16[272,512]{1,0:T(8,128)(2,1)S(1)}, u32[]{:S(2)}, u32[]{:S(2)}) collective-permute-start(bf16[272,512]{1,0:T(8,128)(2,1)S(1)} %shard_map.109), channel_id=1, source_target_pairs={{0,12},{1,13},{2,14},{3,15},{4,0},{5,1},{6,2},{7,3},{8,4},{9,5},{1... | collective-permute-start | bytes 835592 | tf_op jit(solution)/shard_map/ppermute | solution.py:53
  186.3 3.4 %copy-start.2 = (bf16[16384,256]{1,0:T(8,128)(2,1)S(1)}, bf16[16384,256]{1,0:T(8,128)(2,1)}, u32[]{:S(2)}) copy-start(bf16[16384,256]{1,0:T(8,128)(2,1)} %all-gather.2.cloned.1.call-done) | copy-start | bytes 25165828
Sparse Core Ops, SparseCore 0:
  24.2 143.9 all-gather.1

commit v2 on v1

--- a/solution.py
+++ b/solution.py
@@ -17,8 +17,9 @@
 TOKENS = PAIRS * SPAN
 STATE_ROWS = PAIRS * HALF * CHANNELS
 PAYLOAD_ROWS = STATE_ROWS + 16
+SPOT = ((0, 2, 3, 1), (1, 2, 3, 0), (3, 0, 1, 2), (2, 0, 1, 3))
 TOKEN_ROWS = TOKENS + 16
-NX = NZL = NCORE = NY = NZH = 4
+NX = NZL = NY = NZH = 4
 NCORE = 2
 EXACT = lax.Precision.HIGHEST
 f32 = jnp.float32
@@ -74,21 +75,33 @@
 
 
 def swap_z(value):
-    return send(value, lambda x, zl, c, y, zh: (x, zh, c, y, zl))
+    return send(value, lambda x, zl, c, y, zh: (x, SPOT[zl][zh], c, y, zl))
+
+
+def gather(block, key):
+    groups = {}
+    for x in range(NX):
+        for zl in range(NZL):
+            for core in range(NCORE):
+                groups.setdefault(key(x, zl, core), []).append(seq_index(x, zl, core))
+    return lax.all_gather(
+        block, "seq", axis=0, tiled=True, axis_index_groups=list(groups.values())
+    )
 
 
 VMEM = pl.BlockSpec(memory_space=pltpu.VMEM)
 SMEM = pl.BlockSpec(memory_space=pltpu.SMEM)
 
 
-def call(kernel, outs, specs, args, flops, moved, limit=None):
+def call(kernel, outs, specs, args, flops, moved, scratch=(), limit=16 * 2**20):
     return pl.pallas_call(
         kernel,
         out_shape=outs,
         in_specs=specs,
         out_specs=jax.tree.map(lambda _: VMEM, outs),
+        scratch_shapes=scratch,
         cost_estimate=pl.CostEstimate(flops=flops, bytes_accessed=moved, transcendentals=0),
-        compiler_params=pltpu.CompilerParams(vmem_limit_bytes=limit or 16 * 2**20),
+        compiler_params=pltpu.CompilerParams(vmem_limit_bytes=limit),
     )(*args)
 
 
@@ -102,16 +115,6 @@
     for h in range(HEADS_LOCAL):
         out = jnp.where(rows == h, scalars[h], out)
     return out
-
-
-def split(value):
-    high = value.astype(bf16)
-    low = (value - high.astype(f32)).astype(bf16)
-    return high, low
-
-
-def flag(condition):
-    return jnp.where(condition, 1.0, 0.0).astype(f32)
 
 
 def states_kernel(meta, decay_logs, x, writes, steps, out, mine, decay_mine):
@@ -259,15 +262,22 @@
             late[p, :, here] = opened * reached * jnp.exp(column)
 
 
-def hidden_kernel(meta, keep, got, reads, early, late, gain, out):
+def scaled_kernel(weight, gain, out):
+    row = lax.broadcasted_iota(jnp.int32, (SPAN, SPAN), 0)
+    col = lax.broadcasted_iota(jnp.int32, (SPAN, SPAN), 1)
+    for part in range(WIDTH // SPAN):
+        here = pl.ds(part * SPAN, SPAN)
+        gains = jnp.broadcast_to(gain[:, part * SPAN : (part + 1) * SPAN], (SPAN, SPAN))
+        turned = jnp.sum(jnp.where(row == col, gains, 0.0), axis=1, keepdims=True)
+        out[here, :] = (weight[here, :].astype(f32) * turned).astype(bf16)
+
+
+def hidden_kernel(meta, keep, got, reads, early, late, *outs):
     core = meta[1]
     rows = HALF * CHANNELS
-    ones = jnp.ones((8, WIDTH), f32)
-    highs, lows = [], []
-    for p in range(PAIRS):
+    for p, out in enumerate(outs):
         here = pl.ds(p * rows, rows)
         own, other = keep[here, :], got[here, :]
-        total = jnp.zeros((8, SPAN), f32)
         for half in range(2):
             state = jnp.where(core == half, own, other)
             columns = slice(half * rows, (half + 1) * rows)
@@ -275,58 +285,65 @@
                 reads[p], state, (((1,), (1,)), ((), ())), preferred_element_type=f32
             )
             gated = early[p, :, columns] + late[p, :, columns] * carry
-            out[pl.ds(p * SPAN, SPAN), columns] = (gated * gain[:, columns]).astype(bf16)
-            total += lax.dot_general(
-                ones[:, columns],
-                gated * gated,
-                (((1,), (1,)), ((), ())),
-                precision=EXACT,
-                preferred_element_type=f32,
-            )
-        high = total.astype(bf16).astype(f32)
-        highs.append(high)
-        lows.append(total - high)
-    squares = jnp.concatenate(highs + lows, axis=1)
-    out[pl.ds(TOKENS, 16), :] = jnp.concatenate([squares, squares], axis=0).astype(bf16)
-
-
-def project_kernel(index, own, up, down, far, weight, out):
-    half = pl.program_id(0)
-    total = jnp.zeros((TOKENS, WIDTH // 2), f32)
-    squares = jnp.zeros((16, TOKENS), f32)
-    for k, ref in enumerate((own, up, down, far)):
-        total += jnp.dot(
-            ref[pl.ds(0, TOKENS), :], weight[0, index[1 + k], 0], preferred_element_type=f32
+            out[:, columns] = gated.astype(bf16)
+
+
+def arrange_kernel(meta, spot, *refs):
+    chunks, hidden, tails = refs[: PAIRS * NZH], refs[-2], refs[-1]
+    zh = meta[5]
+    ones = jnp.ones((8, WIDTH), f32)
+    for p in range(PAIRS):
+        here = pl.ds(p * SPAN, SPAN)
+        total = jnp.zeros((SPAN, WIDTH), f32)
+        for k, move in enumerate((0, NZH - 1, 1, 2)):
+            chunk = chunks[PAIRS * k + p][...]
+            turn = spot[zh * NZH + (zh + move) % NZH]
+            columns = pl.ds(pl.multiple_of(turn * WIDTH, WIDTH), WIDTH)
+            hidden[here, columns] = chunk
+            wide = chunk.astype(f32)
+            total += wide * wide
+        squares = lax.dot_general(
+            ones, total, (((1,), (1,)), ((), ())), precision=EXACT, preferred_element_type=f32
         )
-        tail = ref[pl.ds(TOKENS, 16), :].astype(f32)
-        squares += tail[:, :TOKENS] + tail[:, TOKENS:]
-    out[pl.ds(0, TOKENS), :] = total.astype(bf16)
-    high = squares.astype(bf16).astype(f32)
-    out[pl.ds(TOKENS, 16), :] = jnp.where(half == 0, high, squares - high).astype(bf16)
-
-
-def project(index, parts, weight):
-    whole = pl.BlockSpec((TOKEN_ROWS, WIDTH), lambda half, index: (0, 0))
-    return pl.pallas_call(
-        project_kernel,
-        out_shape=shape((TOKEN_ROWS, WIDTH), bf16),
-        grid_spec=pltpu.PrefetchScalarGridSpec(
-            num_scalar_prefetch=1,
-            grid=(2,),
-            in_specs=[whole] * 4
-            + [
-                pl.BlockSpec(
-                    (1, NZH, 1, WIDTH, WIDTH // 2),
-                    lambda half, index: (index[0], 0, half, 0, 0),
-                )
-            ],
-            out_specs=pl.BlockSpec((TOKEN_ROWS, WIDTH // 2), lambda half, index: (0, half)),
-        ),
-        cost_estimate=pl.CostEstimate(
-            flops=2 * TOKENS * WIDTH * 4 * WIDTH, bytes_accessed=3 * 2**20, transcendentals=0
-        ),
-        compiler_params=pltpu.CompilerParams(vmem_limit_bytes=16 * 2**20),
-    )(index, *parts, weight)
+        high = squares.astype(bf16).astype(f32)
+        for place, part in ((p * SPAN, high), (TOKENS + p * SPAN, squares - high)):
+            tails[:, pl.ds(place, SPAN)] = jnp.concatenate([part, part], axis=0).astype(bf16)
+
+
+def project_kernel(meta, hidden, tails, weight, *refs):
+    outs, here, sem = refs[:NY], refs[NY], refs[NY + 1]
+    half = WIDTH // 2
+    order = [(d, core) for d in (2, 1, 3, 0) for core in range(NCORE)]
+    copies = []
+    for slot, (d, core) in enumerate(order):
+        copy = pltpu.make_async_copy(
+            weight.at[(meta[6] + d) % NY, core], here.at[slot], sem.at[slot]
+        )
+        copy.start()
+        copies.append(copy)
+    for out in outs:
+        out[pl.ds(TOKENS, 16), :] = tails[...]
+    for slot, (d, core) in enumerate(order):
+        copies[slot].wait()
+        total = jnp.dot(hidden[...], here[slot], preferred_element_type=f32)
+        outs[d][pl.ds(0, TOKENS), pl.ds(core * half, half)] = total.astype(bf16)
+
+
+def finish_kernel(own, got1, got2, got3, out):
+    refs = (own, got1, got2, got3)
+    row = lax.broadcasted_iota(jnp.int32, (SPAN, SPAN), 0)
+    col = lax.broadcasted_iota(jnp.int32, (SPAN, SPAN), 1)
+    for p in range(PAIRS):
+        here = pl.ds(p * SPAN, SPAN)
+        squares = jnp.zeros((16, SPAN), f32)
+        for ref in refs:
+            squares += ref[pl.ds(TOKENS, 16), pl.ds(p * SPAN, SPAN)].astype(f32)
+            squares += ref[pl.ds(TOKENS, 16), pl.ds(TOKENS + p * SPAN, SPAN)].astype(f32)
+        factor = lax.rsqrt(squares / INNER + EPSILON)
+        spread = jnp.broadcast_to(factor[:1], (SPAN, SPAN))
+        turned = jnp.sum(jnp.where(row == col, spread, 0.0), axis=1, keepdims=True)
+        total = sum(ref[here, :].astype(f32) for ref in refs)
+        out[p] = (total * turned).astype(bf16)
 
 
 def finish_kernel(own, got1, got2, got3, out):
@@ -369,11 +386,8 @@
     y, zh = head // NZH, head % NZH
     first = seq * SPAN
     meta = jnp.concatenate(
-        [jnp.stack([first, core]).astype(jnp.int32), boundary, jnp.stack([zl, zh]).astype(jnp.int32)]
-    )
-
-    weight = lax.all_gather(swap_z(out_weight), "seq", axis=0, tiled=True)
-    weight = weight.reshape(NY, NZH, NCORE, WIDTH, WIDTH // 2)
+        [jnp.stack([first, core]).astype(jnp.int32), boundary, jnp.stack([zl, zh, y]).astype(jnp.int32)]
+    )
 
     group = head // 2
     writes = lax.dynamic_index_in_dim(write_vectors, group, 2, keepdims=False)
@@ -382,6 +396,15 @@
     payload = shape((PAYLOAD_ROWS, STATE), bf16)
     wide = shape((STATE_ROWS, STATE), f32)
     small = shape((PAIRS * HALF, STATE), f32)
+    scaled = call(
+        scaled_kernel,
+        shape((WIDTH, WIDTH // 2), bf16),
+        [VMEM, VMEM],
+        (out_weight, norm_gain.reshape(1, WIDTH)),
+        2**18,
+        2**19,
+    )
+    near = swap_z(scaled)
     leaving, mine, decay_mine = call(
         states_kernel,
         (payload, wide, small),
@@ -398,26 +421,6 @@
         2**18,
         2**19,
     )
-    line, state_before, decay_before = call(
-        line_kernel,
-        (payload, wide, small),
-        [SMEM] + [VMEM] * 4,
-        (meta, total, to_zl(total, 1), to_zl(total, 2), to_zl(total, 3)),
-        2**18,
-        2**19,
-    )
-    half_state = shape((STATE_ROWS, STATE), bf16)
-    crossing, keep = call(
-        whole_kernel,
-        (half_state, half_state),
-        [SMEM] + [VMEM] * 7,
-        (meta, to_x(line, 1), to_x(line, 2), to_x(line, 3))
-        + (state_before, decay_before, state_first, decay_first),
-        2**18,
-        2**19,
-    )
-    got = to_core(crossing)
-
     local = shape((PAIRS, SPAN, WIDTH), f32)
     early, late = call(
         inside_kernel,
@@ -427,27 +430,78 @@
         2**26,
         2**21,
     )
-    hidden = call(
+    near, total = lax.optimization_barrier((near, total))
+    from_zl = [to_zl(total, d) for d in (1, 2, 3)]
+    early, *from_zl = lax.optimization_barrier((early, *from_zl))
+    line, state_before, decay_before = call(
+        line_kernel,
+        (payload, wide, small),
+        [SMEM] + [VMEM] * 4,
+        (meta, total, *from_zl),
+        2**18,
+        2**19,
+    )
+    from_x = [to_x(line, d) for d in (1, 2, 3)]
+    half_state = shape((STATE_ROWS, STATE), bf16)
+    crossing, keep = call(
+        whole_kernel,
+        (half_state, half_state),
+        [SMEM] + [VMEM] * 7,
+        (meta, *from_x)
+        + (state_before, decay_before, state_first, decay_first),
+        2**18,
+        2**19,
+    )
+    got = to_core(crossing)
+
+    token_part = shape((SPAN, WIDTH), bf16)
+    first, second = call(
         hidden_kernel,
-        shape((TOKEN_ROWS, WIDTH), bf16),
-        [SMEM] + [VMEM] * 6,
-        (meta, keep, got, reads, early, late, norm_gain.reshape(1, WIDTH)),
+        (token_part, token_part),
+        [SMEM] + [VMEM] * 5,
+        (meta, keep, got, reads, early, late),
         2**25,
         2**21,
     )
-    parts = (hidden, to_zh(hidden, 1), to_zh(hidden, NZH - 1), to_zh(hidden, 2))
-    blocks = [zh, (zh + NZH - 1) % NZH, (zh + 1) % NZH, (zh + 2) % NZH]
-
-    def partial(d):
-        index = jnp.stack([(y + d) % NY] + blocks).astype(jnp.int32)
-        return project(index, parts, weight)
-
-    arrived = [to_y(partial(d), d) for d in (2, 1, 3)]
+    line_weight = gather(near, lambda x, zl, core: (x, core))
+    line_weight, first, second = lax.optimization_barrier((line_weight, first, second))
+    weight = gather(line_weight, lambda x, zl, core: zl)
+    weight = weight.reshape(NX, NCORE, NZH * WIDTH, WIDTH // 2)
+
+    first_below, second_above = to_zh(first, 1), to_zh(second, NZH - 1)
+    second_below, first_above = to_zh(second, 1), to_zh(first, NZH - 1)
+    far = (to_zh(first_below, 1), to_zh(second_above, NZH - 1))
+    chunks = (first, second, first_below, second_below, first_above, second_above) + far
+    places = jnp.array(SPOT, jnp.int32).reshape(-1)
+    arranged, tails = call(
+        arrange_kernel,
+        (shape((TOKENS, NZH * WIDTH), bf16), shape((16, WIDTH), bf16)),
+        [SMEM, SMEM] + [VMEM] * PAIRS * NZH,
+        (meta, places, *chunks),
+        2**24,
+        2**21,
+    )
+    partial = shape((TOKEN_ROWS, WIDTH), bf16)
+    blocks = NY * NCORE
+    partials = call(
+        project_kernel,
+        (partial,) * NY,
+        [SMEM, VMEM, VMEM, pl.BlockSpec(memory_space=pl.ANY)],
+        (meta, arranged, tails, weight),
+        2**31,
+        2**23,
+        [
+            pltpu.VMEM((blocks, NZH * WIDTH, WIDTH // 2), bf16),
+            pltpu.SemaphoreType.DMA((blocks,)),
+        ],
+        58 * 2**20,
+    )
+    arrived = [to_y(partials[d], d) for d in (2, 1, 3)]
     return call(
         finish_kernel,
         shape((PAIRS, SPAN, WIDTH), bf16),
         [VMEM] * 4,
-        (partial(0), *arrived),
+        (partials[0], *arrived),
         2**20,
         2**20,
     )

time: 204 us -> 169 us (0.83)
  the two profiles are of different devices: /device:TPU:158 before, /device:TPU:1 now
where the time goes in v2:
time: 169 us
  starting transfers between devices  77.3 us (46%)
  waiting for transfers between devices  45.7 us (27%)
  Pallas kernels  17.9 us (11%)
  local copies, waits for them, and re-layouts  13.9 us (8%)
  between operations  13.8 us (8%)
    ppermute x18, starting transfers between devices, send(): return lax.ppermute(value, ('seq', 'head'), route(move))  77.2 us
    ppermute x18, waiting for transfers between devices, send(): return lax.ppermute(value, ('seq', 'head'), route(move))  36.5 us
    pallas_call x10, Pallas kernels, call(): pl.pallas_call(kernel, out_shape=outs, in_specs=specs, out_specs=jax.tree...  17.9 us
    unnamed x34, local copies, waits for them, and re-layouts  11.8 us
    all_gather x2, waiting for transfers between devices, gather(): lax.all_gather(block, 'seq', axis=0, tiled=True, axis_index_groups=list(g...  9.16 us
  transfers between devices with their start and end apart: 20, of which 11 were waited for; matrix products, arithmetic and copies ran while one was open for 1% of the time, Pallas kernels for 5%

profile of v2, /device:TPU:1, one launch (start us, length us, event | category | flops | bytes accessed | tf_op | source)
XLA Modules:
  0.0 168.5 jit_solution(8603005570582556643)
XLA Ops:
  6.5 1.0 copy-done.5
  7.6 0.7 copy-done.11
  8.2 0.1 shard_map.109
  8.4 0.7 collective-permute-start
  9.1 0.1 constant_dynamic-slice_fusion.1
  9.3 1.2 constant_dynamic-slice_fusion
  10.5 0.7 concatenate.3.meta
  11.3 0.0 copy-start.2
  11.3 0.9 copy-done.2
  12.2 0.7 copy-done.8
  12.9 0.7 copy-done.12
  13.6 1.4 shard_map.110
  15.0 8.8 %collective-permute-start.1 = (bf16[528,128]{1,0:T(8,128)(2,1)S(1)}, bf16[528,128]{1,0:T(8,128)(2,1)S(1)}, u32[]{:S(2)}, u32[]{:S(2)}) collective-permute-start(bf16[528,128]{1,0:T(8,128)(2,1)S(1)} %get-tuple-element.35), channel_id=1, source_target_pairs={{0,16},{1,17},{2,18},{3,19},{4,20},{5,21},{6,22},{7,23},{8,24},{9,... | collective-permute-start | bytes 405512 | tf_op jit(solution)/shard_map/ppermute | solution.py:54
  23.8 1.0 collective-permute-done.1.got
  24.8 0.6 shard_map.111
  25.4 0.0 collective-permute-done
  25.4 0.0 copy-start.16
  25.4 0.7 copy-done.16
  26.1 0.0 all-gather.3.cloned.1.call-update
  26.1 0.0 all-gather.5.cloned.1.call-start
  26.2 13.1 %collective-permute-start.4 = (bf16[528,128]{1,0:T(8,128)(2,1)S(1)}, bf16[528,128]{1,0:T(8,128)(2,1)S(1)}, u32[]{:S(2)}, u32[]{:S(2)}) collective-permute-start(bf16[528,128]{1,0:T(8,128)(2,1)S(1)} %get-tuple-element.40.own), channel_id=1, source_target_pairs={{0,96},{1,97},{2,98},{3,99},{4,100},{5,101},{6,102},{7,103},{8,104... | collective-permute-start | bytes 405512 | tf_op jit(solution)/shard_map/ppermute | solution.py:54
  39.3 1.9 %collective-permute-start.3 = (bf16[528,128]{1,0:T(8,128)(2,1)S(1)}, bf16[528,128]{1,0:T(8,128)(2,1)S(1)}, u32[]{:S(2)}, u32[]{:S(2)}) collective-permute-start(bf16[528,128]{1,0:T(8,128)(2,1)S(1)} %get-tuple-element.40.own), channel_id=1, source_target_pairs={{0,64},{1,65},{2,66},{3,67},{4,68},{5,69},{6,70},{7,71},{8,72},{9,... | collective-permute-start | bytes 405512 | tf_op jit(solution)/shard_map/ppermute | solution.py:54
  41.2 2.6 %collective-permute-start.2 = (bf16[528,128]{1,0:T(8,128)(2,1)S(1)}, bf16[528,128]{1,0:T(8,128)(2,1)S(1)}, u32[]{:S(2)}, u32[]{:S(2)}) collective-permute-start(bf16[528,128]{1,0:T(8,128)(2,1)S(1)} %get-tuple-element.40.own), channel_id=1, source_target_pairs={{0,32},{1,33},{2,34},{3,35},{4,36},{5,37},{6,38},{7,39},{8,40},{9,... | collective-permute-start | bytes 405512 | tf_op jit(solution)/shard_map/ppermute | solution.py:54
  43.8 0.0 copy-start.3
  43.8 0.9 copy-done.3
  44.8 0.9 copy-done.6
  45.7 0.7 copy-done.9
  46.4 0.7 copy-done.13
  47.1 0.7 copy-done.15
  47.7 2.4 %shard_map.112 = (f32[2,128,512]{2,1,0:T(8,128)S(1)}, f32[2,128,512]{2,1,0:T(8,128)S(1)}) custom-call(s32[7]{0:T(128)S(1)} %concatenate.3.meta, f32[8]{0:T(128)S(1)} %copy-done.13, f32[8]{0:T(128)S(1)} %copy-done.15, bf16[2,128,512]{2,1,0:T(8,128)(2,1)S(1)} %copy-done.3, bf16[2,128,128]{2,1,0:T(8,128)(2,1)S(1)} %get-tuple-element.66.writes, ...), custom_call_target="tpu_custom_call" | custom-call | flops 67108864 | bytes 2097152 | tf_op jit(solution)/shard_map/pallas_call | solution.py:97
  50.2 2.2 %collective-permute-done.3.from2 = bf16[528,128]{1,0:T(8,128)(2,1)S(1)} collective-permute-done((bf16[528,128]{1,0:T(8,128)(2,1)S(1)}, bf16[528,128]{1,0:T(8,128)(2,1)S(1)}, u32[]{:S(2)}, u32[]{:S(2)}) %collective-permute-start.3) | collective-permute-done | bytes 135200 | tf_op jit(solution)/shard_map/ppermute | solution.py:54
  52.4 0.8 shard_map.113
  53.2 4.4 %collective-permute-start.7 = (bf16[528,128]{1,0:T(8,128)(2,1)S(1)}, bf16[528,128]{1,0:T(8,128)(2,1)S(1)}, u32[]{:S(2)}, u32[]{:S(2)}) collective-permute-start(bf16[528,128]{1,0:T(8,128)(2,1)S(1)} %get-tuple-element.45), channel_id=1, source_target_pairs={{0,384},{1,385},{2,386},{3,387},{4,388},{5,389},{6,390},{7,391},{8... | collective-permute-start | bytes 405512 | tf_op jit(solution)/shard_map/ppermute | solution.py:54
  57.6 1.3 collective-permute-start.6
  58.9 2.5 %collective-permute-start.5 = (bf16[528,128]{1,0:T(8,128)(2,1)S(1)}, bf16[528,128]{1,0:T(8,128)(2,1)S(1)}, u32[]{:S(2)}, u32[]{:S(2)}) collective-permute-start(bf16[528,128]{1,0:T(8,128)(2,1)S(1)} %get-tuple-element.45), channel_id=1, source_target_pairs={{0,128},{1,129},{2,130},{3,131},{4,132},{5,133},{6,134},{7,135},{8... | collective-permute-start | bytes 405512 | tf_op jit(solution)/shard_map/ppermute | solution.py:54
  61.4 2.9 %collective-permute-done.5.from1 = bf16[528,128]{1,0:T(8,128)(2,1)S(1)} collective-permute-done((bf16[528,128]{1,0:T(8,128)(2,1)S(1)}, bf16[528,128]{1,0:T(8,128)(2,1)S(1)}, u32[]{:S(2)}, u32[]{:S(2)}) %collective-permute-start.5) | collective-permute-done | bytes 135200 | tf_op jit(solution)/shard_map/ppermute | solution.py:54
  64.3 0.7 shard_map.114
  65.0 3.2 %collective-permute-start.8 = (bf16[512,128]{1,0:T(8,128)(2,1)S(1)}, bf16[512,128]{1,0:T(8,128)(2,1)S(1)}, u32[]{:S(2)}, u32[]{:S(2)}) collective-permute-start(bf16[512,128]{1,0:T(8,128)(2,1)S(1)} %get-tuple-element.51), channel_id=1, source_target_pairs={{0,16},{1,17},{2,18},{3,19},{4,20},{5,21},{6,22},{7,23},{8,24},{9,... | collective-permute-start | bytes 393224 | tf_op jit(solution)/shard_map/ppermute | solution.py:54
  68.2 1.0 collective-permute-done.8.got
  69.2 0.8 shard_map.115
  69.9 3.5 %all-gather.3.cloned.1.call-done = bf16[2048,256]{1,0:T(8,128)(2,1)} async-done(((bf16[512,256]{1,0:T(8,128)(2,1)}), bf16[2048,256]{1,0:T(8,128)(2,1)}) %all-gather.3.cloned.1.call-update) | async-done | bytes 1048592 | tf_op jit(solution)/shard_map/all_gather | solution.py:87
  73.5 0.0 all-gather.5.cloned.1.call-update
  73.5 7.4 %collective-permute-start.9 = (bf16[128,512]{1,0:T(8,128)(2,1)S(1)}, bf16[128,512]{1,0:T(8,128)(2,1)S(1)}, u32[]{:S(2)}, u32[]{:S(2)}) collective-permute-start(bf16[128,512]{1,0:T(8,128)(2,1)S(1)} %get-tuple-element.56.refs_0_), channel_id=1, source_target_pairs={{0,1},{1,2},{2,3},{3,0},{4,5},{5,6},{6,7},{7,4},{8,9},{9,10},{10,1... | collective-permute-start | bytes 393224 | tf_op jit(solution)/shard_map/ppermute | solution.py:54
  80.9 1.9 %collective-permute-start.12 = (bf16[128,512]{1,0:T(8,128)(2,1)S(1)}, bf16[128,512]{1,0:T(8,128)(2,1)S(1)}, u32[]{:S(2)}, u32[]{:S(2)}) collective-permute-start(bf16[128,512]{1,0:T(8,128)(2,1)S(1)} %get-tuple-element.57.refs_1_), channel_id=1, source_target_pairs={{0,3},{1,0},{2,1},{3,2},{4,7},{5,4},{6,5},{7,6},{8,11},{9,8},{10,9... | collective-permute-start | bytes 393224 | tf_op jit(solution)/shard_map/ppermute | solution.py:54
  82.8 6.1 %collective-permute-start.11 = (bf16[128,512]{1,0:T(8,128)(2,1)S(1)}, bf16[128,512]{1,0:T(8,128)(2,1)S(1)}, u32[]{:S(2)}, u32[]{:S(2)}) collective-permute-start(bf16[128,512]{1,0:T(8,128)(2,1)S(1)} %get-tuple-element.56.refs_0_), channel_id=1, source_target_pairs={{0,3},{1,0},{2,1},{3,2},{4,7},{5,4},{6,5},{7,6},{8,11},{9,8},{10,9... | collective-permute-start | bytes 393224 | tf_op jit(solution)/shard_map/ppermute | solution.py:54
  89.0 3.0 %collective-permute-start.10 = (bf16[128,512]{1,0:T(8,128)(2,1)S(1)}, bf16[128,512]{1,0:T(8,128)(2,1)S(1)}, u32[]{:S(2)}, u32[]{:S(2)}) collective-permute-start(bf16[128,512]{1,0:T(8,128)(2,1)S(1)} %get-tuple-element.57.refs_1_), channel_id=1, source_target_pairs={{0,1},{1,2},{2,3},{3,0},{4,5},{5,6},{6,7},{7,4},{8,9},{9,10},{10,1... | collective-permute-start | bytes 393224 | tf_op jit(solution)/shard_map/ppermute | solution.py:54
  92.0 7.3 %collective-permute-start.13 = (bf16[128,512]{1,0:T(8,128)(2,1)S(1)}, bf16[128,512]{1,0:T(8,128)(2,1)S(1)}, u32[]{:S(2)}, u32[]{:S(2)}) collective-permute-start(bf16[128,512]{1,0:T(8,128)(2,1)S(1)} %collective-permute-done.9.refs_2_), channel_id=1, source_target_pairs={{0,1},{1,2},{2,3},{3,0},{4,5},{5,6},{6,7},{7,4},{8,9},{9,10},{10,1... | collective-permute-start | bytes 393224 | tf_op jit(solution)/shard_map/ppermute | solution.py:54
  99.3 10.4 %collective-permute-done.12.refs_5_ = bf16[128,512]{1,0:T(8,128)(2,1)S(1)} collective-permute-done((bf16[128,512]{1,0:T(8,128)(2,1)S(1)}, bf16[128,512]{1,0:T(8,128)(2,1)S(1)}, u32[]{:S(2)}, u32[]{:S(2)}) %collective-permute-start.12) | collective-permute-done | bytes 131104 | tf_op jit(solution)/shard_map/ppermute | solution.py:54
  109.7 1.9 %collective-permute-start.14 = (bf16[128,512]{1,0:T(8,128)(2,1)S(1)}, bf16[128,512]{1,0:T(8,128)(2,1)S(1)}, u32[]{:S(2)}, u32[]{:S(2)}) collective-permute-start(bf16[128,512]{1,0:T(8,128)(2,1)S(1)} %collective-permute-done.12.refs_5_), channel_id=1, source_target_pairs={{0,3},{1,0},{2,1},{3,2},{4,7},{5,4},{6,5},{7,6},{8,11},{9,8},{10,9... | collective-permute-start | bytes 393224 | tf_op jit(solution)/shard_map/ppermute | solution.py:54
  111.6 2.8 %collective-permute-done.11.refs_4_ = bf16[128,512]{1,0:T(8,128)(2,1)S(1)} collective-permute-done((bf16[128,512]{1,0:T(8,128)(2,1)S(1)}, bf16[128,512]{1,0:T(8,128)(2,1)S(1)}, u32[]{:S(2)}, u32[]{:S(2)}) %collective-permute-start.11) | collective-permute-done | bytes 131104 | tf_op jit(solution)/shard_map/ppermute | solution.py:54
  114.4 9.3 %collective-permute-done.14.refs_7_ = bf16[128,512]{1,0:T(8,128)(2,1)S(1)} collective-permute-done((bf16[128,512]{1,0:T(8,128)(2,1)S(1)}, bf16[128,512]{1,0:T(8,128)(2,1)S(1)}, u32[]{:S(2)}, u32[]{:S(2)}) %collective-permute-start.14) | collective-permute-done | bytes 131104 | tf_op jit(solution)/shard_map/ppermute | solution.py:54
  123.6 0.7 copy-done.14
  124.3 1.2 shard_map.116
  125.5 1.0 copy-done.1
  126.5 0.6 copy-done.10
  127.1 5.6 %all-gather.5.cloned.1.call-done = bf16[16384,256]{1,0:T(8,128)(2,1)} async-done(((bf16[2048,256]{1,0:T(8,128)(2,1)}), bf16[16384,256]{1,0:T(8,128)(2,1)}) %all-gather.5.cloned.1.call-update) | async-done | bytes 8388624 | tf_op jit(solution)/shard_map/all_gather | solution.py:87
  132.7 8.8 %shard_map.117 = (bf16[272,512]{1,0:T(8,128)(2,1)}, bf16[272,512]{1,0:T(8,128)(2,1)}, bf16[272,512]{1,0:T(8,128)(2,1)}, bf16[272,512]{1,0:T(8,128)(2,1)}) custom-call(s32[7]{0:T(128)} %copy-done.7, bf16[256,2048]{1,0:T(8,128)(2,1)} %copy-done.1, bf16[16,512]{1,0:T(8,128)(2,1)} %copy-done.10, bf16[4,2,2048,256]{3,2,1,0:T(8,128)(2,1)} %bitcast.12), custom_call_target="tpu_custom_call" | custom-call | flops 2147483648 | bytes 8388608 | tf_op jit(solution)/shard_map/pallas_call | solution.py:97
  141.5 4.6 %collective-permute-start.15 = (bf16[272,512]{1,0:T(8,128)(2,1)}, bf16[272,512]{1,0:T(8,128)(2,1)S(1)}, u32[]{:S(2)}, u32[]{:S(2)}) collective-permute-start(bf16[272,512]{1,0:T(8,128)(2,1)} %get-tuple-element.62), channel_id=1, source_target_pairs={{0,8},{1,9},{2,10},{3,11},{4,12},{5,13},{6,14},{7,15},{8,0},{9,1},... | collective-permute-start | bytes 835592 | tf_op jit(solution)/shard_map/ppermute | solution.py:54
  146.2 2.2 %collective-permute-start.16 = (bf16[272,512]{1,0:T(8,128)(2,1)}, bf16[272,512]{1,0:T(8,128)(2,1)S(1)}, u32[]{:S(2)}, u32[]{:S(2)}) collective-permute-start(bf16[272,512]{1,0:T(8,128)(2,1)} %get-tuple-element.63), channel_id=1, source_target_pairs={{0,4},{1,5},{2,6},{3,7},{4,8},{5,9},{6,10},{7,11},{8,12},{9,13},{1... | collective-permute-start | bytes 835592 | tf_op jit(solution)/shard_map/ppermute | solution.py:54
  148.4 4.3 %collective-permute-start.17 = (bf16[272,512]{1,0:T(8,128)(2,1)}, bf16[272,512]{1,0:T(8,128)(2,1)S(1)}, u32[]{:S(2)}, u32[]{:S(2)}) collective-permute-start(bf16[272,512]{1,0:T(8,128)(2,1)} %get-tuple-element.64), channel_id=1, source_target_pairs={{0,12},{1,13},{2,14},{3,15},{4,0},{5,1},{6,2},{7,3},{8,4},{9,5},{1... | collective-permute-start | bytes 835592 | tf_op jit(solution)/shard_map/ppermute | solution.py:54
  152.7 0.5 collective-permute-done.15.got1
  153.1 6.5 %collective-permute-done.16.got2 = bf16[272,512]{1,0:T(8,128)(2,1)S(1)} collective-permute-done((bf16[272,512]{1,0:T(8,128)(2,1)}, bf16[272,512]{1,0:T(8,128)(2,1)S(1)}, u32[]{:S(2)}, u32[]{:S(2)}) %collective-permute-start.16) | collective-permute-done | bytes 278560 | tf_op jit(solution)/shard_map/ppermute | solution.py:54
  159.7 1.0 copy-done.4
  160.6 1.1 shard_map.118
  (26 shorter events, 0.1 us)
Async XLA Ops:
  6.5 2.6 %copy-start = (bf16[2,128,8,128]{3,2,1,0:T(8,128)(2,1)S(1)}, bf16[2,128,8,128]{3,2,1,0:T(8,128)(2,1)}, u32[]{:S(2)}) copy-start(bf16[2,128,8,128]{3,2,1,0:T(8,128)(2,1)} %param.13) | copy-start | bytes 1572868
  6.5 66.9 %all-gather.3.cloned.1.call-start = ((), (), s32[]{:S(2)}) async-start(), calls=%async_computation | async-start | bytes 1310720 | tf_op jit(solution)/shard_map/all_gather | solution.py:87
  6.5 1.0 copy-start.5
  7.5 0.7 copy-start.11
  8.4 17.0 %collective-permute-start = (bf16[512,256]{1,0:T(8,128)(2,1)S(1)}, bf16[512,256]{1,0:T(8,128)(2,1)S(1)}, u32[]{:S(2)}, u32[]{:S(2)}) collective-permute-start(bf16[512,256]{1,0:T(8,128)(2,1)S(1)} %shard_map.109), channel_id=1, source_target_pairs={{0,0},{1,64},{2,96},{3,32},{4,4},{5,68},{6,100},{7,36},{8,8},{9,72... | collective-permute-start | bytes 786440 | tf_op jit(solution)/shard_map/ppermute | solution.py:54
  11.2 121.5 %copy-start.7 = (s32[7]{0:T(128)}, s32[7]{0:T(128)S(1)}, u32[]{:S(2)}) copy-start(s32[7]{0:T(128)S(1)} %concatenate.3.meta) | copy-start | bytes 88
  11.3 1.0 copy-start.2
  12.2 0.7 copy-start.8
  12.9 0.7 copy-start.12
  15.0 9.8 %collective-permute-start.1 = (bf16[528,128]{1,0:T(8,128)(2,1)S(1)}, bf16[528,128]{1,0:T(8,128)(2,1)S(1)}, u32[]{:S(2)}, u32[]{:S(2)}) collective-permute-start(bf16[528,128]{1,0:T(8,128)(2,1)S(1)} %get-tuple-element.35), channel_id=1, source_target_pairs={{0,16},{1,17},{2,18},{3,19},{4,20},{5,21},{6,22},{7,23},{8,24},{9,... | collective-permute-start | bytes 405512 | tf_op jit(solution)/shard_map/ppermute | solution.py:54
  25.4 0.7 copy-start.16
  26.1 106.6 %all-gather.5.cloned.1.call-start = ((), (), s32[]{:S(2)}) async-start(), calls=%async_computation.1 | async-start | bytes 9437184 | tf_op jit(solution)/shard_map/all_gather | solution.py:87
  26.2 24.0 %collective-permute-start.4 = (bf16[528,128]{1,0:T(8,128)(2,1)S(1)}, bf16[528,128]{1,0:T(8,128)(2,1)S(1)}, u32[]{:S(2)}, u32[]{:S(2)}) collective-permute-start(bf16[528,128]{1,0:T(8,128)(2,1)S(1)} %get-tuple-element.40.own), channel_id=1, source_target_pairs={{0,96},{1,97},{2,98},{3,99},{4,100},{5,101},{6,102},{7,103},{8,104... | collective-permute-start | bytes 405512 | tf_op jit(solution)/shard_map/ppermute | solution.py:54
  39.3 13.1 %collective-permute-start.3 = (bf16[528,128]{1,0:T(8,128)(2,1)S(1)}, bf16[528,128]{1,0:T(8,128)(2,1)S(1)}, u32[]{:S(2)}, u32[]{:S(2)}) collective-permute-start(bf16[528,128]{1,0:T(8,128)(2,1)S(1)} %get-tuple-element.40.own), channel_id=1, source_target_pairs={{0,64},{1,65},{2,66},{3,67},{4,68},{5,69},{6,70},{7,71},{8,72},{9,... | collective-permute-start | bytes 405512 | tf_op jit(solution)/shard_map/ppermute | solution.py:54
  41.2 11.2 %collective-permute-start.2 = (bf16[528,128]{1,0:T(8,128)(2,1)S(1)}, bf16[528,128]{1,0:T(8,128)(2,1)S(1)}, u32[]{:S(2)}, u32[]{:S(2)}) collective-permute-start(bf16[528,128]{1,0:T(8,128)(2,1)S(1)} %get-tuple-element.40.own), channel_id=1, source_target_pairs={{0,32},{1,33},{2,34},{3,35},{4,36},{5,37},{6,38},{7,39},{8,40},{9,... | collective-permute-start | bytes 405512 | tf_op jit(solution)/shard_map/ppermute | solution.py:54
  43.8 1.0 copy-start.3
  44.8 0.9 copy-start.6
  45.7 0.7 copy-start.9
  46.4 0.7 copy-start.13
  47.1 0.7 copy-start.15
  53.2 8.2 %collective-permute-start.7 = (bf16[528,128]{1,0:T(8,128)(2,1)S(1)}, bf16[528,128]{1,0:T(8,128)(2,1)S(1)}, u32[]{:S(2)}, u32[]{:S(2)}) collective-permute-start(bf16[528,128]{1,0:T(8,128)(2,1)S(1)} %get-tuple-element.45), channel_id=1, source_target_pairs={{0,384},{1,385},{2,386},{3,387},{4,388},{5,389},{6,390},{7,391},{8... | collective-permute-start | bytes 405512 | tf_op jit(solution)/shard_map/ppermute | solution.py:54
  57.6 3.8 %collective-permute-start.6 = (bf16[528,128]{1,0:T(8,128)(2,1)S(1)}, bf16[528,128]{1,0:T(8,128)(2,1)S(1)}, u32[]{:S(2)}, u32[]{:S(2)}) collective-permute-start(bf16[528,128]{1,0:T(8,128)(2,1)S(1)} %get-tuple-element.45), channel_id=1, source_target_pairs={{0,256},{1,257},{2,258},{3,259},{4,260},{5,261},{6,262},{7,263},{8... | collective-permute-start | bytes 405512 | tf_op jit(solution)/shard_map/ppermute | solution.py:54
  58.9 5.4 %collective-permute-start.5 = (bf16[528,128]{1,0:T(8,128)(2,1)S(1)}, bf16[528,128]{1,0:T(8,128)(2,1)S(1)}, u32[]{:S(2)}, u32[]{:S(2)}) collective-permute-start(bf16[528,128]{1,0:T(8,128)(2,1)S(1)} %get-tuple-element.45), channel_id=1, source_target_pairs={{0,128},{1,129},{2,130},{3,131},{4,132},{5,133},{6,134},{7,135},{8... | collective-permute-start | bytes 405512 | tf_op jit(solution)/shard_map/ppermute | solution.py:54
  65.0 4.1 %collective-permute-start.8 = (bf16[512,128]{1,0:T(8,128)(2,1)S(1)}, bf16[512,128]{1,0:T(8,128)(2,1)S(1)}, u32[]{:S(2)}, u32[]{:S(2)}) collective-permute-start(bf16[512,128]{1,0:T(8,128)(2,1)S(1)} %get-tuple-element.51), channel_id=1, source_target_pairs={{0,16},{1,17},{2,18},{3,19},{4,20},{5,21},{6,22},{7,23},{8,24},{9,... | collective-permute-start | bytes 393224 | tf_op jit(solution)/shard_map/ppermute | solution.py:54
  73.5 18.5 %collective-permute-start.9 = (bf16[128,512]{1,0:T(8,128)(2,1)S(1)}, bf16[128,512]{1,0:T(8,128)(2,1)S(1)}, u32[]{:S(2)}, u32[]{:S(2)}) collective-permute-start(bf16[128,512]{1,0:T(8,128)(2,1)S(1)} %get-tuple-element.56.refs_0_), channel_id=1, source_target_pairs={{0,1},{1,2},{2,3},{3,0},{4,5},{5,6},{6,7},{7,4},{8,9},{9,10},{10,1... | collective-permute-start | bytes 393224 | tf_op jit(solution)/shard_map/ppermute | solution.py:54
  80.9 28.8 %collective-permute-start.12 = (bf16[128,512]{1,0:T(8,128)(2,1)S(1)}, bf16[128,512]{1,0:T(8,128)(2,1)S(1)}, u32[]{:S(2)}, u32[]{:S(2)}) collective-permute-start(bf16[128,512]{1,0:T(8,128)(2,1)S(1)} %get-tuple-element.57.refs_1_), channel_id=1, source_target_pairs={{0,3},{1,0},{2,1},{3,2},{4,7},{5,4},{6,5},{7,6},{8,11},{9,8},{10,9... | collective-permute-start | bytes 393224 | tf_op jit(solution)/shard_map/ppermute | solution.py:54
  82.8 31.5 %collective-permute-start.11 = (bf16[128,512]{1,0:T(8,128)(2,1)S(1)}, bf16[128,512]{1,0:T(8,128)(2,1)S(1)}, u32[]{:S(2)}, u32[]{:S(2)}) collective-permute-start(bf16[128,512]{1,0:T(8,128)(2,1)S(1)} %get-tuple-element.56.refs_0_), channel_id=1, source_target_pairs={{0,3},{1,0},{2,1},{3,2},{4,7},{5,4},{6,5},{7,6},{8,11},{9,8},{10,9... | collective-permute-start | bytes 393224 | tf_op jit(solution)/shard_map/ppermute | solution.py:54
  89.0 25.4 %collective-permute-start.10 = (bf16[128,512]{1,0:T(8,128)(2,1)S(1)}, bf16[128,512]{1,0:T(8,128)(2,1)S(1)}, u32[]{:S(2)}, u32[]{:S(2)}) collective-permute-start(bf16[128,512]{1,0:T(8,128)(2,1)S(1)} %get-tuple-element.57.refs_1_), channel_id=1, source_target_pairs={{0,1},{1,2},{2,3},{3,0},{4,5},{5,6},{6,7},{7,4},{8,9},{9,10},{10,1... | collective-permute-start | bytes 393224 | tf_op jit(solution)/shard_map/ppermute | solution.py:54
  92.0 22.3 %collective-permute-start.13 = (bf16[128,512]{1,0:T(8,128)(2,1)S(1)}, bf16[128,512]{1,0:T(8,128)(2,1)S(1)}, u32[]{:S(2)}, u32[]{:S(2)}) collective-permute-start(bf16[128,512]{1,0:T(8,128)(2,1)S(1)} %collective-permute-done.9.refs_2_), channel_id=1, source_target_pairs={{0,1},{1,2},{2,3},{3,0},{4,5},{5,6},{6,7},{7,4},{8,9},{9,10},{10,1... | collective-permute-start | bytes 393224 | tf_op jit(solution)/shard_map/ppermute | solution.py:54
  109.7 13.9 %collective-permute-start.14 = (bf16[128,512]{1,0:T(8,128)(2,1)S(1)}, bf16[128,512]{1,0:T(8,128)(2,1)S(1)}, u32[]{:S(2)}, u32[]{:S(2)}) collective-permute-start(bf16[128,512]{1,0:T(8,128)(2,1)S(1)} %collective-permute-done.12.refs_5_), channel_id=1, source_target_pairs={{0,3},{1,0},{2,1},{3,2},{4,7},{5,4},{6,5},{7,6},{8,11},{9,8},{10,9... | collective-permute-start | bytes 393224 | tf_op jit(solution)/shard_map/ppermute | solution.py:54
  123.6 0.7 copy-start.14
  125.5 1.0 copy-start.1
  126.5 0.6 copy-start.10
  141.5 11.6 %collective-permute-start.15 = (bf16[272,512]{1,0:T(8,128)(2,1)}, bf16[272,512]{1,0:T(8,128)(2,1)S(1)}, u32[]{:S(2)}, u32[]{:S(2)}) collective-permute-start(bf16[272,512]{1,0:T(8,128)(2,1)} %get-tuple-element.62), channel_id=1, source_target_pairs={{0,8},{1,9},{2,10},{3,11},{4,12},{5,13},{6,14},{7,15},{8,0},{9,1},... | collective-permute-start | bytes 835592 | tf_op jit(solution)/shard_map/ppermute | solution.py:54
  146.2 13.5 %collective-permute-start.16 = (bf16[272,512]{1,0:T(8,128)(2,1)}, bf16[272,512]{1,0:T(8,128)(2,1)S(1)}, u32[]{:S(2)}, u32[]{:S(2)}) collective-permute-start(bf16[272,512]{1,0:T(8,128)(2,1)} %get-tuple-element.63), channel_id=1, source_target_pairs={{0,4},{1,5},{2,6},{3,7},{4,8},{5,9},{6,10},{7,11},{8,12},{9,13},{1... | collective-permute-start | bytes 835592 | tf_op jit(solution)/shard_map/ppermute | solution.py:54
  148.4 11.3 %collective-permute-start.17 = (bf16[272,512]{1,0:T(8,128)(2,1)}, bf16[272,512]{1,0:T(8,128)(2,1)S(1)}, u32[]{:S(2)}, u32[]{:S(2)}) collective-permute-start(bf16[272,512]{1,0:T(8,128)(2,1)} %get-tuple-element.64), channel_id=1, source_target_pairs={{0,12},{1,13},{2,14},{3,15},{4,0},{5,1},{6,2},{7,3},{8,4},{9,5},{1... | collective-permute-start | bytes 835592 | tf_op jit(solution)/shard_map/ppermute | solution.py:54
  159.7 1.0 copy-start.4
Sparse Core Ops, SparseCore 0:
  26.2 47.1 all-gather.2
  75.6 57.0 all-gather.4

commit v3 on v2

--- a/solution.py
+++ b/solution.py
@@ -310,23 +310,12 @@
             tails[:, pl.ds(place, SPAN)] = jnp.concatenate([part, part], axis=0).astype(bf16)
 
 
-def project_kernel(meta, hidden, tails, weight, *refs):
-    outs, here, sem = refs[:NY], refs[NY], refs[NY + 1]
+def project_kernel(index, hidden, tails, weight, out):
     half = WIDTH // 2
-    order = [(d, core) for d in (2, 1, 3, 0) for core in range(NCORE)]
-    copies = []
-    for slot, (d, core) in enumerate(order):
-        copy = pltpu.make_async_copy(
-            weight.at[(meta[6] + d) % NY, core], here.at[slot], sem.at[slot]
-        )
-        copy.start()
-        copies.append(copy)
-    for out in outs:
-        out[pl.ds(TOKENS, 16), :] = tails[...]
-    for slot, (d, core) in enumerate(order):
-        copies[slot].wait()
-        total = jnp.dot(hidden[...], here[slot], preferred_element_type=f32)
-        outs[d][pl.ds(0, TOKENS), pl.ds(core * half, half)] = total.astype(bf16)
+    for core in range(NCORE):
+        total = jnp.dot(hidden[...], weight[index[0], core], preferred_element_type=f32)
+        out[pl.ds(0, TOKENS), pl.ds(core * half, half)] = total.astype(bf16)
+    out[pl.ds(TOKENS, 16), :] = tails[...]
 
 
 def finish_kernel(own, got1, got2, got3, out):
@@ -481,27 +470,24 @@
         2**24,
         2**21,
     )
-    partial = shape((TOKEN_ROWS, WIDTH), bf16)
-    blocks = NY * NCORE
-    partials = call(
-        project_kernel,
-        (partial,) * NY,
-        [SMEM, VMEM, VMEM, pl.BlockSpec(memory_space=pl.ANY)],
-        (meta, arranged, tails, weight),
-        2**31,
-        2**23,
-        [
-            pltpu.VMEM((blocks, NZH * WIDTH, WIDTH // 2), bf16),
-            pltpu.SemaphoreType.DMA((blocks,)),
-        ],
-        58 * 2**20,
-    )
-    arrived = [to_y(partials[d], d) for d in (2, 1, 3)]
+    def partial(d):
+        return call(
+            project_kernel,
+            shape((TOKEN_ROWS, WIDTH), bf16),
+            [SMEM] + [VMEM] * 3,
+            (((y + d) % NY).reshape(1), arranged, tails, weight),
+            2**29,
+            2**21,
+            (),
+            24 * 2**20,
+        )
+
+    arrived = [to_y(partial(d), d) for d in (2, 1, 3)]
     return call(
         finish_kernel,
         shape((PAIRS, SPAN, WIDTH), bf16),
         [VMEM] * 4,
-        (partials[0], *arrived),
+        (partial(0), *arrived),
         2**20,
         2**20,
     )

time: 169 us -> 165 us (0.976)
  Pallas kernels: 17.9 us -> 12 us
  local copies, waits for them, and re-layouts: 13.9 us -> 18.1 us
  waiting for transfers between devices: 45.7 us -> 42.9 us
    pallas_call x10 -> x13, Pallas kernels: 17.9 us -> 12 us  [call(): pl.pallas_call(kernel, out_shape=outs, in_specs=specs, out_specs=jax.tree...]
    ppermute x18, waiting for transfers between devices: 36.5 us -> 32.1 us  [send(): return lax.ppermute(value, ('seq', 'head'), route(move))]
    unnamed x34 -> x30, local copies, waits for them, and re-layouts: 11.8 us -> 16 us
  transfers between devices with their start and end apart: 20 -> 20, of which waited for: 11 -> 10; matrix products, arithmetic and copies ran while one was open for 1% -> 1% of each run, Pallas kernels for 5% -> 5%
where the time goes in v3:
time: 165 us; the launch traced here: 164 us
  starting transfers between devices  77.3 us (47%)
  waiting for transfers between devices  42.9 us (26%)
  local copies, waits for them, and re-layouts  18.1 us (11%)
  between operations  13.9 us (8%)
  Pallas kernels  12 us (7%)
    ppermute x18, starting transfers between devices, send(): return lax.ppermute(value, ('seq', 'head'), route(move))  77.2 us
    ppermute x18, waiting for transfers between devices, send(): return lax.ppermute(value, ('seq', 'head'), route(move))  32.1 us
    unnamed x30, local copies, waits for them, and re-layouts  16 us
    pallas_call x13, Pallas kernels, call(): pl.pallas_call(kernel, out_shape=outs, in_specs=specs, out_specs=jax.tree...  12 us
    all_gather x2, waiting for transfers between devices, gather(): lax.all_gather(block, 'seq', axis=0, tiled=True, axis_index_groups=list(g...  10.8 us
  transfers between devices with their start and end apart: 20, of which 10 were waited for; matrix products, arithmetic and copies ran while one was open for 1% of the time, Pallas kernels for 5%

profile of v3, /device:TPU:1, one launch (start us, length us, event | category | flops | bytes accessed | tf_op | source)
XLA Modules:
  0.0 164.1 jit_solution(1470946853939451799)
XLA Ops:
  6.5 1.0 copy-done.5
  7.6 0.7 copy-done.9
  8.2 0.1 shard_map.109
  8.4 0.7 collective-permute-start
  9.1 0.1 constant_dynamic-slice_fusion.1
  9.3 1.2 constant_dynamic-slice_fusion
  10.5 0.7 concatenate.3.meta
  11.3 0.0 copy-start.3
  11.3 0.9 copy-done.3
  12.2 0.7 copy-done.7
  12.9 0.7 copy-done.10
  13.6 1.4 shard_map.110
  15.0 8.8 %collective-permute-start.1 = (bf16[528,128]{1,0:T(8,128)(2,1)S(1)}, bf16[528,128]{1,0:T(8,128)(2,1)S(1)}, u32[]{:S(2)}, u32[]{:S(2)}) collective-permute-start(bf16[528,128]{1,0:T(8,128)(2,1)S(1)} %get-tuple-element.31), channel_id=1, source_target_pairs={{0,16},{1,17},{2,18},{3,19},{4,20},{5,21},{6,22},{7,23},{8,24},{9,... | collective-permute-start | bytes 405512 | tf_op jit(solution)/shard_map/ppermute | solution.py:54
  23.8 1.0 collective-permute-done.1.got
  24.8 0.6 shard_map.111
  25.4 0.0 copy-start.14
  25.4 0.7 copy-done.14
  26.1 0.0 all-gather.3.cloned.1.call-update
  26.1 0.0 all-gather.5.cloned.1.call-start
  26.2 13.1 %collective-permute-start.4 = (bf16[528,128]{1,0:T(8,128)(2,1)S(1)}, bf16[528,128]{1,0:T(8,128)(2,1)S(1)}, u32[]{:S(2)}, u32[]{:S(2)}) collective-permute-start(bf16[528,128]{1,0:T(8,128)(2,1)S(1)} %get-tuple-element.36.own), channel_id=1, source_target_pairs={{0,96},{1,97},{2,98},{3,99},{4,100},{5,101},{6,102},{7,103},{8,104... | collective-permute-start | bytes 405512 | tf_op jit(solution)/shard_map/ppermute | solution.py:54
  39.3 1.9 %collective-permute-start.3 = (bf16[528,128]{1,0:T(8,128)(2,1)S(1)}, bf16[528,128]{1,0:T(8,128)(2,1)S(1)}, u32[]{:S(2)}, u32[]{:S(2)}) collective-permute-start(bf16[528,128]{1,0:T(8,128)(2,1)S(1)} %get-tuple-element.36.own), channel_id=1, source_target_pairs={{0,64},{1,65},{2,66},{3,67},{4,68},{5,69},{6,70},{7,71},{8,72},{9,... | collective-permute-start | bytes 405512 | tf_op jit(solution)/shard_map/ppermute | solution.py:54
  41.2 2.6 %collective-permute-start.2 = (bf16[528,128]{1,0:T(8,128)(2,1)S(1)}, bf16[528,128]{1,0:T(8,128)(2,1)S(1)}, u32[]{:S(2)}, u32[]{:S(2)}) collective-permute-start(bf16[528,128]{1,0:T(8,128)(2,1)S(1)} %get-tuple-element.36.own), channel_id=1, source_target_pairs={{0,32},{1,33},{2,34},{3,35},{4,36},{5,37},{6,38},{7,39},{8,40},{9,... | collective-permute-start | bytes 405512 | tf_op jit(solution)/shard_map/ppermute | solution.py:54
  43.8 0.0 copy-start.4
  43.8 0.9 copy-done.4
  44.8 0.9 copy-done.6
  45.7 0.7 copy-done.8
  46.4 0.7 copy-done.11
  47.1 0.7 copy-done.13
  47.7 2.4 %shard_map.112 = (f32[2,128,512]{2,1,0:T(8,128)S(1)}, f32[2,128,512]{2,1,0:T(8,128)S(1)}) custom-call(s32[7]{0:T(128)S(1)} %concatenate.3.meta, f32[8]{0:T(128)S(1)} %copy-done.11, f32[8]{0:T(128)S(1)} %copy-done.13, bf16[2,128,512]{2,1,0:T(8,128)(2,1)S(1)} %copy-done.4, bf16[2,128,128]{2,1,0:T(8,128)(2,1)S(1)} %get-tuple-element.58.writes, ...), custom_call_target="tpu_custom_call" | custom-call | flops 67108864 | bytes 2097152 | tf_op jit(solution)/shard_map/pallas_call | solution.py:97
  50.2 2.2 %collective-permute-done.3.from2 = bf16[528,128]{1,0:T(8,128)(2,1)S(1)} collective-permute-done((bf16[528,128]{1,0:T(8,128)(2,1)S(1)}, bf16[528,128]{1,0:T(8,128)(2,1)S(1)}, u32[]{:S(2)}, u32[]{:S(2)}) %collective-permute-start.3) | collective-permute-done | bytes 135200 | tf_op jit(solution)/shard_map/ppermute | solution.py:54
  52.4 0.8 shard_map.113
  53.2 4.4 %collective-permute-start.7 = (bf16[528,128]{1,0:T(8,128)(2,1)S(1)}, bf16[528,128]{1,0:T(8,128)(2,1)S(1)}, u32[]{:S(2)}, u32[]{:S(2)}) collective-permute-start(bf16[528,128]{1,0:T(8,128)(2,1)S(1)} %get-tuple-element.41), channel_id=1, source_target_pairs={{0,384},{1,385},{2,386},{3,387},{4,388},{5,389},{6,390},{7,391},{8... | collective-permute-start | bytes 405512 | tf_op jit(solution)/shard_map/ppermute | solution.py:54
  57.6 1.3 collective-permute-start.6
  58.9 2.5 %collective-permute-start.5 = (bf16[528,128]{1,0:T(8,128)(2,1)S(1)}, bf16[528,128]{1,0:T(8,128)(2,1)S(1)}, u32[]{:S(2)}, u32[]{:S(2)}) collective-permute-start(bf16[528,128]{1,0:T(8,128)(2,1)S(1)} %get-tuple-element.41), channel_id=1, source_target_pairs={{0,128},{1,129},{2,130},{3,131},{4,132},{5,133},{6,134},{7,135},{8... | collective-permute-start | bytes 405512 | tf_op jit(solution)/shard_map/ppermute | solution.py:54
  61.4 2.9 %collective-permute-done.5.from1 = bf16[528,128]{1,0:T(8,128)(2,1)S(1)} collective-permute-done((bf16[528,128]{1,0:T(8,128)(2,1)S(1)}, bf16[528,128]{1,0:T(8,128)(2,1)S(1)}, u32[]{:S(2)}, u32[]{:S(2)}) %collective-permute-start.5) | collective-permute-done | bytes 135200 | tf_op jit(solution)/shard_map/ppermute | solution.py:54
  64.3 0.7 shard_map.114
  65.0 3.2 %collective-permute-start.8 = (bf16[512,128]{1,0:T(8,128)(2,1)S(1)}, bf16[512,128]{1,0:T(8,128)(2,1)S(1)}, u32[]{:S(2)}, u32[]{:S(2)}) collective-permute-start(bf16[512,128]{1,0:T(8,128)(2,1)S(1)} %get-tuple-element.47), channel_id=1, source_target_pairs={{0,16},{1,17},{2,18},{3,19},{4,20},{5,21},{6,22},{7,23},{8,24},{9,... | collective-permute-start | bytes 393224 | tf_op jit(solution)/shard_map/ppermute | solution.py:54
  68.2 1.0 collective-permute-done.8.got
  69.2 0.8 shard_map.115
  69.9 3.5 %all-gather.3.cloned.1.call-done = bf16[2048,256]{1,0:T(8,128)(2,1)} async-done(((bf16[512,256]{1,0:T(8,128)(2,1)}), bf16[2048,256]{1,0:T(8,128)(2,1)}) %all-gather.3.cloned.1.call-update) | async-done | bytes 1048592 | tf_op jit(solution)/shard_map/all_gather | solution.py:87
  73.5 0.0 all-gather.5.cloned.1.call-update
  73.5 7.4 %collective-permute-start.9 = (bf16[128,512]{1,0:T(8,128)(2,1)S(1)}, bf16[128,512]{1,0:T(8,128)(2,1)S(1)}, u32[]{:S(2)}, u32[]{:S(2)}) collective-permute-start(bf16[128,512]{1,0:T(8,128)(2,1)S(1)} %get-tuple-element.52.refs_0_), channel_id=1, source_target_pairs={{0,1},{1,2},{2,3},{3,0},{4,5},{5,6},{6,7},{7,4},{8,9},{9,10},{10,1... | collective-permute-start | bytes 393224 | tf_op jit(solution)/shard_map/ppermute | solution.py:54
  80.9 1.9 %collective-permute-start.12 = (bf16[128,512]{1,0:T(8,128)(2,1)S(1)}, bf16[128,512]{1,0:T(8,128)(2,1)S(1)}, u32[]{:S(2)}, u32[]{:S(2)}) collective-permute-start(bf16[128,512]{1,0:T(8,128)(2,1)S(1)} %get-tuple-element.53.refs_1_), channel_id=1, source_target_pairs={{0,3},{1,0},{2,1},{3,2},{4,7},{5,4},{6,5},{7,6},{8,11},{9,8},{10,9... | collective-permute-start | bytes 393224 | tf_op jit(solution)/shard_map/ppermute | solution.py:54
  82.8 6.1 %collective-permute-start.11 = (bf16[128,512]{1,0:T(8,128)(2,1)S(1)}, bf16[128,512]{1,0:T(8,128)(2,1)S(1)}, u32[]{:S(2)}, u32[]{:S(2)}) collective-permute-start(bf16[128,512]{1,0:T(8,128)(2,1)S(1)} %get-tuple-element.52.refs_0_), channel_id=1, source_target_pairs={{0,3},{1,0},{2,1},{3,2},{4,7},{5,4},{6,5},{7,6},{8,11},{9,8},{10,9... | collective-permute-start | bytes 393224 | tf_op jit(solution)/shard_map/ppermute | solution.py:54
  89.0 3.0 %collective-permute-start.10 = (bf16[128,512]{1,0:T(8,128)(2,1)S(1)}, bf16[128,512]{1,0:T(8,128)(2,1)S(1)}, u32[]{:S(2)}, u32[]{:S(2)}) collective-permute-start(bf16[128,512]{1,0:T(8,128)(2,1)S(1)} %get-tuple-element.53.refs_1_), channel_id=1, source_target_pairs={{0,1},{1,2},{2,3},{3,0},{4,5},{5,6},{6,7},{7,4},{8,9},{9,10},{10,1... | collective-permute-start | bytes 393224 | tf_op jit(solution)/shard_map/ppermute | solution.py:54
  92.0 7.3 %collective-permute-start.13 = (bf16[128,512]{1,0:T(8,128)(2,1)S(1)}, bf16[128,512]{1,0:T(8,128)(2,1)S(1)}, u32[]{:S(2)}, u32[]{:S(2)}) collective-permute-start(bf16[128,512]{1,0:T(8,128)(2,1)S(1)} %collective-permute-done.9.refs_2_), channel_id=1, source_target_pairs={{0,1},{1,2},{2,3},{3,0},{4,5},{5,6},{6,7},{7,4},{8,9},{9,10},{10,1... | collective-permute-start | bytes 393224 | tf_op jit(solution)/shard_map/ppermute | solution.py:54
  99.3 10.4 %collective-permute-done.12.refs_5_ = bf16[128,512]{1,0:T(8,128)(2,1)S(1)} collective-permute-done((bf16[128,512]{1,0:T(8,128)(2,1)S(1)}, bf16[128,512]{1,0:T(8,128)(2,1)S(1)}, u32[]{:S(2)}, u32[]{:S(2)}) %collective-permute-start.12) | collective-permute-done | bytes 131104 | tf_op jit(solution)/shard_map/ppermute | solution.py:54
  109.7 1.9 %collective-permute-start.14 = (bf16[128,512]{1,0:T(8,128)(2,1)S(1)}, bf16[128,512]{1,0:T(8,128)(2,1)S(1)}, u32[]{:S(2)}, u32[]{:S(2)}) collective-permute-start(bf16[128,512]{1,0:T(8,128)(2,1)S(1)} %collective-permute-done.12.refs_5_), channel_id=1, source_target_pairs={{0,3},{1,0},{2,1},{3,2},{4,7},{5,4},{6,5},{7,6},{8,11},{9,8},{10,9... | collective-permute-start | bytes 393224 | tf_op jit(solution)/shard_map/ppermute | solution.py:54
  111.7 2.7 %collective-permute-done.11.refs_4_ = bf16[128,512]{1,0:T(8,128)(2,1)S(1)} collective-permute-done((bf16[128,512]{1,0:T(8,128)(2,1)S(1)}, bf16[128,512]{1,0:T(8,128)(2,1)S(1)}, u32[]{:S(2)}, u32[]{:S(2)}) %collective-permute-start.11) | collective-permute-done | bytes 131104 | tf_op jit(solution)/shard_map/ppermute | solution.py:54
  114.4 9.3 %collective-permute-done.14.refs_7_ = bf16[128,512]{1,0:T(8,128)(2,1)S(1)} collective-permute-done((bf16[128,512]{1,0:T(8,128)(2,1)S(1)}, bf16[128,512]{1,0:T(8,128)(2,1)S(1)}, u32[]{:S(2)}, u32[]{:S(2)}) %collective-permute-start.14) | collective-permute-done | bytes 131104 | tf_op jit(solution)/shard_map/ppermute | solution.py:54
  123.6 0.7 copy-done.12
  124.3 1.2 shard_map.116
  125.5 7.2 %all-gather.5.cloned.1.call-done = bf16[16384,256]{1,0:T(8,128)(2,1)} async-done(((bf16[2048,256]{1,0:T(8,128)(2,1)}), bf16[16384,256]{1,0:T(8,128)(2,1)}) %all-gather.5.cloned.1.call-update) | async-done | bytes 8388624 | tf_op jit(solution)/shard_map/all_gather | solution.py:87
  132.7 3.4 %copy-done.1 = bf16[16384,256]{1,0:T(8,128)(2,1)S(1)} copy-done((bf16[16384,256]{1,0:T(8,128)(2,1)S(1)}, bf16[16384,256]{1,0:T(8,128)(2,1)}, u32[]{:S(2)}) %copy-start.1) | copy-done | bytes 8388632
  136.1 0.7 shard_map.120
  136.8 0.7 shard_map.119
  137.6 0.7 shard_map.118
  138.3 4.6 %collective-permute-start.15 = (bf16[272,512]{1,0:T(8,128)(2,1)S(1)}, bf16[272,512]{1,0:T(8,128)(2,1)S(1)}, u32[]{:S(2)}, u32[]{:S(2)}) collective-permute-start(bf16[272,512]{1,0:T(8,128)(2,1)S(1)} %shard_map.118), channel_id=1, source_target_pairs={{0,8},{1,9},{2,10},{3,11},{4,12},{5,13},{6,14},{7,15},{8,0},{9,1},... | collective-permute-start | bytes 835592 | tf_op jit(solution)/shard_map/ppermute | solution.py:54
  142.9 2.2 %collective-permute-start.16 = (bf16[272,512]{1,0:T(8,128)(2,1)S(1)}, bf16[272,512]{1,0:T(8,128)(2,1)S(1)}, u32[]{:S(2)}, u32[]{:S(2)}) collective-permute-start(bf16[272,512]{1,0:T(8,128)(2,1)S(1)} %shard_map.119), channel_id=1, source_target_pairs={{0,4},{1,5},{2,6},{3,7},{4,8},{5,9},{6,10},{7,11},{8,12},{9,13},{1... | collective-permute-start | bytes 835592 | tf_op jit(solution)/shard_map/ppermute | solution.py:54
  145.1 4.3 %collective-permute-start.17 = (bf16[272,512]{1,0:T(8,128)(2,1)S(1)}, bf16[272,512]{1,0:T(8,128)(2,1)S(1)}, u32[]{:S(2)}, u32[]{:S(2)}) collective-permute-start(bf16[272,512]{1,0:T(8,128)(2,1)S(1)} %shard_map.120), channel_id=1, source_target_pairs={{0,12},{1,13},{2,14},{3,15},{4,0},{5,1},{6,2},{7,3},{8,4},{9,5},{1... | collective-permute-start | bytes 835592 | tf_op jit(solution)/shard_map/ppermute | solution.py:54
  149.5 3.4 %copy-done.2 = bf16[16384,256]{1,0:T(8,128)(2,1)S(1)} copy-done((bf16[16384,256]{1,0:T(8,128)(2,1)S(1)}, bf16[16384,256]{1,0:T(8,128)(2,1)}, u32[]{:S(2)}) %copy-start.2) | copy-done | bytes 8388632
  152.8 0.7 shard_map.117.own
  153.6 2.6 %collective-permute-done.16.got2 = bf16[272,512]{1,0:T(8,128)(2,1)S(1)} collective-permute-done((bf16[272,512]{1,0:T(8,128)(2,1)S(1)}, bf16[272,512]{1,0:T(8,128)(2,1)S(1)}, u32[]{:S(2)}, u32[]{:S(2)}) %collective-permute-start.16) | collective-permute-done | bytes 278560 | tf_op jit(solution)/shard_map/ppermute | solution.py:54
  156.2 1.1 shard_map.121
  (25 shorter events, 0.1 us)
Async XLA Ops:
  6.5 2.6 %copy-start = (bf16[2,128,8,128]{3,2,1,0:T(8,128)(2,1)S(1)}, bf16[2,128,8,128]{3,2,1,0:T(8,128)(2,1)}, u32[]{:S(2)}) copy-start(bf16[2,128,8,128]{3,2,1,0:T(8,128)(2,1)} %param.13) | copy-start | bytes 1572868
  6.5 66.9 %all-gather.3.cloned.1.call-start = ((), (), s32[]{:S(2)}) async-start(), calls=%async_computation | async-start | bytes 1310720 | tf_op jit(solution)/shard_map/all_gather | solution.py:87
  6.5 1.0 copy-start.5
  7.5 0.7 copy-start.9
  8.4 17.0 %collective-permute-start = (bf16[512,256]{1,0:T(8,128)(2,1)S(1)}, bf16[512,256]{1,0:T(8,128)(2,1)S(1)}, u32[]{:S(2)}, u32[]{:S(2)}) collective-permute-start(bf16[512,256]{1,0:T(8,128)(2,1)S(1)} %shard_map.109), channel_id=1, source_target_pairs={{0,0},{1,64},{2,96},{3,32},{4,4},{5,68},{6,100},{7,36},{8,8},{9,72... | collective-permute-start | bytes 786440 | tf_op jit(solution)/shard_map/ppermute | solution.py:54
  11.3 1.0 copy-start.3
  12.2 0.7 copy-start.7
  12.9 0.7 copy-start.10
  15.0 9.8 %collective-permute-start.1 = (bf16[528,128]{1,0:T(8,128)(2,1)S(1)}, bf16[528,128]{1,0:T(8,128)(2,1)S(1)}, u32[]{:S(2)}, u32[]{:S(2)}) collective-permute-start(bf16[528,128]{1,0:T(8,128)(2,1)S(1)} %get-tuple-element.31), channel_id=1, source_target_pairs={{0,16},{1,17},{2,18},{3,19},{4,20},{5,21},{6,22},{7,23},{8,24},{9,... | collective-permute-start | bytes 405512 | tf_op jit(solution)/shard_map/ppermute | solution.py:54
  25.4 0.7 copy-start.14
  26.1 106.6 %all-gather.5.cloned.1.call-start = ((), (), s32[]{:S(2)}) async-start(), calls=%async_computation.1 | async-start | bytes 9437184 | tf_op jit(solution)/shard_map/all_gather | solution.py:87
  26.2 24.0 %collective-permute-start.4 = (bf16[528,128]{1,0:T(8,128)(2,1)S(1)}, bf16[528,128]{1,0:T(8,128)(2,1)S(1)}, u32[]{:S(2)}, u32[]{:S(2)}) collective-permute-start(bf16[528,128]{1,0:T(8,128)(2,1)S(1)} %get-tuple-element.36.own), channel_id=1, source_target_pairs={{0,96},{1,97},{2,98},{3,99},{4,100},{5,101},{6,102},{7,103},{8,104... | collective-permute-start | bytes 405512 | tf_op jit(solution)/shard_map/ppermute | solution.py:54
  39.3 13.1 %collective-permute-start.3 = (bf16[528,128]{1,0:T(8,128)(2,1)S(1)}, bf16[528,128]{1,0:T(8,128)(2,1)S(1)}, u32[]{:S(2)}, u32[]{:S(2)}) collective-permute-start(bf16[528,128]{1,0:T(8,128)(2,1)S(1)} %get-tuple-element.36.own), channel_id=1, source_target_pairs={{0,64},{1,65},{2,66},{3,67},{4,68},{5,69},{6,70},{7,71},{8,72},{9,... | collective-permute-start | bytes 405512 | tf_op jit(solution)/shard_map/ppermute | solution.py:54
  41.2 11.2 %collective-permute-start.2 = (bf16[528,128]{1,0:T(8,128)(2,1)S(1)}, bf16[528,128]{1,0:T(8,128)(2,1)S(1)}, u32[]{:S(2)}, u32[]{:S(2)}) collective-permute-start(bf16[528,128]{1,0:T(8,128)(2,1)S(1)} %get-tuple-element.36.own), channel_id=1, source_target_pairs={{0,32},{1,33},{2,34},{3,35},{4,36},{5,37},{6,38},{7,39},{8,40},{9,... | collective-permute-start | bytes 405512 | tf_op jit(solution)/shard_map/ppermute | solution.py:54
  43.8 1.0 copy-start.4
  44.8 0.9 copy-start.6
  45.7 0.7 copy-start.8
  46.4 0.7 copy-start.11
  47.1 0.7 copy-start.13
  53.2 8.2 %collective-permute-start.7 = (bf16[528,128]{1,0:T(8,128)(2,1)S(1)}, bf16[528,128]{1,0:T(8,128)(2,1)S(1)}, u32[]{:S(2)}, u32[]{:S(2)}) collective-permute-start(bf16[528,128]{1,0:T(8,128)(2,1)S(1)} %get-tuple-element.41), channel_id=1, source_target_pairs={{0,384},{1,385},{2,386},{3,387},{4,388},{5,389},{6,390},{7,391},{8... | collective-permute-start | bytes 405512 | tf_op jit(solution)/shard_map/ppermute | solution.py:54
  57.6 3.8 %collective-permute-start.6 = (bf16[528,128]{1,0:T(8,128)(2,1)S(1)}, bf16[528,128]{1,0:T(8,128)(2,1)S(1)}, u32[]{:S(2)}, u32[]{:S(2)}) collective-permute-start(bf16[528,128]{1,0:T(8,128)(2,1)S(1)} %get-tuple-element.41), channel_id=1, source_target_pairs={{0,256},{1,257},{2,258},{3,259},{4,260},{5,261},{6,262},{7,263},{8... | collective-permute-start | bytes 405512 | tf_op jit(solution)/shard_map/ppermute | solution.py:54
  58.9 5.4 %collective-permute-start.5 = (bf16[528,128]{1,0:T(8,128)(2,1)S(1)}, bf16[528,128]{1,0:T(8,128)(2,1)S(1)}, u32[]{:S(2)}, u32[]{:S(2)}) collective-permute-start(bf16[528,128]{1,0:T(8,128)(2,1)S(1)} %get-tuple-element.41), channel_id=1, source_target_pairs={{0,128},{1,129},{2,130},{3,131},{4,132},{5,133},{6,134},{7,135},{8... | collective-permute-start | bytes 405512 | tf_op jit(solution)/shard_map/ppermute | solution.py:54
  65.0 4.1 %collective-permute-start.8 = (bf16[512,128]{1,0:T(8,128)(2,1)S(1)}, bf16[512,128]{1,0:T(8,128)(2,1)S(1)}, u32[]{:S(2)}, u32[]{:S(2)}) collective-permute-start(bf16[512,128]{1,0:T(8,128)(2,1)S(1)} %get-tuple-element.47), channel_id=1, source_target_pairs={{0,16},{1,17},{2,18},{3,19},{4,20},{5,21},{6,22},{7,23},{8,24},{9,... | collective-permute-start | bytes 393224 | tf_op jit(solution)/shard_map/ppermute | solution.py:54
  73.5 18.5 %collective-permute-start.9 = (bf16[128,512]{1,0:T(8,128)(2,1)S(1)}, bf16[128,512]{1,0:T(8,128)(2,1)S(1)}, u32[]{:S(2)}, u32[]{:S(2)}) collective-permute-start(bf16[128,512]{1,0:T(8,128)(2,1)S(1)} %get-tuple-element.52.refs_0_), channel_id=1, source_target_pairs={{0,1},{1,2},{2,3},{3,0},{4,5},{5,6},{6,7},{7,4},{8,9},{9,10},{10,1... | collective-permute-start | bytes 393224 | tf_op jit(solution)/shard_map/ppermute | solution.py:54
  80.9 28.8 %collective-permute-start.12 = (bf16[128,512]{1,0:T(8,128)(2,1)S(1)}, bf16[128,512]{1,0:T(8,128)(2,1)S(1)}, u32[]{:S(2)}, u32[]{:S(2)}) collective-permute-start(bf16[128,512]{1,0:T(8,128)(2,1)S(1)} %get-tuple-element.53.refs_1_), channel_id=1, source_target_pairs={{0,3},{1,0},{2,1},{3,2},{4,7},{5,4},{6,5},{7,6},{8,11},{9,8},{10,9... | collective-permute-start | bytes 393224 | tf_op jit(solution)/shard_map/ppermute | solution.py:54
  82.8 31.5 %collective-permute-start.11 = (bf16[128,512]{1,0:T(8,128)(2,1)S(1)}, bf16[128,512]{1,0:T(8,128)(2,1)S(1)}, u32[]{:S(2)}, u32[]{:S(2)}) collective-permute-start(bf16[128,512]{1,0:T(8,128)(2,1)S(1)} %get-tuple-element.52.refs_0_), channel_id=1, source_target_pairs={{0,3},{1,0},{2,1},{3,2},{4,7},{5,4},{6,5},{7,6},{8,11},{9,8},{10,9... | collective-permute-start | bytes 393224 | tf_op jit(solution)/shard_map/ppermute | solution.py:54
  89.0 25.4 %collective-permute-start.10 = (bf16[128,512]{1,0:T(8,128)(2,1)S(1)}, bf16[128,512]{1,0:T(8,128)(2,1)S(1)}, u32[]{:S(2)}, u32[]{:S(2)}) collective-permute-start(bf16[128,512]{1,0:T(8,128)(2,1)S(1)} %get-tuple-element.53.refs_1_), channel_id=1, source_target_pairs={{0,1},{1,2},{2,3},{3,0},{4,5},{5,6},{6,7},{7,4},{8,9},{9,10},{10,1... | collective-permute-start | bytes 393224 | tf_op jit(solution)/shard_map/ppermute | solution.py:54
  92.0 22.3 %collective-permute-start.13 = (bf16[128,512]{1,0:T(8,128)(2,1)S(1)}, bf16[128,512]{1,0:T(8,128)(2,1)S(1)}, u32[]{:S(2)}, u32[]{:S(2)}) collective-permute-start(bf16[128,512]{1,0:T(8,128)(2,1)S(1)} %collective-permute-done.9.refs_2_), channel_id=1, source_target_pairs={{0,1},{1,2},{2,3},{3,0},{4,5},{5,6},{6,7},{7,4},{8,9},{9,10},{10,1... | collective-permute-start | bytes 393224 | tf_op jit(solution)/shard_map/ppermute | solution.py:54
  109.7 13.9 %collective-permute-start.14 = (bf16[128,512]{1,0:T(8,128)(2,1)S(1)}, bf16[128,512]{1,0:T(8,128)(2,1)S(1)}, u32[]{:S(2)}, u32[]{:S(2)}) collective-permute-start(bf16[128,512]{1,0:T(8,128)(2,1)S(1)} %collective-permute-done.12.refs_5_), channel_id=1, source_target_pairs={{0,3},{1,0},{2,1},{3,2},{4,7},{5,4},{6,5},{7,6},{8,11},{9,8},{10,9... | collective-permute-start | bytes 393224 | tf_op jit(solution)/shard_map/ppermute | solution.py:54
  123.6 0.7 copy-start.12
  132.7 3.4 %copy-start.1 = (bf16[16384,256]{1,0:T(8,128)(2,1)S(1)}, bf16[16384,256]{1,0:T(8,128)(2,1)}, u32[]{:S(2)}) copy-start(bf16[16384,256]{1,0:T(8,128)(2,1)} %all-gather.5.cloned.1.call-done) | copy-start | bytes 25165828
  138.3 15.3 %collective-permute-start.15 = (bf16[272,512]{1,0:T(8,128)(2,1)S(1)}, bf16[272,512]{1,0:T(8,128)(2,1)S(1)}, u32[]{:S(2)}, u32[]{:S(2)}) collective-permute-start(bf16[272,512]{1,0:T(8,128)(2,1)S(1)} %shard_map.118), channel_id=1, source_target_pairs={{0,8},{1,9},{2,10},{3,11},{4,12},{5,13},{6,14},{7,15},{8,0},{9,1},... | collective-permute-start | bytes 835592 | tf_op jit(solution)/shard_map/ppermute | solution.py:54
  142.9 13.3 %collective-permute-start.16 = (bf16[272,512]{1,0:T(8,128)(2,1)S(1)}, bf16[272,512]{1,0:T(8,128)(2,1)S(1)}, u32[]{:S(2)}, u32[]{:S(2)}) collective-permute-start(bf16[272,512]{1,0:T(8,128)(2,1)S(1)} %shard_map.119), channel_id=1, source_target_pairs={{0,4},{1,5},{2,6},{3,7},{4,8},{5,9},{6,10},{7,11},{8,12},{9,13},{1... | collective-permute-start | bytes 835592 | tf_op jit(solution)/shard_map/ppermute | solution.py:54
  145.1 11.1 %collective-permute-start.17 = (bf16[272,512]{1,0:T(8,128)(2,1)S(1)}, bf16[272,512]{1,0:T(8,128)(2,1)S(1)}, u32[]{:S(2)}, u32[]{:S(2)}) collective-permute-start(bf16[272,512]{1,0:T(8,128)(2,1)S(1)} %shard_map.120), channel_id=1, source_target_pairs={{0,12},{1,13},{2,14},{3,15},{4,0},{5,1},{6,2},{7,3},{8,4},{9,5},{1... | collective-permute-start | bytes 835592 | tf_op jit(solution)/shard_map/ppermute | solution.py:54
  149.4 3.4 %copy-start.2 = (bf16[16384,256]{1,0:T(8,128)(2,1)S(1)}, bf16[16384,256]{1,0:T(8,128)(2,1)}, u32[]{:S(2)}) copy-start(bf16[16384,256]{1,0:T(8,128)(2,1)} %all-gather.5.cloned.1.call-done) | copy-start | bytes 25165828
Sparse Core Ops, SparseCore 0:
  26.2 47.1 all-gather.2
  75.6 57.0 all-gather.4

commit v4 on v3

--- a/solution.py
+++ b/solution.py
@@ -322,40 +322,16 @@
     refs = (own, got1, got2, got3)
     row = lax.broadcasted_iota(jnp.int32, (SPAN, SPAN), 0)
     col = lax.broadcasted_iota(jnp.int32, (SPAN, SPAN), 1)
+    tail = pl.ds(TOKENS, 16)
+    both = sum(ref[tail, :].astype(f32) for ref in refs)
+    squares = both[:1, :TOKENS] + both[:1, TOKENS:]
+    factor = lax.rsqrt(squares / INNER + EPSILON)
     for p in range(PAIRS):
         here = pl.ds(p * SPAN, SPAN)
-        squares = jnp.zeros((16, SPAN), f32)
-        for ref in refs:
-            squares += ref[pl.ds(TOKENS, 16), pl.ds(p * SPAN, SPAN)].astype(f32)
-            squares += ref[pl.ds(TOKENS, 16), pl.ds(TOKENS + p * SPAN, SPAN)].astype(f32)
-        factor = lax.rsqrt(squares / INNER + EPSILON)
-        spread = jnp.broadcast_to(factor[:1], (SPAN, SPAN))
+        spread = jnp.broadcast_to(factor[:, p * SPAN : (p + 1) * SPAN], (SPAN, SPAN))
         turned = jnp.sum(jnp.where(row == col, spread, 0.0), axis=1, keepdims=True)
         total = sum(ref[here, :].astype(f32) for ref in refs)
         out[p] = (total * turned).astype(bf16)
-
-
-def finish_kernel(own, got1, got2, got3, out):
-    refs = (own, got1, got2, got3)
-    squares = jnp.zeros((16, TOKENS), f32)
-    for ref in refs:
-        tail = ref[pl.ds(TOKENS, 16), :].astype(f32)
-        squares += tail[:, :TOKENS] + tail[:, TOKENS:]
-    factor = lax.rsqrt(squares[:8] / INNER + EPSILON)
-    row = lax.broadcasted_iota(jnp.int32, (SPAN, SPAN), 0)
-    col = lax.broadcasted_iota(jnp.int32, (SPAN, SPAN), 1)
-    same = jnp.where(row == col, 1.0, 0.0).astype(f32)
-    for p in range(PAIRS):
-        here = pl.ds(p * SPAN, SPAN)
-        turned = lax.dot_general(
-            same,
-            factor[:, p * SPAN : (p + 1) * SPAN],
-            (((1,), (1,)), ((), ())),
-            precision=EXACT,
-            preferred_element_type=f32,
-        )
-        total = sum(ref[here, :].astype(f32) for ref in refs)
-        out[p] = (total * turned[:, :1]).astype(bf16)
 
 
 def shards(

time: 165 us -> 165 us (level)
  no operation moved by 1% of the time
where the time goes in v4:
time: 165 us; the launch traced here: 164 us
  starting transfers between devices  77.3 us (47%)
  waiting for transfers between devices  42.9 us (26%)
  local copies, waits for them, and re-layouts  18.1 us (11%)
  between operations  13.9 us (8%)
  Pallas kernels  11.8 us (7%)
    ppermute x18, starting transfers between devices, send(): return lax.ppermute(value, ('seq', 'head'), route(move))  77.2 us
    ppermute x18, waiting for transfers between devices, send(): return lax.ppermute(value, ('seq', 'head'), route(move))  32.1 us
    unnamed x30, local copies, waits for them, and re-layouts  16 us
    pallas_call x13, Pallas kernels, call(): pl.pallas_call(kernel, out_shape=outs, in_specs=specs, out_specs=jax.tree...  11.8 us
    all_gather x2, waiting for transfers between devices, gather(): lax.all_gather(block, 'seq', axis=0, tiled=True, axis_index_groups=list(g...  10.8 us
  transfers between devices with their start and end apart: 20, of which 10 were waited for; matrix products, arithmetic and copies ran while one was open for 1% of the time, Pallas kernels for 5%

profile of v4, /device:TPU:1, one launch (start us, length us, event | category | flops | bytes accessed | tf_op | source)
XLA Modules:
  0.0 163.9 jit_solution(4457542540016970700)
XLA Ops:
  6.5 1.0 copy-done.5
  7.6 0.7 copy-done.9
  8.2 0.1 shard_map.109
  8.4 0.7 collective-permute-start
  9.1 0.1 constant_dynamic-slice_fusion.1
  9.3 1.2 constant_dynamic-slice_fusion
  10.5 0.7 concatenate.3.meta
  11.3 0.0 copy-start.3
  11.3 0.9 copy-done.3
  12.2 0.7 copy-done.7
  12.9 0.7 copy-done.10
  13.6 1.4 shard_map.110
  15.0 8.8 %collective-permute-start.1 = (bf16[528,128]{1,0:T(8,128)(2,1)S(1)}, bf16[528,128]{1,0:T(8,128)(2,1)S(1)}, u32[]{:S(2)}, u32[]{:S(2)}) collective-permute-start(bf16[528,128]{1,0:T(8,128)(2,1)S(1)} %get-tuple-element.31), channel_id=1, source_target_pairs={{0,16},{1,17},{2,18},{3,19},{4,20},{5,21},{6,22},{7,23},{8,24},{9,... | collective-permute-start | bytes 405512 | tf_op jit(solution)/shard_map/ppermute | solution.py:54
  23.8 1.0 collective-permute-done.1.got
  24.8 0.6 shard_map.111
  25.4 0.0 copy-start.14
  25.4 0.7 copy-done.14
  26.1 0.0 all-gather.3.cloned.1.call-update
  26.1 0.0 all-gather.5.cloned.1.call-start
  26.2 13.1 %collective-permute-start.4 = (bf16[528,128]{1,0:T(8,128)(2,1)S(1)}, bf16[528,128]{1,0:T(8,128)(2,1)S(1)}, u32[]{:S(2)}, u32[]{:S(2)}) collective-permute-start(bf16[528,128]{1,0:T(8,128)(2,1)S(1)} %get-tuple-element.36.own), channel_id=1, source_target_pairs={{0,96},{1,97},{2,98},{3,99},{4,100},{5,101},{6,102},{7,103},{8,104... | collective-permute-start | bytes 405512 | tf_op jit(solution)/shard_map/ppermute | solution.py:54
  39.3 1.9 %collective-permute-start.3 = (bf16[528,128]{1,0:T(8,128)(2,1)S(1)}, bf16[528,128]{1,0:T(8,128)(2,1)S(1)}, u32[]{:S(2)}, u32[]{:S(2)}) collective-permute-start(bf16[528,128]{1,0:T(8,128)(2,1)S(1)} %get-tuple-element.36.own), channel_id=1, source_target_pairs={{0,64},{1,65},{2,66},{3,67},{4,68},{5,69},{6,70},{7,71},{8,72},{9,... | collective-permute-start | bytes 405512 | tf_op jit(solution)/shard_map/ppermute | solution.py:54
  41.2 2.6 %collective-permute-start.2 = (bf16[528,128]{1,0:T(8,128)(2,1)S(1)}, bf16[528,128]{1,0:T(8,128)(2,1)S(1)}, u32[]{:S(2)}, u32[]{:S(2)}) collective-permute-start(bf16[528,128]{1,0:T(8,128)(2,1)S(1)} %get-tuple-element.36.own), channel_id=1, source_target_pairs={{0,32},{1,33},{2,34},{3,35},{4,36},{5,37},{6,38},{7,39},{8,40},{9,... | collective-permute-start | bytes 405512 | tf_op jit(solution)/shard_map/ppermute | solution.py:54
  43.8 0.0 copy-start.4
  43.8 0.9 copy-done.4
  44.8 0.9 copy-done.6
  45.7 0.7 copy-done.8
  46.4 0.7 copy-done.11
  47.1 0.7 copy-done.13
  47.7 2.4 %shard_map.112 = (f32[2,128,512]{2,1,0:T(8,128)S(1)}, f32[2,128,512]{2,1,0:T(8,128)S(1)}) custom-call(s32[7]{0:T(128)S(1)} %concatenate.3.meta, f32[8]{0:T(128)S(1)} %copy-done.11, f32[8]{0:T(128)S(1)} %copy-done.13, bf16[2,128,512]{2,1,0:T(8,128)(2,1)S(1)} %copy-done.4, bf16[2,128,128]{2,1,0:T(8,128)(2,1)S(1)} %get-tuple-element.58.writes, ...), custom_call_target="tpu_custom_call" | custom-call | flops 67108864 | bytes 2097152 | tf_op jit(solution)/shard_map/pallas_call | solution.py:97
  50.2 2.2 %collective-permute-done.3.from2 = bf16[528,128]{1,0:T(8,128)(2,1)S(1)} collective-permute-done((bf16[528,128]{1,0:T(8,128)(2,1)S(1)}, bf16[528,128]{1,0:T(8,128)(2,1)S(1)}, u32[]{:S(2)}, u32[]{:S(2)}) %collective-permute-start.3) | collective-permute-done | bytes 135200 | tf_op jit(solution)/shard_map/ppermute | solution.py:54
  52.4 0.8 shard_map.113
  53.2 4.4 %collective-permute-start.7 = (bf16[528,128]{1,0:T(8,128)(2,1)S(1)}, bf16[528,128]{1,0:T(8,128)(2,1)S(1)}, u32[]{:S(2)}, u32[]{:S(2)}) collective-permute-start(bf16[528,128]{1,0:T(8,128)(2,1)S(1)} %get-tuple-element.41), channel_id=1, source_target_pairs={{0,384},{1,385},{2,386},{3,387},{4,388},{5,389},{6,390},{7,391},{8... | collective-permute-start | bytes 405512 | tf_op jit(solution)/shard_map/ppermute | solution.py:54
  57.6 1.3 collective-permute-start.6
  58.9 2.5 %collective-permute-start.5 = (bf16[528,128]{1,0:T(8,128)(2,1)S(1)}, bf16[528,128]{1,0:T(8,128)(2,1)S(1)}, u32[]{:S(2)}, u32[]{:S(2)}) collective-permute-start(bf16[528,128]{1,0:T(8,128)(2,1)S(1)} %get-tuple-element.41), channel_id=1, source_target_pairs={{0,128},{1,129},{2,130},{3,131},{4,132},{5,133},{6,134},{7,135},{8... | collective-permute-start | bytes 405512 | tf_op jit(solution)/shard_map/ppermute | solution.py:54
  61.4 2.9 %collective-permute-done.5.from1 = bf16[528,128]{1,0:T(8,128)(2,1)S(1)} collective-permute-done((bf16[528,128]{1,0:T(8,128)(2,1)S(1)}, bf16[528,128]{1,0:T(8,128)(2,1)S(1)}, u32[]{:S(2)}, u32[]{:S(2)}) %collective-permute-start.5) | collective-permute-done | bytes 135200 | tf_op jit(solution)/shard_map/ppermute | solution.py:54
  64.3 0.7 shard_map.114
  65.0 3.2 %collective-permute-start.8 = (bf16[512,128]{1,0:T(8,128)(2,1)S(1)}, bf16[512,128]{1,0:T(8,128)(2,1)S(1)}, u32[]{:S(2)}, u32[]{:S(2)}) collective-permute-start(bf16[512,128]{1,0:T(8,128)(2,1)S(1)} %get-tuple-element.47), channel_id=1, source_target_pairs={{0,16},{1,17},{2,18},{3,19},{4,20},{5,21},{6,22},{7,23},{8,24},{9,... | collective-permute-start | bytes 393224 | tf_op jit(solution)/shard_map/ppermute | solution.py:54
  68.2 1.0 collective-permute-done.8.got
  69.2 0.8 shard_map.115
  69.9 3.5 %all-gather.3.cloned.1.call-done = bf16[2048,256]{1,0:T(8,128)(2,1)} async-done(((bf16[512,256]{1,0:T(8,128)(2,1)}), bf16[2048,256]{1,0:T(8,128)(2,1)}) %all-gather.3.cloned.1.call-update) | async-done | bytes 1048592 | tf_op jit(solution)/shard_map/all_gather | solution.py:87
  73.5 0.0 all-gather.5.cloned.1.call-update
  73.5 7.4 %collective-permute-start.9 = (bf16[128,512]{1,0:T(8,128)(2,1)S(1)}, bf16[128,512]{1,0:T(8,128)(2,1)S(1)}, u32[]{:S(2)}, u32[]{:S(2)}) collective-permute-start(bf16[128,512]{1,0:T(8,128)(2,1)S(1)} %get-tuple-element.52.refs_0_), channel_id=1, source_target_pairs={{0,1},{1,2},{2,3},{3,0},{4,5},{5,6},{6,7},{7,4},{8,9},{9,10},{10,1... | collective-permute-start | bytes 393224 | tf_op jit(solution)/shard_map/ppermute | solution.py:54
  80.9 1.9 %collective-permute-start.12 = (bf16[128,512]{1,0:T(8,128)(2,1)S(1)}, bf16[128,512]{1,0:T(8,128)(2,1)S(1)}, u32[]{:S(2)}, u32[]{:S(2)}) collective-permute-start(bf16[128,512]{1,0:T(8,128)(2,1)S(1)} %get-tuple-element.53.refs_1_), channel_id=1, source_target_pairs={{0,3},{1,0},{2,1},{3,2},{4,7},{5,4},{6,5},{7,6},{8,11},{9,8},{10,9... | collective-permute-start | bytes 393224 | tf_op jit(solution)/shard_map/ppermute | solution.py:54
  82.8 6.1 %collective-permute-start.11 = (bf16[128,512]{1,0:T(8,128)(2,1)S(1)}, bf16[128,512]{1,0:T(8,128)(2,1)S(1)}, u32[]{:S(2)}, u32[]{:S(2)}) collective-permute-start(bf16[128,512]{1,0:T(8,128)(2,1)S(1)} %get-tuple-element.52.refs_0_), channel_id=1, source_target_pairs={{0,3},{1,0},{2,1},{3,2},{4,7},{5,4},{6,5},{7,6},{8,11},{9,8},{10,9... | collective-permute-start | bytes 393224 | tf_op jit(solution)/shard_map/ppermute | solution.py:54
  89.0 3.0 %collective-permute-start.10 = (bf16[128,512]{1,0:T(8,128)(2,1)S(1)}, bf16[128,512]{1,0:T(8,128)(2,1)S(1)}, u32[]{:S(2)}, u32[]{:S(2)}) collective-permute-start(bf16[128,512]{1,0:T(8,128)(2,1)S(1)} %get-tuple-element.53.refs_1_), channel_id=1, source_target_pairs={{0,1},{1,2},{2,3},{3,0},{4,5},{5,6},{6,7},{7,4},{8,9},{9,10},{10,1... | collective-permute-start | bytes 393224 | tf_op jit(solution)/shard_map/ppermute | solution.py:54
  92.0 7.3 %collective-permute-start.13 = (bf16[128,512]{1,0:T(8,128)(2,1)S(1)}, bf16[128,512]{1,0:T(8,128)(2,1)S(1)}, u32[]{:S(2)}, u32[]{:S(2)}) collective-permute-start(bf16[128,512]{1,0:T(8,128)(2,1)S(1)} %collective-permute-done.9.refs_2_), channel_id=1, source_target_pairs={{0,1},{1,2},{2,3},{3,0},{4,5},{5,6},{6,7},{7,4},{8,9},{9,10},{10,1... | collective-permute-start | bytes 393224 | tf_op jit(solution)/shard_map/ppermute | solution.py:54
  99.3 10.4 %collective-permute-done.12.refs_5_ = bf16[128,512]{1,0:T(8,128)(2,1)S(1)} collective-permute-done((bf16[128,512]{1,0:T(8,128)(2,1)S(1)}, bf16[128,512]{1,0:T(8,128)(2,1)S(1)}, u32[]{:S(2)}, u32[]{:S(2)}) %collective-permute-start.12) | collective-permute-done | bytes 131104 | tf_op jit(solution)/shard_map/ppermute | solution.py:54
  109.7 1.9 %collective-permute-start.14 = (bf16[128,512]{1,0:T(8,128)(2,1)S(1)}, bf16[128,512]{1,0:T(8,128)(2,1)S(1)}, u32[]{:S(2)}, u32[]{:S(2)}) collective-permute-start(bf16[128,512]{1,0:T(8,128)(2,1)S(1)} %collective-permute-done.12.refs_5_), channel_id=1, source_target_pairs={{0,3},{1,0},{2,1},{3,2},{4,7},{5,4},{6,5},{7,6},{8,11},{9,8},{10,9... | collective-permute-start | bytes 393224 | tf_op jit(solution)/shard_map/ppermute | solution.py:54
  111.7 2.7 %collective-permute-done.11.refs_4_ = bf16[128,512]{1,0:T(8,128)(2,1)S(1)} collective-permute-done((bf16[128,512]{1,0:T(8,128)(2,1)S(1)}, bf16[128,512]{1,0:T(8,128)(2,1)S(1)}, u32[]{:S(2)}, u32[]{:S(2)}) %collective-permute-start.11) | collective-permute-done | bytes 131104 | tf_op jit(solution)/shard_map/ppermute | solution.py:54
  114.4 9.3 %collective-permute-done.14.refs_7_ = bf16[128,512]{1,0:T(8,128)(2,1)S(1)} collective-permute-done((bf16[128,512]{1,0:T(8,128)(2,1)S(1)}, bf16[128,512]{1,0:T(8,128)(2,1)S(1)}, u32[]{:S(2)}, u32[]{:S(2)}) %collective-permute-start.14) | collective-permute-done | bytes 131104 | tf_op jit(solution)/shard_map/ppermute | solution.py:54
  123.6 0.7 copy-done.12
  124.3 1.2 shard_map.116
  125.5 7.2 %all-gather.5.cloned.1.call-done = bf16[16384,256]{1,0:T(8,128)(2,1)} async-done(((bf16[2048,256]{1,0:T(8,128)(2,1)}), bf16[16384,256]{1,0:T(8,128)(2,1)}) %all-gather.5.cloned.1.call-update) | async-done | bytes 8388624 | tf_op jit(solution)/shard_map/all_gather | solution.py:87
  132.7 3.4 %copy-done.1 = bf16[16384,256]{1,0:T(8,128)(2,1)S(1)} copy-done((bf16[16384,256]{1,0:T(8,128)(2,1)S(1)}, bf16[16384,256]{1,0:T(8,128)(2,1)}, u32[]{:S(2)}) %copy-start.1) | copy-done | bytes 8388632
  136.1 0.7 shard_map.120
  136.8 0.7 shard_map.119
  137.6 0.7 shard_map.118
  138.3 4.6 %collective-permute-start.15 = (bf16[272,512]{1,0:T(8,128)(2,1)S(1)}, bf16[272,512]{1,0:T(8,128)(2,1)S(1)}, u32[]{:S(2)}, u32[]{:S(2)}) collective-permute-start(bf16[272,512]{1,0:T(8,128)(2,1)S(1)} %shard_map.118), channel_id=1, source_target_pairs={{0,8},{1,9},{2,10},{3,11},{4,12},{5,13},{6,14},{7,15},{8,0},{9,1},... | collective-permute-start | bytes 835592 | tf_op jit(solution)/shard_map/ppermute | solution.py:54
  142.9 2.2 %collective-permute-start.16 = (bf16[272,512]{1,0:T(8,128)(2,1)S(1)}, bf16[272,512]{1,0:T(8,128)(2,1)S(1)}, u32[]{:S(2)}, u32[]{:S(2)}) collective-permute-start(bf16[272,512]{1,0:T(8,128)(2,1)S(1)} %shard_map.119), channel_id=1, source_target_pairs={{0,4},{1,5},{2,6},{3,7},{4,8},{5,9},{6,10},{7,11},{8,12},{9,13},{1... | collective-permute-start | bytes 835592 | tf_op jit(solution)/shard_map/ppermute | solution.py:54
  145.1 4.3 %collective-permute-start.17 = (bf16[272,512]{1,0:T(8,128)(2,1)S(1)}, bf16[272,512]{1,0:T(8,128)(2,1)S(1)}, u32[]{:S(2)}, u32[]{:S(2)}) collective-permute-start(bf16[272,512]{1,0:T(8,128)(2,1)S(1)} %shard_map.120), channel_id=1, source_target_pairs={{0,12},{1,13},{2,14},{3,15},{4,0},{5,1},{6,2},{7,3},{8,4},{9,5},{1... | collective-permute-start | bytes 835592 | tf_op jit(solution)/shard_map/ppermute | solution.py:54
  149.5 3.4 %copy-done.2 = bf16[16384,256]{1,0:T(8,128)(2,1)S(1)} copy-done((bf16[16384,256]{1,0:T(8,128)(2,1)S(1)}, bf16[16384,256]{1,0:T(8,128)(2,1)}, u32[]{:S(2)}) %copy-start.2) | copy-done | bytes 8388632
  152.8 0.7 shard_map.117.own
  153.6 2.6 %collective-permute-done.16.got2 = bf16[272,512]{1,0:T(8,128)(2,1)S(1)} collective-permute-done((bf16[272,512]{1,0:T(8,128)(2,1)S(1)}, bf16[272,512]{1,0:T(8,128)(2,1)S(1)}, u32[]{:S(2)}, u32[]{:S(2)}) %collective-permute-start.16) | collective-permute-done | bytes 278560 | tf_op jit(solution)/shard_map/ppermute | solution.py:54
  156.2 0.9 shard_map.121
  (25 shorter events, 0.1 us)
Async XLA Ops:
  6.5 2.6 %copy-start = (bf16[2,128,8,128]{3,2,1,0:T(8,128)(2,1)S(1)}, bf16[2,128,8,128]{3,2,1,0:T(8,128)(2,1)}, u32[]{:S(2)}) copy-start(bf16[2,128,8,128]{3,2,1,0:T(8,128)(2,1)} %param.13) | copy-start | bytes 1572868
  6.5 66.9 %all-gather.3.cloned.1.call-start = ((), (), s32[]{:S(2)}) async-start(), calls=%async_computation | async-start | bytes 1310720 | tf_op jit(solution)/shard_map/all_gather | solution.py:87
  6.5 1.0 copy-start.5
  7.5 0.7 copy-start.9
  8.4 17.0 %collective-permute-start = (bf16[512,256]{1,0:T(8,128)(2,1)S(1)}, bf16[512,256]{1,0:T(8,128)(2,1)S(1)}, u32[]{:S(2)}, u32[]{:S(2)}) collective-permute-start(bf16[512,256]{1,0:T(8,128)(2,1)S(1)} %shard_map.109), channel_id=1, source_target_pairs={{0,0},{1,64},{2,96},{3,32},{4,4},{5,68},{6,100},{7,36},{8,8},{9,72... | collective-permute-start | bytes 786440 | tf_op jit(solution)/shard_map/ppermute | solution.py:54
  11.3 1.0 copy-start.3
  12.2 0.7 copy-start.7
  12.9 0.7 copy-start.10
  15.0 9.8 %collective-permute-start.1 = (bf16[528,128]{1,0:T(8,128)(2,1)S(1)}, bf16[528,128]{1,0:T(8,128)(2,1)S(1)}, u32[]{:S(2)}, u32[]{:S(2)}) collective-permute-start(bf16[528,128]{1,0:T(8,128)(2,1)S(1)} %get-tuple-element.31), channel_id=1, source_target_pairs={{0,16},{1,17},{2,18},{3,19},{4,20},{5,21},{6,22},{7,23},{8,24},{9,... | collective-permute-start | bytes 405512 | tf_op jit(solution)/shard_map/ppermute | solution.py:54
  25.4 0.7 copy-start.14
  26.1 106.6 %all-gather.5.cloned.1.call-start = ((), (), s32[]{:S(2)}) async-start(), calls=%async_computation.1 | async-start | bytes 9437184 | tf_op jit(solution)/shard_map/all_gather | solution.py:87
  26.2 24.0 %collective-permute-start.4 = (bf16[528,128]{1,0:T(8,128)(2,1)S(1)}, bf16[528,128]{1,0:T(8,128)(2,1)S(1)}, u32[]{:S(2)}, u32[]{:S(2)}) collective-permute-start(bf16[528,128]{1,0:T(8,128)(2,1)S(1)} %get-tuple-element.36.own), channel_id=1, source_target_pairs={{0,96},{1,97},{2,98},{3,99},{4,100},{5,101},{6,102},{7,103},{8,104... | collective-permute-start | bytes 405512 | tf_op jit(solution)/shard_map/ppermute | solution.py:54
  39.3 13.1 %collective-permute-start.3 = (bf16[528,128]{1,0:T(8,128)(2,1)S(1)}, bf16[528,128]{1,0:T(8,128)(2,1)S(1)}, u32[]{:S(2)}, u32[]{:S(2)}) collective-permute-start(bf16[528,128]{1,0:T(8,128)(2,1)S(1)} %get-tuple-element.36.own), channel_id=1, source_target_pairs={{0,64},{1,65},{2,66},{3,67},{4,68},{5,69},{6,70},{7,71},{8,72},{9,... | collective-permute-start | bytes 405512 | tf_op jit(solution)/shard_map/ppermute | solution.py:54
  41.2 11.2 %collective-permute-start.2 = (bf16[528,128]{1,0:T(8,128)(2,1)S(1)}, bf16[528,128]{1,0:T(8,128)(2,1)S(1)}, u32[]{:S(2)}, u32[]{:S(2)}) collective-permute-start(bf16[528,128]{1,0:T(8,128)(2,1)S(1)} %get-tuple-element.36.own), channel_id=1, source_target_pairs={{0,32},{1,33},{2,34},{3,35},{4,36},{5,37},{6,38},{7,39},{8,40},{9,... | collective-permute-start | bytes 405512 | tf_op jit(solution)/shard_map/ppermute | solution.py:54
  43.8 1.0 copy-start.4
  44.8 0.9 copy-start.6
  45.7 0.7 copy-start.8
  46.4 0.7 copy-start.11
  47.1 0.7 copy-start.13
  53.2 8.2 %collective-permute-start.7 = (bf16[528,128]{1,0:T(8,128)(2,1)S(1)}, bf16[528,128]{1,0:T(8,128)(2,1)S(1)}, u32[]{:S(2)}, u32[]{:S(2)}) collective-permute-start(bf16[528,128]{1,0:T(8,128)(2,1)S(1)} %get-tuple-element.41), channel_id=1, source_target_pairs={{0,384},{1,385},{2,386},{3,387},{4,388},{5,389},{6,390},{7,391},{8... | collective-permute-start | bytes 405512 | tf_op jit(solution)/shard_map/ppermute | solution.py:54
  57.6 3.8 %collective-permute-start.6 = (bf16[528,128]{1,0:T(8,128)(2,1)S(1)}, bf16[528,128]{1,0:T(8,128)(2,1)S(1)}, u32[]{:S(2)}, u32[]{:S(2)}) collective-permute-start(bf16[528,128]{1,0:T(8,128)(2,1)S(1)} %get-tuple-element.41), channel_id=1, source_target_pairs={{0,256},{1,257},{2,258},{3,259},{4,260},{5,261},{6,262},{7,263},{8... | collective-permute-start | bytes 405512 | tf_op jit(solution)/shard_map/ppermute | solution.py:54
  58.9 5.4 %collective-permute-start.5 = (bf16[528,128]{1,0:T(8,128)(2,1)S(1)}, bf16[528,128]{1,0:T(8,128)(2,1)S(1)}, u32[]{:S(2)}, u32[]{:S(2)}) collective-permute-start(bf16[528,128]{1,0:T(8,128)(2,1)S(1)} %get-tuple-element.41), channel_id=1, source_target_pairs={{0,128},{1,129},{2,130},{3,131},{4,132},{5,133},{6,134},{7,135},{8... | collective-permute-start | bytes 405512 | tf_op jit(solution)/shard_map/ppermute | solution.py:54
  65.0 4.1 %collective-permute-start.8 = (bf16[512,128]{1,0:T(8,128)(2,1)S(1)}, bf16[512,128]{1,0:T(8,128)(2,1)S(1)}, u32[]{:S(2)}, u32[]{:S(2)}) collective-permute-start(bf16[512,128]{1,0:T(8,128)(2,1)S(1)} %get-tuple-element.47), channel_id=1, source_target_pairs={{0,16},{1,17},{2,18},{3,19},{4,20},{5,21},{6,22},{7,23},{8,24},{9,... | collective-permute-start | bytes 393224 | tf_op jit(solution)/shard_map/ppermute | solution.py:54
  73.5 18.5 %collective-permute-start.9 = (bf16[128,512]{1,0:T(8,128)(2,1)S(1)}, bf16[128,512]{1,0:T(8,128)(2,1)S(1)}, u32[]{:S(2)}, u32[]{:S(2)}) collective-permute-start(bf16[128,512]{1,0:T(8,128)(2,1)S(1)} %get-tuple-element.52.refs_0_), channel_id=1, source_target_pairs={{0,1},{1,2},{2,3},{3,0},{4,5},{5,6},{6,7},{7,4},{8,9},{9,10},{10,1... | collective-permute-start | bytes 393224 | tf_op jit(solution)/shard_map/ppermute | solution.py:54
  80.9 28.8 %collective-permute-start.12 = (bf16[128,512]{1,0:T(8,128)(2,1)S(1)}, bf16[128,512]{1,0:T(8,128)(2,1)S(1)}, u32[]{:S(2)}, u32[]{:S(2)}) collective-permute-start(bf16[128,512]{1,0:T(8,128)(2,1)S(1)} %get-tuple-element.53.refs_1_), channel_id=1, source_target_pairs={{0,3},{1,0},{2,1},{3,2},{4,7},{5,4},{6,5},{7,6},{8,11},{9,8},{10,9... | collective-permute-start | bytes 393224 | tf_op jit(solution)/shard_map/ppermute | solution.py:54
  82.8 31.5 %collective-permute-start.11 = (bf16[128,512]{1,0:T(8,128)(2,1)S(1)}, bf16[128,512]{1,0:T(8,128)(2,1)S(1)}, u32[]{:S(2)}, u32[]{:S(2)}) collective-permute-start(bf16[128,512]{1,0:T(8,128)(2,1)S(1)} %get-tuple-element.52.refs_0_), channel_id=1, source_target_pairs={{0,3},{1,0},{2,1},{3,2},{4,7},{5,4},{6,5},{7,6},{8,11},{9,8},{10,9... | collective-permute-start | bytes 393224 | tf_op jit(solution)/shard_map/ppermute | solution.py:54
  89.0 25.4 %collective-permute-start.10 = (bf16[128,512]{1,0:T(8,128)(2,1)S(1)}, bf16[128,512]{1,0:T(8,128)(2,1)S(1)}, u32[]{:S(2)}, u32[]{:S(2)}) collective-permute-start(bf16[128,512]{1,0:T(8,128)(2,1)S(1)} %get-tuple-element.53.refs_1_), channel_id=1, source_target_pairs={{0,1},{1,2},{2,3},{3,0},{4,5},{5,6},{6,7},{7,4},{8,9},{9,10},{10,1... | collective-permute-start | bytes 393224 | tf_op jit(solution)/shard_map/ppermute | solution.py:54
  92.0 22.3 %collective-permute-start.13 = (bf16[128,512]{1,0:T(8,128)(2,1)S(1)}, bf16[128,512]{1,0:T(8,128)(2,1)S(1)}, u32[]{:S(2)}, u32[]{:S(2)}) collective-permute-start(bf16[128,512]{1,0:T(8,128)(2,1)S(1)} %collective-permute-done.9.refs_2_), channel_id=1, source_target_pairs={{0,1},{1,2},{2,3},{3,0},{4,5},{5,6},{6,7},{7,4},{8,9},{9,10},{10,1... | collective-permute-start | bytes 393224 | tf_op jit(solution)/shard_map/ppermute | solution.py:54
  109.7 13.9 %collective-permute-start.14 = (bf16[128,512]{1,0:T(8,128)(2,1)S(1)}, bf16[128,512]{1,0:T(8,128)(2,1)S(1)}, u32[]{:S(2)}, u32[]{:S(2)}) collective-permute-start(bf16[128,512]{1,0:T(8,128)(2,1)S(1)} %collective-permute-done.12.refs_5_), channel_id=1, source_target_pairs={{0,3},{1,0},{2,1},{3,2},{4,7},{5,4},{6,5},{7,6},{8,11},{9,8},{10,9... | collective-permute-start | bytes 393224 | tf_op jit(solution)/shard_map/ppermute | solution.py:54
  123.6 0.7 copy-start.12
  132.7 3.4 %copy-start.1 = (bf16[16384,256]{1,0:T(8,128)(2,1)S(1)}, bf16[16384,256]{1,0:T(8,128)(2,1)}, u32[]{:S(2)}) copy-start(bf16[16384,256]{1,0:T(8,128)(2,1)} %all-gather.5.cloned.1.call-done) | copy-start | bytes 25165828
  138.3 15.3 %collective-permute-start.15 = (bf16[272,512]{1,0:T(8,128)(2,1)S(1)}, bf16[272,512]{1,0:T(8,128)(2,1)S(1)}, u32[]{:S(2)}, u32[]{:S(2)}) collective-permute-start(bf16[272,512]{1,0:T(8,128)(2,1)S(1)} %shard_map.118), channel_id=1, source_target_pairs={{0,8},{1,9},{2,10},{3,11},{4,12},{5,13},{6,14},{7,15},{8,0},{9,1},... | collective-permute-start | bytes 835592 | tf_op jit(solution)/shard_map/ppermute | solution.py:54
  142.9 13.3 %collective-permute-start.16 = (bf16[272,512]{1,0:T(8,128)(2,1)S(1)}, bf16[272,512]{1,0:T(8,128)(2,1)S(1)}, u32[]{:S(2)}, u32[]{:S(2)}) collective-permute-start(bf16[272,512]{1,0:T(8,128)(2,1)S(1)} %shard_map.119), channel_id=1, source_target_pairs={{0,4},{1,5},{2,6},{3,7},{4,8},{5,9},{6,10},{7,11},{8,12},{9,13},{1... | collective-permute-start | bytes 835592 | tf_op jit(solution)/shard_map/ppermute | solution.py:54
  145.1 11.1 %collective-permute-start.17 = (bf16[272,512]{1,0:T(8,128)(2,1)S(1)}, bf16[272,512]{1,0:T(8,128)(2,1)S(1)}, u32[]{:S(2)}, u32[]{:S(2)}) collective-permute-start(bf16[272,512]{1,0:T(8,128)(2,1)S(1)} %shard_map.120), channel_id=1, source_target_pairs={{0,12},{1,13},{2,14},{3,15},{4,0},{5,1},{6,2},{7,3},{8,4},{9,5},{1... | collective-permute-start | bytes 835592 | tf_op jit(solution)/shard_map/ppermute | solution.py:54
  149.4 3.4 %copy-start.2 = (bf16[16384,256]{1,0:T(8,128)(2,1)S(1)}, bf16[16384,256]{1,0:T(8,128)(2,1)}, u32[]{:S(2)}) copy-start(bf16[16384,256]{1,0:T(8,128)(2,1)} %all-gather.5.cloned.1.call-done) | copy-start | bytes 25165828
Sparse Core Ops, SparseCore 0:
  26.2 47.1 all-gather.2
  75.6 57.0 all-gather.4

commit v5 on v4

--- a/solution.py
+++ b/solution.py
@@ -446,24 +446,26 @@
         2**24,
         2**21,
     )
-    def partial(d):
+    def partial(target, weights, flops=2**29):
         return call(
             project_kernel,
             shape((TOKEN_ROWS, WIDTH), bf16),
             [SMEM] + [VMEM] * 3,
-            (((y + d) % NY).reshape(1), arranged, tails, weight),
-            2**29,
+            (target.reshape(1), arranged, tails, weights),
+            flops,
             2**21,
             (),
             24 * 2**20,
         )
 
-    arrived = [to_y(partial(d), d) for d in (2, 1, 3)]
+    first_weight = lax.dynamic_slice_in_dim(weight, (y + 2) % NY, 1, 0)
+    sent = to_y(partial(jnp.zeros((), jnp.int32), first_weight, 2**33), 2)
+    arrived = [sent] + [to_y(partial((y + d) % NY, weight), d) for d in (1, 3)]
     return call(
         finish_kernel,
         shape((PAIRS, SPAN, WIDTH), bf16),
         [VMEM] * 4,
-        (partial(0), *arrived),
+        (partial(y, weight), *arrived),
         2**20,
         2**20,
     )

time: 165 us -> 163 us (0.988)
  local copies, waits for them, and re-layouts: 18.1 us -> 13.2 us
  starting transfers between devices: 77.3 us -> 80.1 us
    unnamed x30, local copies, waits for them, and re-layouts: 16 us -> 9.25 us
    ppermute x18, waiting for transfers between devices: 32.1 us -> 26.3 us  [send(): return lax.ppermute(value, ('seq', 'head'), route(move))]
    all_gather x2, waiting for transfers between devices: 10.8 us -> 15.5 us  [gather(): lax.all_gather(block, 'seq', axis=0, tiled=True, axis_index_groups=list(g...]
    ppermute x18, starting transfers between devices: 77.2 us -> 80.1 us  [send(): return lax.ppermute(value, ('seq', 'head'), route(move))]
    dynamic_slice x0 -> x1, local copies, waits for them, and re-layouts: none -> 1.88 us  [shards(): first_weight = lax.dynamic_slice_in_dim(weight, (y + 2) % NY, 1, 0)]
  transfers between devices with their start and end apart: 20 -> 20, of which waited for: 10 -> 13; matrix products, arithmetic and copies ran while one was open for 1% -> 1% of each run, Pallas kernels for 5% -> 6%
where the time goes in v5:
time: 163 us; the launch traced here: 161 us
  starting transfers between devices  80.1 us (49%)
  waiting for transfers between devices  41.8 us (26%)
  between operations  13.9 us (9%)
  local copies, waits for them, and re-layouts  13.2 us (8%)
  Pallas kernels  11.8 us (7%)
    ppermute x18, starting transfers between devices, send(): return lax.ppermute(value, ('seq', 'head'), route(move))  80.1 us
    ppermute x18, waiting for transfers between devices, send(): return lax.ppermute(value, ('seq', 'head'), route(move))  26.3 us
    all_gather x2, waiting for transfers between devices, gather(): lax.all_gather(block, 'seq', axis=0, tiled=True, axis_index_groups=list(g...  15.5 us
    pallas_call x13, Pallas kernels, call(): pl.pallas_call(kernel, out_shape=outs, in_specs=specs, out_specs=jax.tree...  11.8 us
    unnamed x30, local copies, waits for them, and re-layouts  9.25 us
  transfers between devices with their start and end apart: 20, of which 13 were waited for; matrix products, arithmetic and copies ran while one was open for 1% of the time, Pallas kernels for 6%

profile of v5, /device:TPU:1, one launch (start us, length us, event | category | flops | bytes accessed | tf_op | source)
XLA Modules:
  0.0 160.9 jit_solution(15605835895236799526)
XLA Ops:
  6.5 1.0 copy-done.3
  7.6 0.7 copy-done.7
  8.2 0.1 shard_map.109
  8.4 0.7 collective-permute-start
  9.1 0.1 constant_dynamic-slice_fusion.1
  9.3 1.2 constant_dynamic-slice_fusion.2
  10.5 0.7 concatenate.3.meta
  11.3 0.9 copy-done.1
  12.2 0.7 copy-done.5
  12.9 0.7 copy-done.8
  13.6 1.4 shard_map.110
  15.0 8.8 %collective-permute-start.1 = (bf16[528,128]{1,0:T(8,128)(2,1)S(1)}, bf16[528,128]{1,0:T(8,128)(2,1)S(1)}, u32[]{:S(2)}, u32[]{:S(2)}) collective-permute-start(bf16[528,128]{1,0:T(8,128)(2,1)S(1)} %get-tuple-element.31), channel_id=1, source_target_pairs={{0,16},{1,17},{2,18},{3,19},{4,20},{5,21},{6,22},{7,23},{8,24},{9,... | collective-permute-start | bytes 405512 | tf_op jit(solution)/shard_map/ppermute | solution.py:54
  23.8 1.0 collective-permute-done.1.got
  24.8 0.6 shard_map.111
  25.4 0.0 copy-start.12
  25.4 0.7 copy-done.12
  26.1 0.0 all-gather.3.cloned.1.call-update
  26.1 0.0 all-gather.5.cloned.1.call-start
  26.2 11.0 %collective-permute-start.2 = (bf16[528,128]{1,0:T(8,128)(2,1)S(1)}, bf16[528,128]{1,0:T(8,128)(2,1)S(1)}, u32[]{:S(2)}, u32[]{:S(2)}) collective-permute-start(bf16[528,128]{1,0:T(8,128)(2,1)S(1)} %get-tuple-element.36.own), channel_id=1, source_target_pairs={{0,32},{1,33},{2,34},{3,35},{4,36},{5,37},{6,38},{7,39},{8,40},{9,... | collective-permute-start | bytes 405512 | tf_op jit(solution)/shard_map/ppermute | solution.py:54
  37.2 4.3 %collective-permute-start.3 = (bf16[528,128]{1,0:T(8,128)(2,1)S(1)}, bf16[528,128]{1,0:T(8,128)(2,1)S(1)}, u32[]{:S(2)}, u32[]{:S(2)}) collective-permute-start(bf16[528,128]{1,0:T(8,128)(2,1)S(1)} %get-tuple-element.36.own), channel_id=1, source_target_pairs={{0,64},{1,65},{2,66},{3,67},{4,68},{5,69},{6,70},{7,71},{8,72},{9,... | collective-permute-start | bytes 405512 | tf_op jit(solution)/shard_map/ppermute | solution.py:54
  41.5 3.2 %collective-permute-start.4 = (bf16[528,128]{1,0:T(8,128)(2,1)S(1)}, bf16[528,128]{1,0:T(8,128)(2,1)S(1)}, u32[]{:S(2)}, u32[]{:S(2)}) collective-permute-start(bf16[528,128]{1,0:T(8,128)(2,1)S(1)} %get-tuple-element.36.own), channel_id=1, source_target_pairs={{0,96},{1,97},{2,98},{3,99},{4,100},{5,101},{6,102},{7,103},{8,104... | collective-permute-start | bytes 405512 | tf_op jit(solution)/shard_map/ppermute | solution.py:54
  44.7 0.9 copy-done.2
  45.7 0.9 copy-done.4
  46.6 0.7 copy-done.6
  47.3 0.7 copy-done.9
  48.0 0.7 copy-done.11
  48.6 2.4 %shard_map.112 = (f32[2,128,512]{2,1,0:T(8,128)S(1)}, f32[2,128,512]{2,1,0:T(8,128)S(1)}) custom-call(s32[7]{0:T(128)S(1)} %concatenate.3.meta, f32[8]{0:T(128)S(1)} %copy-done.9, f32[8]{0:T(128)S(1)} %copy-done.11, bf16[2,128,512]{2,1,0:T(8,128)(2,1)S(1)} %copy-done.2, bf16[2,128,128]{2,1,0:T(8,128)(2,1)S(1)} %get-tuple-element.58.writes, ...), custom_call_target="tpu_custom_call" | custom-call | flops 67108864 | bytes 2097152 | tf_op jit(solution)/shard_map/pallas_call | solution.py:97
  51.1 0.8 shard_map.113
  51.9 3.1 %collective-permute-start.5 = (bf16[528,128]{1,0:T(8,128)(2,1)S(1)}, bf16[528,128]{1,0:T(8,128)(2,1)S(1)}, u32[]{:S(2)}, u32[]{:S(2)}) collective-permute-start(bf16[528,128]{1,0:T(8,128)(2,1)S(1)} %get-tuple-element.41), channel_id=1, source_target_pairs={{0,128},{1,129},{2,130},{3,131},{4,132},{5,133},{6,134},{7,135},{8... | collective-permute-start | bytes 405512 | tf_op jit(solution)/shard_map/ppermute | solution.py:54
  55.0 4.4 %collective-permute-start.6 = (bf16[528,128]{1,0:T(8,128)(2,1)S(1)}, bf16[528,128]{1,0:T(8,128)(2,1)S(1)}, u32[]{:S(2)}, u32[]{:S(2)}) collective-permute-start(bf16[528,128]{1,0:T(8,128)(2,1)S(1)} %get-tuple-element.41), channel_id=1, source_target_pairs={{0,256},{1,257},{2,258},{3,259},{4,260},{5,261},{6,262},{7,263},{8... | collective-permute-start | bytes 405512 | tf_op jit(solution)/shard_map/ppermute | solution.py:54
  59.4 1.3 collective-permute-start.7
  60.7 0.6 collective-permute-done.6.from2
  61.3 1.6 collective-permute-done.7.from3
  62.9 0.7 shard_map.114
  63.6 4.0 %collective-permute-start.8 = (bf16[512,128]{1,0:T(8,128)(2,1)S(1)}, bf16[512,128]{1,0:T(8,128)(2,1)S(1)}, u32[]{:S(2)}, u32[]{:S(2)}) collective-permute-start(bf16[512,128]{1,0:T(8,128)(2,1)S(1)} %get-tuple-element.47), channel_id=1, source_target_pairs={{0,16},{1,17},{2,18},{3,19},{4,20},{5,21},{6,22},{7,23},{8,24},{9,... | collective-permute-start | bytes 393224 | tf_op jit(solution)/shard_map/ppermute | solution.py:54
  67.6 1.0 collective-permute-done.8.got
  68.6 0.8 shard_map.115
  69.3 4.0 %all-gather.3.cloned.1.call-done = bf16[2048,256]{1,0:T(8,128)(2,1)} async-done(((bf16[512,256]{1,0:T(8,128)(2,1)}), bf16[2048,256]{1,0:T(8,128)(2,1)}) %all-gather.3.cloned.1.call-update) | async-done | bytes 1048592 | tf_op jit(solution)/shard_map/all_gather | solution.py:87
  73.4 0.0 all-gather.5.cloned.1.call-update
  73.4 7.4 %collective-permute-start.9 = (bf16[128,512]{1,0:T(8,128)(2,1)S(1)}, bf16[128,512]{1,0:T(8,128)(2,1)S(1)}, u32[]{:S(2)}, u32[]{:S(2)}) collective-permute-start(bf16[128,512]{1,0:T(8,128)(2,1)S(1)} %get-tuple-element.52.refs_0_), channel_id=1, source_target_pairs={{0,1},{1,2},{2,3},{3,0},{4,5},{5,6},{6,7},{7,4},{8,9},{9,10},{10,1... | collective-permute-start | bytes 393224 | tf_op jit(solution)/shard_map/ppermute | solution.py:54
  80.8 1.9 %collective-permute-start.12 = (bf16[128,512]{1,0:T(8,128)(2,1)S(1)}, bf16[128,512]{1,0:T(8,128)(2,1)S(1)}, u32[]{:S(2)}, u32[]{:S(2)}) collective-permute-start(bf16[128,512]{1,0:T(8,128)(2,1)S(1)} %get-tuple-element.53.refs_1_), channel_id=1, source_target_pairs={{0,3},{1,0},{2,1},{3,2},{4,7},{5,4},{6,5},{7,6},{8,11},{9,8},{10,9... | collective-permute-start | bytes 393224 | tf_op jit(solution)/shard_map/ppermute | solution.py:54
  82.7 7.3 %collective-permute-start.10 = (bf16[128,512]{1,0:T(8,128)(2,1)S(1)}, bf16[128,512]{1,0:T(8,128)(2,1)S(1)}, u32[]{:S(2)}, u32[]{:S(2)}) collective-permute-start(bf16[128,512]{1,0:T(8,128)(2,1)S(1)} %get-tuple-element.53.refs_1_), channel_id=1, source_target_pairs={{0,1},{1,2},{2,3},{3,0},{4,5},{5,6},{6,7},{7,4},{8,9},{9,10},{10,1... | collective-permute-start | bytes 393224 | tf_op jit(solution)/shard_map/ppermute | solution.py:54
  90.0 1.9 %collective-permute-start.11 = (bf16[128,512]{1,0:T(8,128)(2,1)S(1)}, bf16[128,512]{1,0:T(8,128)(2,1)S(1)}, u32[]{:S(2)}, u32[]{:S(2)}) collective-permute-start(bf16[128,512]{1,0:T(8,128)(2,1)S(1)} %get-tuple-element.52.refs_0_), channel_id=1, source_target_pairs={{0,3},{1,0},{2,1},{3,2},{4,7},{5,4},{6,5},{7,6},{8,11},{9,8},{10,9... | collective-permute-start | bytes 393224 | tf_op jit(solution)/shard_map/ppermute | solution.py:54
  91.9 7.3 %collective-permute-start.13 = (bf16[128,512]{1,0:T(8,128)(2,1)S(1)}, bf16[128,512]{1,0:T(8,128)(2,1)S(1)}, u32[]{:S(2)}, u32[]{:S(2)}) collective-permute-start(bf16[128,512]{1,0:T(8,128)(2,1)S(1)} %collective-permute-done.9.refs_2_), channel_id=1, source_target_pairs={{0,1},{1,2},{2,3},{3,0},{4,5},{5,6},{6,7},{7,4},{8,9},{9,10},{10,1... | collective-permute-start | bytes 393224 | tf_op jit(solution)/shard_map/ppermute | solution.py:54
  99.2 5.0 %collective-permute-done.12.refs_5_ = bf16[128,512]{1,0:T(8,128)(2,1)S(1)} collective-permute-done((bf16[128,512]{1,0:T(8,128)(2,1)S(1)}, bf16[128,512]{1,0:T(8,128)(2,1)S(1)}, u32[]{:S(2)}, u32[]{:S(2)}) %collective-permute-start.12) | collective-permute-done | bytes 131104 | tf_op jit(solution)/shard_map/ppermute | solution.py:54
  104.3 2.3 %collective-permute-start.14 = (bf16[128,512]{1,0:T(8,128)(2,1)S(1)}, bf16[128,512]{1,0:T(8,128)(2,1)S(1)}, u32[]{:S(2)}, u32[]{:S(2)}) collective-permute-start(bf16[128,512]{1,0:T(8,128)(2,1)S(1)} %collective-permute-done.12.refs_5_), channel_id=1, source_target_pairs={{0,3},{1,0},{2,1},{3,2},{4,7},{5,4},{6,5},{7,6},{8,11},{9,8},{10,9... | collective-permute-start | bytes 393224 | tf_op jit(solution)/shard_map/ppermute | solution.py:54
  106.6 2.9 %collective-permute-done.10.refs_3_ = bf16[128,512]{1,0:T(8,128)(2,1)S(1)} collective-permute-done((bf16[128,512]{1,0:T(8,128)(2,1)S(1)}, bf16[128,512]{1,0:T(8,128)(2,1)S(1)}, u32[]{:S(2)}, u32[]{:S(2)}) %collective-permute-start.10) | collective-permute-done | bytes 131104 | tf_op jit(solution)/shard_map/ppermute | solution.py:54
  109.6 0.1 collective-permute-done.11.refs_4_
  109.7 7.1 %collective-permute-done.13.refs_6_ = bf16[128,512]{1,0:T(8,128)(2,1)S(1)} collective-permute-done((bf16[128,512]{1,0:T(8,128)(2,1)S(1)}, bf16[128,512]{1,0:T(8,128)(2,1)S(1)}, u32[]{:S(2)}, u32[]{:S(2)}) %collective-permute-start.13) | collective-permute-done | bytes 131104 | tf_op jit(solution)/shard_map/ppermute | solution.py:54
  116.8 2.5 %collective-permute-done.14.refs_7_ = bf16[128,512]{1,0:T(8,128)(2,1)S(1)} collective-permute-done((bf16[128,512]{1,0:T(8,128)(2,1)S(1)}, bf16[128,512]{1,0:T(8,128)(2,1)S(1)}, u32[]{:S(2)}, u32[]{:S(2)}) %collective-permute-start.14) | collective-permute-done | bytes 131104 | tf_op jit(solution)/shard_map/ppermute | solution.py:54
  119.3 0.7 copy-done.10
  120.0 1.2 shard_map.116
  121.2 11.5 %all-gather.5.cloned.1.call-done = bf16[16384,256]{1,0:T(8,128)(2,1)} async-done(((bf16[2048,256]{1,0:T(8,128)(2,1)}), bf16[16384,256]{1,0:T(8,128)(2,1)}) %all-gather.5.cloned.1.call-update) | async-done | bytes 8388624 | tf_op jit(solution)/shard_map/all_gather | solution.py:87
  132.7 1.9 %constant_dynamic-slice_fusion.weight = bf16[1,2,2048,256]{3,2,1,0:T(8,128)(2,1)S(1)} fusion(bf16[4,2,2048,256]{3,2,1,0:T(8,128)(2,1)} %bitcast.13, s32[]{:T(128)S(6)} %select_n.53), kind=kLoop, calls=%fused_computation.2 | loop fusion | bytes 4194308 | tf_op jit(solution)/shard_map/dynamic_slice | solution.py:461
  134.5 0.7 shard_map.118
  135.3 4.8 %collective-permute-start.15 = (bf16[272,512]{1,0:T(8,128)(2,1)S(1)}, bf16[272,512]{1,0:T(8,128)(2,1)S(1)}, u32[]{:S(2)}, u32[]{:S(2)}) collective-permute-start(bf16[272,512]{1,0:T(8,128)(2,1)S(1)} %shard_map.118), channel_id=1, source_target_pairs={{0,8},{1,9},{2,10},{3,11},{4,12},{5,13},{6,14},{7,15},{8,0},{9,1},... | collective-permute-start | bytes 835592 | tf_op jit(solution)/shard_map/ppermute | solution.py:54
  140.1 0.7 shard_map.119
  140.8 2.2 %collective-permute-start.16 = (bf16[272,512]{1,0:T(8,128)(2,1)S(1)}, bf16[272,512]{1,0:T(8,128)(2,1)S(1)}, u32[]{:S(2)}, u32[]{:S(2)}) collective-permute-start(bf16[272,512]{1,0:T(8,128)(2,1)S(1)} %shard_map.119), channel_id=1, source_target_pairs={{0,4},{1,5},{2,6},{3,7},{4,8},{5,9},{6,10},{7,11},{8,12},{9,13},{1... | collective-permute-start | bytes 835592 | tf_op jit(solution)/shard_map/ppermute | solution.py:54
  143.0 0.7 shard_map.120
  143.8 4.3 %collective-permute-start.17 = (bf16[272,512]{1,0:T(8,128)(2,1)S(1)}, bf16[272,512]{1,0:T(8,128)(2,1)S(1)}, u32[]{:S(2)}, u32[]{:S(2)}) collective-permute-start(bf16[272,512]{1,0:T(8,128)(2,1)S(1)} %shard_map.120), channel_id=1, source_target_pairs={{0,12},{1,13},{2,14},{3,15},{4,0},{5,1},{6,2},{7,3},{8,4},{9,5},{1... | collective-permute-start | bytes 835592 | tf_op jit(solution)/shard_map/ppermute | solution.py:54
  148.0 0.7 shard_map.117.own
  148.8 4.2 %collective-permute-done.16.got2 = bf16[272,512]{1,0:T(8,128)(2,1)S(1)} collective-permute-done((bf16[272,512]{1,0:T(8,128)(2,1)S(1)}, bf16[272,512]{1,0:T(8,128)(2,1)S(1)}, u32[]{:S(2)}, u32[]{:S(2)}) %collective-permute-start.16) | collective-permute-done | bytes 278560 | tf_op jit(solution)/shard_map/ppermute | solution.py:54
  153.0 0.2 collective-permute-done.17.got3
  153.2 0.9 shard_map.121
  (27 shorter events, 0.1 us)
Async XLA Ops:
  6.5 2.6 %copy-start = (bf16[2,128,8,128]{3,2,1,0:T(8,128)(2,1)S(1)}, bf16[2,128,8,128]{3,2,1,0:T(8,128)(2,1)}, u32[]{:S(2)}) copy-start(bf16[2,128,8,128]{3,2,1,0:T(8,128)(2,1)} %param.14) | copy-start | bytes 1572868
  6.5 66.9 %all-gather.3.cloned.1.call-start = ((), (), s32[]{:S(2)}) async-start(), calls=%async_computation | async-start | bytes 1310720 | tf_op jit(solution)/shard_map/all_gather | solution.py:87
  6.5 1.0 copy-start.3
  7.5 0.7 copy-start.7
  8.4 17.0 %collective-permute-start = (bf16[512,256]{1,0:T(8,128)(2,1)S(1)}, bf16[512,256]{1,0:T(8,128)(2,1)S(1)}, u32[]{:S(2)}, u32[]{:S(2)}) collective-permute-start(bf16[512,256]{1,0:T(8,128)(2,1)S(1)} %shard_map.109), channel_id=1, source_target_pairs={{0,0},{1,64},{2,96},{3,32},{4,4},{5,68},{6,100},{7,36},{8,8},{9,72... | collective-permute-start | bytes 786440 | tf_op jit(solution)/shard_map/ppermute | solution.py:54
  11.3 1.0 copy-start.1
  12.2 0.7 copy-start.5
  12.9 0.7 copy-start.8
  15.0 9.8 %collective-permute-start.1 = (bf16[528,128]{1,0:T(8,128)(2,1)S(1)}, bf16[528,128]{1,0:T(8,128)(2,1)S(1)}, u32[]{:S(2)}, u32[]{:S(2)}) collective-permute-start(bf16[528,128]{1,0:T(8,128)(2,1)S(1)} %get-tuple-element.31), channel_id=1, source_target_pairs={{0,16},{1,17},{2,18},{3,19},{4,20},{5,21},{6,22},{7,23},{8,24},{9,... | collective-permute-start | bytes 405512 | tf_op jit(solution)/shard_map/ppermute | solution.py:54
  25.4 0.7 copy-start.12
  26.1 106.5 %all-gather.5.cloned.1.call-start = ((), (), s32[]{:S(2)}) async-start(), calls=%async_computation.1 | async-start | bytes 9437184 | tf_op jit(solution)/shard_map/all_gather | solution.py:87
  26.2 24.9 %collective-permute-start.2 = (bf16[528,128]{1,0:T(8,128)(2,1)S(1)}, bf16[528,128]{1,0:T(8,128)(2,1)S(1)}, u32[]{:S(2)}, u32[]{:S(2)}) collective-permute-start(bf16[528,128]{1,0:T(8,128)(2,1)S(1)} %get-tuple-element.36.own), channel_id=1, source_target_pairs={{0,32},{1,33},{2,34},{3,35},{4,36},{5,37},{6,38},{7,39},{8,40},{9,... | collective-permute-start | bytes 405512 | tf_op jit(solution)/shard_map/ppermute | solution.py:54
  37.2 13.8 %collective-permute-start.3 = (bf16[528,128]{1,0:T(8,128)(2,1)S(1)}, bf16[528,128]{1,0:T(8,128)(2,1)S(1)}, u32[]{:S(2)}, u32[]{:S(2)}) collective-permute-start(bf16[528,128]{1,0:T(8,128)(2,1)S(1)} %get-tuple-element.36.own), channel_id=1, source_target_pairs={{0,64},{1,65},{2,66},{3,67},{4,68},{5,69},{6,70},{7,71},{8,72},{9,... | collective-permute-start | bytes 405512 | tf_op jit(solution)/shard_map/ppermute | solution.py:54
  41.5 9.6 %collective-permute-start.4 = (bf16[528,128]{1,0:T(8,128)(2,1)S(1)}, bf16[528,128]{1,0:T(8,128)(2,1)S(1)}, u32[]{:S(2)}, u32[]{:S(2)}) collective-permute-start(bf16[528,128]{1,0:T(8,128)(2,1)S(1)} %get-tuple-element.36.own), channel_id=1, source_target_pairs={{0,96},{1,97},{2,98},{3,99},{4,100},{5,101},{6,102},{7,103},{8,104... | collective-permute-start | bytes 405512 | tf_op jit(solution)/shard_map/ppermute | solution.py:54
  44.7 1.0 copy-start.2
  45.7 0.9 copy-start.4
  46.6 0.7 copy-start.6
  47.3 0.7 copy-start.9
  48.0 0.7 copy-start.11
  51.9 8.8 %collective-permute-start.5 = (bf16[528,128]{1,0:T(8,128)(2,1)S(1)}, bf16[528,128]{1,0:T(8,128)(2,1)S(1)}, u32[]{:S(2)}, u32[]{:S(2)}) collective-permute-start(bf16[528,128]{1,0:T(8,128)(2,1)S(1)} %get-tuple-element.41), channel_id=1, source_target_pairs={{0,128},{1,129},{2,130},{3,131},{4,132},{5,133},{6,134},{7,135},{8... | collective-permute-start | bytes 405512 | tf_op jit(solution)/shard_map/ppermute | solution.py:54
  55.0 6.3 %collective-permute-start.6 = (bf16[528,128]{1,0:T(8,128)(2,1)S(1)}, bf16[528,128]{1,0:T(8,128)(2,1)S(1)}, u32[]{:S(2)}, u32[]{:S(2)}) collective-permute-start(bf16[528,128]{1,0:T(8,128)(2,1)S(1)} %get-tuple-element.41), channel_id=1, source_target_pairs={{0,256},{1,257},{2,258},{3,259},{4,260},{5,261},{6,262},{7,263},{8... | collective-permute-start | bytes 405512 | tf_op jit(solution)/shard_map/ppermute | solution.py:54
  59.4 3.5 %collective-permute-start.7 = (bf16[528,128]{1,0:T(8,128)(2,1)S(1)}, bf16[528,128]{1,0:T(8,128)(2,1)S(1)}, u32[]{:S(2)}, u32[]{:S(2)}) collective-permute-start(bf16[528,128]{1,0:T(8,128)(2,1)S(1)} %get-tuple-element.41), channel_id=1, source_target_pairs={{0,384},{1,385},{2,386},{3,387},{4,388},{5,389},{6,390},{7,391},{8... | collective-permute-start | bytes 405512 | tf_op jit(solution)/shard_map/ppermute | solution.py:54
  63.6 4.9 %collective-permute-start.8 = (bf16[512,128]{1,0:T(8,128)(2,1)S(1)}, bf16[512,128]{1,0:T(8,128)(2,1)S(1)}, u32[]{:S(2)}, u32[]{:S(2)}) collective-permute-start(bf16[512,128]{1,0:T(8,128)(2,1)S(1)} %get-tuple-element.47), channel_id=1, source_target_pairs={{0,16},{1,17},{2,18},{3,19},{4,20},{5,21},{6,22},{7,23},{8,24},{9,... | collective-permute-start | bytes 393224 | tf_op jit(solution)/shard_map/ppermute | solution.py:54
  73.4 18.5 %collective-permute-start.9 = (bf16[128,512]{1,0:T(8,128)(2,1)S(1)}, bf16[128,512]{1,0:T(8,128)(2,1)S(1)}, u32[]{:S(2)}, u32[]{:S(2)}) collective-permute-start(bf16[128,512]{1,0:T(8,128)(2,1)S(1)} %get-tuple-element.52.refs_0_), channel_id=1, source_target_pairs={{0,1},{1,2},{2,3},{3,0},{4,5},{5,6},{6,7},{7,4},{8,9},{9,10},{10,1... | collective-permute-start | bytes 393224 | tf_op jit(solution)/shard_map/ppermute | solution.py:54
  80.8 23.5 %collective-permute-start.12 = (bf16[128,512]{1,0:T(8,128)(2,1)S(1)}, bf16[128,512]{1,0:T(8,128)(2,1)S(1)}, u32[]{:S(2)}, u32[]{:S(2)}) collective-permute-start(bf16[128,512]{1,0:T(8,128)(2,1)S(1)} %get-tuple-element.53.refs_1_), channel_id=1, source_target_pairs={{0,3},{1,0},{2,1},{3,2},{4,7},{5,4},{6,5},{7,6},{8,11},{9,8},{10,9... | collective-permute-start | bytes 393224 | tf_op jit(solution)/shard_map/ppermute | solution.py:54
  82.7 26.9 %collective-permute-start.10 = (bf16[128,512]{1,0:T(8,128)(2,1)S(1)}, bf16[128,512]{1,0:T(8,128)(2,1)S(1)}, u32[]{:S(2)}, u32[]{:S(2)}) collective-permute-start(bf16[128,512]{1,0:T(8,128)(2,1)S(1)} %get-tuple-element.53.refs_1_), channel_id=1, source_target_pairs={{0,1},{1,2},{2,3},{3,0},{4,5},{5,6},{6,7},{7,4},{8,9},{9,10},{10,1... | collective-permute-start | bytes 393224 | tf_op jit(solution)/shard_map/ppermute | solution.py:54
  90.0 19.7 %collective-permute-start.11 = (bf16[128,512]{1,0:T(8,128)(2,1)S(1)}, bf16[128,512]{1,0:T(8,128)(2,1)S(1)}, u32[]{:S(2)}, u32[]{:S(2)}) collective-permute-start(bf16[128,512]{1,0:T(8,128)(2,1)S(1)} %get-tuple-element.52.refs_0_), channel_id=1, source_target_pairs={{0,3},{1,0},{2,1},{3,2},{4,7},{5,4},{6,5},{7,6},{8,11},{9,8},{10,9... | collective-permute-start | bytes 393224 | tf_op jit(solution)/shard_map/ppermute | solution.py:54
  91.9 24.9 %collective-permute-start.13 = (bf16[128,512]{1,0:T(8,128)(2,1)S(1)}, bf16[128,512]{1,0:T(8,128)(2,1)S(1)}, u32[]{:S(2)}, u32[]{:S(2)}) collective-permute-start(bf16[128,512]{1,0:T(8,128)(2,1)S(1)} %collective-permute-done.9.refs_2_), channel_id=1, source_target_pairs={{0,1},{1,2},{2,3},{3,0},{4,5},{5,6},{6,7},{7,4},{8,9},{9,10},{10,1... | collective-permute-start | bytes 393224 | tf_op jit(solution)/shard_map/ppermute | solution.py:54
  104.3 15.1 %collective-permute-start.14 = (bf16[128,512]{1,0:T(8,128)(2,1)S(1)}, bf16[128,512]{1,0:T(8,128)(2,1)S(1)}, u32[]{:S(2)}, u32[]{:S(2)}) collective-permute-start(bf16[128,512]{1,0:T(8,128)(2,1)S(1)} %collective-permute-done.12.refs_5_), channel_id=1, source_target_pairs={{0,3},{1,0},{2,1},{3,2},{4,7},{5,4},{6,5},{7,6},{8,11},{9,8},{10,9... | collective-permute-start | bytes 393224 | tf_op jit(solution)/shard_map/ppermute | solution.py:54
  119.3 0.7 copy-start.10
  132.6 7.4 %slice-start = ((s8[8388608]{0:T(1024)(128)(4,1)}), s8[4194304]{0:T(1024)(128)(4,1)S(1)}, s32[]{:S(2)}) async-start(s8[8388608]{0:T(1024)(128)(4,1)} %bitcast.14), calls=%async_computation.2 | async-start | bytes 8388608
  134.5 5.5 %slice-start.1 = ((s8[8388608]{0:T(1024)(128)(4,1)}), s8[4194304]{0:T(1024)(128)(4,1)S(1)}, s32[]{:S(2)}) async-start(s8[8388608]{0:T(1024)(128)(4,1)} %bitcast.14), calls=%async_computation.3 | async-start | bytes 8388608
  135.3 13.5 %collective-permute-start.15 = (bf16[272,512]{1,0:T(8,128)(2,1)S(1)}, bf16[272,512]{1,0:T(8,128)(2,1)S(1)}, u32[]{:S(2)}, u32[]{:S(2)}) collective-permute-start(bf16[272,512]{1,0:T(8,128)(2,1)S(1)} %shard_map.118), channel_id=1, source_target_pairs={{0,8},{1,9},{2,10},{3,11},{4,12},{5,13},{6,14},{7,15},{8,0},{9,1},... | collective-permute-start | bytes 835592 | tf_op jit(solution)/shard_map/ppermute | solution.py:54
  140.8 12.2 %collective-permute-start.16 = (bf16[272,512]{1,0:T(8,128)(2,1)S(1)}, bf16[272,512]{1,0:T(8,128)(2,1)S(1)}, u32[]{:S(2)}, u32[]{:S(2)}) collective-permute-start(bf16[272,512]{1,0:T(8,128)(2,1)S(1)} %shard_map.119), channel_id=1, source_target_pairs={{0,4},{1,5},{2,6},{3,7},{4,8},{5,9},{6,10},{7,11},{8,12},{9,13},{1... | collective-permute-start | bytes 835592 | tf_op jit(solution)/shard_map/ppermute | solution.py:54
  143.8 9.4 %collective-permute-start.17 = (bf16[272,512]{1,0:T(8,128)(2,1)S(1)}, bf16[272,512]{1,0:T(8,128)(2,1)S(1)}, u32[]{:S(2)}, u32[]{:S(2)}) collective-permute-start(bf16[272,512]{1,0:T(8,128)(2,1)S(1)} %shard_map.120), channel_id=1, source_target_pairs={{0,12},{1,13},{2,14},{3,15},{4,0},{5,1},{6,2},{7,3},{8,4},{9,5},{1... | collective-permute-start | bytes 835592 | tf_op jit(solution)/shard_map/ppermute | solution.py:54
Sparse Core Ops, SparseCore 0:
  26.2 47.0 all-gather.2
  75.5 57.0 all-gather.4

commit v6 on v5

--- a/solution.py
+++ b/solution.py
@@ -417,6 +417,10 @@
         2**18,
         2**19,
     )
+    line_weight = gather(near, lambda x, zl, core: (x, core))
+    line_weight, crossing = lax.optimization_barrier((line_weight, crossing))
+    weight = gather(line_weight, lambda x, zl, core: zl)
+    weight = weight.reshape(NX, NCORE, NZH * WIDTH, WIDTH // 2)
     got = to_core(crossing)
 
     token_part = shape((SPAN, WIDTH), bf16)
@@ -428,11 +432,6 @@
         2**25,
         2**21,
     )
-    line_weight = gather(near, lambda x, zl, core: (x, core))
-    line_weight, first, second = lax.optimization_barrier((line_weight, first, second))
-    weight = gather(line_weight, lambda x, zl, core: zl)
-    weight = weight.reshape(NX, NCORE, NZH * WIDTH, WIDTH // 2)
-
     first_below, second_above = to_zh(first, 1), to_zh(second, NZH - 1)
     second_below, first_above = to_zh(second, 1), to_zh(first, NZH - 1)
     far = (to_zh(first_below, 1), to_zh(second_above, NZH - 1))

time: 163 us -> 163 us (level)
    ppermute x18, waiting for transfers between devices: 26.3 us -> 29.3 us  [send(): return lax.ppermute(value, ('seq', 'head'), route(move))]
    unnamed x30 -> x28, local copies, waits for them, and re-layouts: 9.25 us -> 8.6 us
  transfers between devices with their start and end apart: 20 -> 20, of which waited for: 13 -> 12; matrix products, arithmetic and copies ran while one was open for 1% -> 1% of each run, Pallas kernels for 6% -> 6%
where the time goes in v6:
time: 163 us; the launch traced here: 161 us
  starting transfers between devices  79.3 us (49%)
  waiting for transfers between devices  43.3 us (27%)
  between operations  13.9 us (9%)
  local copies, waits for them, and re-layouts  12.6 us (8%)
  Pallas kernels  11.8 us (7%)
    ppermute x18, starting transfers between devices, send(): return lax.ppermute(value, ('seq', 'head'), route(move))  79.3 us
    ppermute x18, waiting for transfers between devices, send(): return lax.ppermute(value, ('seq', 'head'), route(move))  29.3 us
    all_gather x2, waiting for transfers between devices, gather(): lax.all_gather(block, 'seq', axis=0, tiled=True, axis_index_groups=list(g...  13.9 us
    pallas_call x13, Pallas kernels, call(): pl.pallas_call(kernel, out_shape=outs, in_specs=specs, out_specs=jax.tree...  11.8 us
    unnamed x28, local copies, waits for them, and re-layouts  8.6 us
  transfers between devices with their start and end apart: 20, of which 12 were waited for; matrix products, arithmetic and copies ran while one was open for 1% of the time, Pallas kernels for 6%

profile of v6, /device:TPU:1, one launch (start us, length us, event | category | flops | bytes accessed | tf_op | source)
XLA Modules:
  0.0 160.9 jit_solution(18016076350577246385)
XLA Ops:
  6.5 1.0 copy-done.3
  7.6 0.7 copy-done.7
  8.2 0.1 shard_map.109
  8.4 0.7 collective-permute-start
  9.1 0.1 constant_dynamic-slice_fusion.1
  9.3 1.2 constant_dynamic-slice_fusion.2
  10.5 0.7 concatenate.3.meta
  11.3 0.0 copy-start.1
  11.3 0.9 copy-done.1
  12.2 0.7 copy-done.5
  12.9 0.7 copy-done.8
  13.6 1.4 shard_map.110
  15.0 8.8 %collective-permute-start.1 = (bf16[528,128]{1,0:T(8,128)(2,1)S(1)}, bf16[528,128]{1,0:T(8,128)(2,1)S(1)}, u32[]{:S(2)}, u32[]{:S(2)}) collective-permute-start(bf16[528,128]{1,0:T(8,128)(2,1)S(1)} %get-tuple-element.30), channel_id=1, source_target_pairs={{0,16},{1,17},{2,18},{3,19},{4,20},{5,21},{6,22},{7,23},{8,24},{9,... | collective-permute-start | bytes 405512 | tf_op jit(solution)/shard_map/ppermute | solution.py:54
  23.8 1.0 collective-permute-done.1.got
  24.8 0.6 shard_map.111
  25.4 0.0 copy-start.11
  25.4 0.7 copy-done.11
  26.1 0.0 all-gather.3.cloned.1.call-update
  26.1 0.0 all-gather.5.cloned.1.call-start
  26.2 11.0 %collective-permute-start.2 = (bf16[528,128]{1,0:T(8,128)(2,1)S(1)}, bf16[528,128]{1,0:T(8,128)(2,1)S(1)}, u32[]{:S(2)}, u32[]{:S(2)}) collective-permute-start(bf16[528,128]{1,0:T(8,128)(2,1)S(1)} %get-tuple-element.34.own), channel_id=1, source_target_pairs={{0,32},{1,33},{2,34},{3,35},{4,36},{5,37},{6,38},{7,39},{8,40},{9,... | collective-permute-start | bytes 405512 | tf_op jit(solution)/shard_map/ppermute | solution.py:54
  37.2 4.3 %collective-permute-start.3 = (bf16[528,128]{1,0:T(8,128)(2,1)S(1)}, bf16[528,128]{1,0:T(8,128)(2,1)S(1)}, u32[]{:S(2)}, u32[]{:S(2)}) collective-permute-start(bf16[528,128]{1,0:T(8,128)(2,1)S(1)} %get-tuple-element.34.own), channel_id=1, source_target_pairs={{0,64},{1,65},{2,66},{3,67},{4,68},{5,69},{6,70},{7,71},{8,72},{9,... | collective-permute-start | bytes 405512 | tf_op jit(solution)/shard_map/ppermute | solution.py:54
  41.5 3.2 %collective-permute-start.4 = (bf16[528,128]{1,0:T(8,128)(2,1)S(1)}, bf16[528,128]{1,0:T(8,128)(2,1)S(1)}, u32[]{:S(2)}, u32[]{:S(2)}) collective-permute-start(bf16[528,128]{1,0:T(8,128)(2,1)S(1)} %get-tuple-element.34.own), channel_id=1, source_target_pairs={{0,96},{1,97},{2,98},{3,99},{4,100},{5,101},{6,102},{7,103},{8,104... | collective-permute-start | bytes 405512 | tf_op jit(solution)/shard_map/ppermute | solution.py:54
  44.7 0.0 copy-start.2
  44.7 0.9 copy-done.2
  45.7 0.9 copy-done.4
  46.6 0.7 copy-done.6
  47.3 0.7 copy-done.10
  48.0 2.4 %shard_map.112 = (f32[2,128,512]{2,1,0:T(8,128)S(1)}, f32[2,128,512]{2,1,0:T(8,128)S(1)}) custom-call(s32[7]{0:T(128)S(1)} %concatenate.3.meta, f32[8]{0:T(128)S(1)} %copy-done.8, f32[8]{0:T(128)S(1)} %copy-done.10, bf16[2,128,512]{2,1,0:T(8,128)(2,1)S(1)} %copy-done.2, bf16[2,128,128]{2,1,0:T(8,128)(2,1)S(1)} %get-tuple-element.56.writes, ...), custom_call_target="tpu_custom_call" | custom-call | flops 67108864 | bytes 2097152 | tf_op jit(solution)/shard_map/pallas_call | solution.py:97
  50.4 0.8 shard_map.113
  51.2 3.1 %collective-permute-start.5 = (bf16[528,128]{1,0:T(8,128)(2,1)S(1)}, bf16[528,128]{1,0:T(8,128)(2,1)S(1)}, u32[]{:S(2)}, u32[]{:S(2)}) collective-permute-start(bf16[528,128]{1,0:T(8,128)(2,1)S(1)} %get-tuple-element.39), channel_id=1, source_target_pairs={{0,128},{1,129},{2,130},{3,131},{4,132},{5,133},{6,134},{7,135},{8... | collective-permute-start | bytes 405512 | tf_op jit(solution)/shard_map/ppermute | solution.py:54
  54.4 4.4 %collective-permute-start.6 = (bf16[528,128]{1,0:T(8,128)(2,1)S(1)}, bf16[528,128]{1,0:T(8,128)(2,1)S(1)}, u32[]{:S(2)}, u32[]{:S(2)}) collective-permute-start(bf16[528,128]{1,0:T(8,128)(2,1)S(1)} %get-tuple-element.39), channel_id=1, source_target_pairs={{0,256},{1,257},{2,258},{3,259},{4,260},{5,261},{6,262},{7,263},{8... | collective-permute-start | bytes 405512 | tf_op jit(solution)/shard_map/ppermute | solution.py:54
  58.7 1.3 collective-permute-start.7
  60.0 0.6 collective-permute-done.6.from2
  60.7 1.6 collective-permute-done.7.from3
  62.3 0.7 shard_map.114
  63.0 10.4 %all-gather.3.cloned.1.call-done = bf16[2048,256]{1,0:T(8,128)(2,1)} async-done(((bf16[512,256]{1,0:T(8,128)(2,1)}), bf16[2048,256]{1,0:T(8,128)(2,1)}) %all-gather.3.cloned.1.call-update) | async-done | bytes 1048592 | tf_op jit(solution)/shard_map/all_gather | solution.py:87
  73.4 0.0 all-gather.5.cloned.1.call-update
  73.4 2.8 %collective-permute-start.8 = (bf16[512,128]{1,0:T(8,128)(2,1)S(1)}, bf16[512,128]{1,0:T(8,128)(2,1)S(1)}, u32[]{:S(2)}, u32[]{:S(2)}) collective-permute-start(bf16[512,128]{1,0:T(8,128)(2,1)S(1)} %get-tuple-element.47), channel_id=1, source_target_pairs={{0,16},{1,17},{2,18},{3,19},{4,20},{5,21},{6,22},{7,23},{8,24},{9,... | collective-permute-start | bytes 393224 | tf_op jit(solution)/shard_map/ppermute | solution.py:54
  76.2 1.0 collective-permute-done.8.got
  77.2 0.8 shard_map.115
  78.0 7.4 %collective-permute-start.9 = (bf16[128,512]{1,0:T(8,128)(2,1)S(1)}, bf16[128,512]{1,0:T(8,128)(2,1)S(1)}, u32[]{:S(2)}, u32[]{:S(2)}) collective-permute-start(bf16[128,512]{1,0:T(8,128)(2,1)S(1)} %get-tuple-element.50.refs_0_), channel_id=1, source_target_pairs={{0,1},{1,2},{2,3},{3,0},{4,5},{5,6},{6,7},{7,4},{8,9},{9,10},{10,1... | collective-permute-start | bytes 393224 | tf_op jit(solution)/shard_map/ppermute | solution.py:54
  85.3 1.9 %collective-permute-start.12 = (bf16[128,512]{1,0:T(8,128)(2,1)S(1)}, bf16[128,512]{1,0:T(8,128)(2,1)S(1)}, u32[]{:S(2)}, u32[]{:S(2)}) collective-permute-start(bf16[128,512]{1,0:T(8,128)(2,1)S(1)} %get-tuple-element.51.refs_1_), channel_id=1, source_target_pairs={{0,3},{1,0},{2,1},{3,2},{4,7},{5,4},{6,5},{7,6},{8,11},{9,8},{10,9... | collective-permute-start | bytes 393224 | tf_op jit(solution)/shard_map/ppermute | solution.py:54
  87.3 7.3 %collective-permute-start.10 = (bf16[128,512]{1,0:T(8,128)(2,1)S(1)}, bf16[128,512]{1,0:T(8,128)(2,1)S(1)}, u32[]{:S(2)}, u32[]{:S(2)}) collective-permute-start(bf16[128,512]{1,0:T(8,128)(2,1)S(1)} %get-tuple-element.51.refs_1_), channel_id=1, source_target_pairs={{0,1},{1,2},{2,3},{3,0},{4,5},{5,6},{6,7},{7,4},{8,9},{9,10},{10,1... | collective-permute-start | bytes 393224 | tf_op jit(solution)/shard_map/ppermute | solution.py:54
  94.6 1.9 %collective-permute-start.11 = (bf16[128,512]{1,0:T(8,128)(2,1)S(1)}, bf16[128,512]{1,0:T(8,128)(2,1)S(1)}, u32[]{:S(2)}, u32[]{:S(2)}) collective-permute-start(bf16[128,512]{1,0:T(8,128)(2,1)S(1)} %get-tuple-element.50.refs_0_), channel_id=1, source_target_pairs={{0,3},{1,0},{2,1},{3,2},{4,7},{5,4},{6,5},{7,6},{8,11},{9,8},{10,9... | collective-permute-start | bytes 393224 | tf_op jit(solution)/shard_map/ppermute | solution.py:54
  96.5 7.3 %collective-permute-start.13 = (bf16[128,512]{1,0:T(8,128)(2,1)S(1)}, bf16[128,512]{1,0:T(8,128)(2,1)S(1)}, u32[]{:S(2)}, u32[]{:S(2)}) collective-permute-start(bf16[128,512]{1,0:T(8,128)(2,1)S(1)} %collective-permute-done.9.refs_2_), channel_id=1, source_target_pairs={{0,1},{1,2},{2,3},{3,0},{4,5},{5,6},{6,7},{7,4},{8,9},{9,10},{10,1... | collective-permute-start | bytes 393224 | tf_op jit(solution)/shard_map/ppermute | solution.py:54
  103.8 4.7 %collective-permute-done.12.refs_5_ = bf16[128,512]{1,0:T(8,128)(2,1)S(1)} collective-permute-done((bf16[128,512]{1,0:T(8,128)(2,1)S(1)}, bf16[128,512]{1,0:T(8,128)(2,1)S(1)}, u32[]{:S(2)}, u32[]{:S(2)}) %collective-permute-start.12) | collective-permute-done | bytes 131104 | tf_op jit(solution)/shard_map/ppermute | solution.py:54
  108.5 2.7 %collective-permute-start.14 = (bf16[128,512]{1,0:T(8,128)(2,1)S(1)}, bf16[128,512]{1,0:T(8,128)(2,1)S(1)}, u32[]{:S(2)}, u32[]{:S(2)}) collective-permute-start(bf16[128,512]{1,0:T(8,128)(2,1)S(1)} %collective-permute-done.12.refs_5_), channel_id=1, source_target_pairs={{0,3},{1,0},{2,1},{3,2},{4,7},{5,4},{6,5},{7,6},{8,11},{9,8},{10,9... | collective-permute-start | bytes 393224 | tf_op jit(solution)/shard_map/ppermute | solution.py:54
  111.3 2.8 %collective-permute-done.10.refs_3_ = bf16[128,512]{1,0:T(8,128)(2,1)S(1)} collective-permute-done((bf16[128,512]{1,0:T(8,128)(2,1)S(1)}, bf16[128,512]{1,0:T(8,128)(2,1)S(1)}, u32[]{:S(2)}, u32[]{:S(2)}) %collective-permute-start.10) | collective-permute-done | bytes 131104 | tf_op jit(solution)/shard_map/ppermute | solution.py:54
  114.1 7.5 %collective-permute-done.13.refs_6_ = bf16[128,512]{1,0:T(8,128)(2,1)S(1)} collective-permute-done((bf16[128,512]{1,0:T(8,128)(2,1)S(1)}, bf16[128,512]{1,0:T(8,128)(2,1)S(1)}, u32[]{:S(2)}, u32[]{:S(2)}) %collective-permute-start.13) | collective-permute-done | bytes 131104 | tf_op jit(solution)/shard_map/ppermute | solution.py:54
  121.7 5.6 %collective-permute-done.14.refs_7_ = bf16[128,512]{1,0:T(8,128)(2,1)S(1)} collective-permute-done((bf16[128,512]{1,0:T(8,128)(2,1)S(1)}, bf16[128,512]{1,0:T(8,128)(2,1)S(1)}, u32[]{:S(2)}, u32[]{:S(2)}) %collective-permute-start.14) | collective-permute-done | bytes 131104 | tf_op jit(solution)/shard_map/ppermute | solution.py:54
  127.3 0.7 copy-done.9
  128.0 1.2 shard_map.116
  129.2 3.5 %all-gather.5.cloned.1.call-done = bf16[16384,256]{1,0:T(8,128)(2,1)} async-done(((bf16[2048,256]{1,0:T(8,128)(2,1)}), bf16[16384,256]{1,0:T(8,128)(2,1)}) %all-gather.5.cloned.1.call-update) | async-done | bytes 8388624 | tf_op jit(solution)/shard_map/all_gather | solution.py:87
  132.7 1.9 %constant_dynamic-slice_fusion.weight = bf16[1,2,2048,256]{3,2,1,0:T(8,128)(2,1)S(1)} fusion(bf16[4,2,2048,256]{3,2,1,0:T(8,128)(2,1)} %bitcast.13, s32[]{:T(128)S(6)} %select_n.53), kind=kLoop, calls=%fused_computation.2 | loop fusion | bytes 4194308 | tf_op jit(solution)/shard_map/dynamic_slice | solution.py:460
  134.6 0.7 shard_map.118
  135.3 4.8 %collective-permute-start.15 = (bf16[272,512]{1,0:T(8,128)(2,1)S(1)}, bf16[272,512]{1,0:T(8,128)(2,1)S(1)}, u32[]{:S(2)}, u32[]{:S(2)}) collective-permute-start(bf16[272,512]{1,0:T(8,128)(2,1)S(1)} %shard_map.118), channel_id=1, source_target_pairs={{0,8},{1,9},{2,10},{3,11},{4,12},{5,13},{6,14},{7,15},{8,0},{9,1},... | collective-permute-start | bytes 835592 | tf_op jit(solution)/shard_map/ppermute | solution.py:54
  140.1 0.7 shard_map.119
  140.8 2.2 %collective-permute-start.16 = (bf16[272,512]{1,0:T(8,128)(2,1)S(1)}, bf16[272,512]{1,0:T(8,128)(2,1)S(1)}, u32[]{:S(2)}, u32[]{:S(2)}) collective-permute-start(bf16[272,512]{1,0:T(8,128)(2,1)S(1)} %shard_map.119), channel_id=1, source_target_pairs={{0,4},{1,5},{2,6},{3,7},{4,8},{5,9},{6,10},{7,11},{8,12},{9,13},{1... | collective-permute-start | bytes 835592 | tf_op jit(solution)/shard_map/ppermute | solution.py:54
  143.0 0.7 shard_map.120
  143.8 4.3 %collective-permute-start.17 = (bf16[272,512]{1,0:T(8,128)(2,1)S(1)}, bf16[272,512]{1,0:T(8,128)(2,1)S(1)}, u32[]{:S(2)}, u32[]{:S(2)}) collective-permute-start(bf16[272,512]{1,0:T(8,128)(2,1)S(1)} %shard_map.120), channel_id=1, source_target_pairs={{0,12},{1,13},{2,14},{3,15},{4,0},{5,1},{6,2},{7,3},{8,4},{9,5},{1... | collective-permute-start | bytes 835592 | tf_op jit(solution)/shard_map/ppermute | solution.py:54
  148.0 0.7 shard_map.117.own
  148.8 4.3 %collective-permute-done.16.got2 = bf16[272,512]{1,0:T(8,128)(2,1)S(1)} collective-permute-done((bf16[272,512]{1,0:T(8,128)(2,1)S(1)}, bf16[272,512]{1,0:T(8,128)(2,1)S(1)}, u32[]{:S(2)}, u32[]{:S(2)}) %collective-permute-start.16) | collective-permute-done | bytes 278560 | tf_op jit(solution)/shard_map/ppermute | solution.py:54
  153.0 0.1 collective-permute-done.17.got3
  153.2 0.9 shard_map.121
  (25 shorter events, 0.1 us)
Async XLA Ops:
  6.5 2.6 %copy-start = (bf16[2,128,8,128]{3,2,1,0:T(8,128)(2,1)S(1)}, bf16[2,128,8,128]{3,2,1,0:T(8,128)(2,1)}, u32[]{:S(2)}) copy-start(bf16[2,128,8,128]{3,2,1,0:T(8,128)(2,1)} %param.14) | copy-start | bytes 1572868
  6.5 66.9 %all-gather.3.cloned.1.call-start = ((), (), s32[]{:S(2)}) async-start(), calls=%async_computation | async-start | bytes 1310720 | tf_op jit(solution)/shard_map/all_gather | solution.py:87
  6.5 1.0 copy-start.3
  7.5 0.7 copy-start.7
  8.4 17.0 %collective-permute-start = (bf16[512,256]{1,0:T(8,128)(2,1)S(1)}, bf16[512,256]{1,0:T(8,128)(2,1)S(1)}, u32[]{:S(2)}, u32[]{:S(2)}) collective-permute-start(bf16[512,256]{1,0:T(8,128)(2,1)S(1)} %shard_map.109), channel_id=1, source_target_pairs={{0,0},{1,64},{2,96},{3,32},{4,4},{5,68},{6,100},{7,36},{8,8},{9,72... | collective-permute-start | bytes 786440 | tf_op jit(solution)/shard_map/ppermute | solution.py:54
  11.3 1.0 copy-start.1
  12.2 0.7 copy-start.5
  12.9 0.7 copy-start.8
  15.0 9.8 %collective-permute-start.1 = (bf16[528,128]{1,0:T(8,128)(2,1)S(1)}, bf16[528,128]{1,0:T(8,128)(2,1)S(1)}, u32[]{:S(2)}, u32[]{:S(2)}) collective-permute-start(bf16[528,128]{1,0:T(8,128)(2,1)S(1)} %get-tuple-element.30), channel_id=1, source_target_pairs={{0,16},{1,17},{2,18},{3,19},{4,20},{5,21},{6,22},{7,23},{8,24},{9,... | collective-permute-start | bytes 405512 | tf_op jit(solution)/shard_map/ppermute | solution.py:54
  25.4 0.7 copy-start.11
  26.1 106.5 %all-gather.5.cloned.1.call-start = ((), (), s32[]{:S(2)}) async-start(), calls=%async_computation.1 | async-start | bytes 9437184 | tf_op jit(solution)/shard_map/all_gather | solution.py:87
  26.2 24.2 %collective-permute-start.2 = (bf16[528,128]{1,0:T(8,128)(2,1)S(1)}, bf16[528,128]{1,0:T(8,128)(2,1)S(1)}, u32[]{:S(2)}, u32[]{:S(2)}) collective-permute-start(bf16[528,128]{1,0:T(8,128)(2,1)S(1)} %get-tuple-element.34.own), channel_id=1, source_target_pairs={{0,32},{1,33},{2,34},{3,35},{4,36},{5,37},{6,38},{7,39},{8,40},{9,... | collective-permute-start | bytes 405512 | tf_op jit(solution)/shard_map/ppermute | solution.py:54
  37.2 13.2 %collective-permute-start.3 = (bf16[528,128]{1,0:T(8,128)(2,1)S(1)}, bf16[528,128]{1,0:T(8,128)(2,1)S(1)}, u32[]{:S(2)}, u32[]{:S(2)}) collective-permute-start(bf16[528,128]{1,0:T(8,128)(2,1)S(1)} %get-tuple-element.34.own), channel_id=1, source_target_pairs={{0,64},{1,65},{2,66},{3,67},{4,68},{5,69},{6,70},{7,71},{8,72},{9,... | collective-permute-start | bytes 405512 | tf_op jit(solution)/shard_map/ppermute | solution.py:54
  41.5 8.9 %collective-permute-start.4 = (bf16[528,128]{1,0:T(8,128)(2,1)S(1)}, bf16[528,128]{1,0:T(8,128)(2,1)S(1)}, u32[]{:S(2)}, u32[]{:S(2)}) collective-permute-start(bf16[528,128]{1,0:T(8,128)(2,1)S(1)} %get-tuple-element.34.own), channel_id=1, source_target_pairs={{0,96},{1,97},{2,98},{3,99},{4,100},{5,101},{6,102},{7,103},{8,104... | collective-permute-start | bytes 405512 | tf_op jit(solution)/shard_map/ppermute | solution.py:54
  44.7 1.0 copy-start.2
  45.7 0.9 copy-start.4
  46.6 0.7 copy-start.6
  47.3 0.7 copy-start.10
  51.2 8.8 %collective-permute-start.5 = (bf16[528,128]{1,0:T(8,128)(2,1)S(1)}, bf16[528,128]{1,0:T(8,128)(2,1)S(1)}, u32[]{:S(2)}, u32[]{:S(2)}) collective-permute-start(bf16[528,128]{1,0:T(8,128)(2,1)S(1)} %get-tuple-element.39), channel_id=1, source_target_pairs={{0,128},{1,129},{2,130},{3,131},{4,132},{5,133},{6,134},{7,135},{8... | collective-permute-start | bytes 405512 | tf_op jit(solution)/shard_map/ppermute | solution.py:54
  54.4 6.3 %collective-permute-start.6 = (bf16[528,128]{1,0:T(8,128)(2,1)S(1)}, bf16[528,128]{1,0:T(8,128)(2,1)S(1)}, u32[]{:S(2)}, u32[]{:S(2)}) collective-permute-start(bf16[528,128]{1,0:T(8,128)(2,1)S(1)} %get-tuple-element.39), channel_id=1, source_target_pairs={{0,256},{1,257},{2,258},{3,259},{4,260},{5,261},{6,262},{7,263},{8... | collective-permute-start | bytes 405512 | tf_op jit(solution)/shard_map/ppermute | solution.py:54
  58.7 3.5 %collective-permute-start.7 = (bf16[528,128]{1,0:T(8,128)(2,1)S(1)}, bf16[528,128]{1,0:T(8,128)(2,1)S(1)}, u32[]{:S(2)}, u32[]{:S(2)}) collective-permute-start(bf16[528,128]{1,0:T(8,128)(2,1)S(1)} %get-tuple-element.39), channel_id=1, source_target_pairs={{0,384},{1,385},{2,386},{3,387},{4,388},{5,389},{6,390},{7,391},{8... | collective-permute-start | bytes 405512 | tf_op jit(solution)/shard_map/ppermute | solution.py:54
  73.4 3.8 %collective-permute-start.8 = (bf16[512,128]{1,0:T(8,128)(2,1)S(1)}, bf16[512,128]{1,0:T(8,128)(2,1)S(1)}, u32[]{:S(2)}, u32[]{:S(2)}) collective-permute-start(bf16[512,128]{1,0:T(8,128)(2,1)S(1)} %get-tuple-element.47), channel_id=1, source_target_pairs={{0,16},{1,17},{2,18},{3,19},{4,20},{5,21},{6,22},{7,23},{8,24},{9,... | collective-permute-start | bytes 393224 | tf_op jit(solution)/shard_map/ppermute | solution.py:54
  78.0 18.5 %collective-permute-start.9 = (bf16[128,512]{1,0:T(8,128)(2,1)S(1)}, bf16[128,512]{1,0:T(8,128)(2,1)S(1)}, u32[]{:S(2)}, u32[]{:S(2)}) collective-permute-start(bf16[128,512]{1,0:T(8,128)(2,1)S(1)} %get-tuple-element.50.refs_0_), channel_id=1, source_target_pairs={{0,1},{1,2},{2,3},{3,0},{4,5},{5,6},{6,7},{7,4},{8,9},{9,10},{10,1... | collective-permute-start | bytes 393224 | tf_op jit(solution)/shard_map/ppermute | solution.py:54
  85.3 23.2 %collective-permute-start.12 = (bf16[128,512]{1,0:T(8,128)(2,1)S(1)}, bf16[128,512]{1,0:T(8,128)(2,1)S(1)}, u32[]{:S(2)}, u32[]{:S(2)}) collective-permute-start(bf16[128,512]{1,0:T(8,128)(2,1)S(1)} %get-tuple-element.51.refs_1_), channel_id=1, source_target_pairs={{0,3},{1,0},{2,1},{3,2},{4,7},{5,4},{6,5},{7,6},{8,11},{9,8},{10,9... | collective-permute-start | bytes 393224 | tf_op jit(solution)/shard_map/ppermute | solution.py:54
  87.3 26.8 %collective-permute-start.10 = (bf16[128,512]{1,0:T(8,128)(2,1)S(1)}, bf16[128,512]{1,0:T(8,128)(2,1)S(1)}, u32[]{:S(2)}, u32[]{:S(2)}) collective-permute-start(bf16[128,512]{1,0:T(8,128)(2,1)S(1)} %get-tuple-element.51.refs_1_), channel_id=1, source_target_pairs={{0,1},{1,2},{2,3},{3,0},{4,5},{5,6},{6,7},{7,4},{8,9},{9,10},{10,1... | collective-permute-start | bytes 393224 | tf_op jit(solution)/shard_map/ppermute | solution.py:54
  94.6 19.6 %collective-permute-start.11 = (bf16[128,512]{1,0:T(8,128)(2,1)S(1)}, bf16[128,512]{1,0:T(8,128)(2,1)S(1)}, u32[]{:S(2)}, u32[]{:S(2)}) collective-permute-start(bf16[128,512]{1,0:T(8,128)(2,1)S(1)} %get-tuple-element.50.refs_0_), channel_id=1, source_target_pairs={{0,3},{1,0},{2,1},{3,2},{4,7},{5,4},{6,5},{7,6},{8,11},{9,8},{10,9... | collective-permute-start | bytes 393224 | tf_op jit(solution)/shard_map/ppermute | solution.py:54
  96.5 25.2 %collective-permute-start.13 = (bf16[128,512]{1,0:T(8,128)(2,1)S(1)}, bf16[128,512]{1,0:T(8,128)(2,1)S(1)}, u32[]{:S(2)}, u32[]{:S(2)}) collective-permute-start(bf16[128,512]{1,0:T(8,128)(2,1)S(1)} %collective-permute-done.9.refs_2_), channel_id=1, source_target_pairs={{0,1},{1,2},{2,3},{3,0},{4,5},{5,6},{6,7},{7,4},{8,9},{9,10},{10,1... | collective-permute-start | bytes 393224 | tf_op jit(solution)/shard_map/ppermute | solution.py:54
  108.5 18.8 %collective-permute-start.14 = (bf16[128,512]{1,0:T(8,128)(2,1)S(1)}, bf16[128,512]{1,0:T(8,128)(2,1)S(1)}, u32[]{:S(2)}, u32[]{:S(2)}) collective-permute-start(bf16[128,512]{1,0:T(8,128)(2,1)S(1)} %collective-permute-done.12.refs_5_), channel_id=1, source_target_pairs={{0,3},{1,0},{2,1},{3,2},{4,7},{5,4},{6,5},{7,6},{8,11},{9,8},{10,9... | collective-permute-start | bytes 393224 | tf_op jit(solution)/shard_map/ppermute | solution.py:54
  127.3 0.7 copy-start.9
  132.7 7.4 %slice-start = ((s8[8388608]{0:T(1024)(128)(4,1)}), s8[4194304]{0:T(1024)(128)(4,1)S(1)}, s32[]{:S(2)}) async-start(s8[8388608]{0:T(1024)(128)(4,1)} %bitcast.14), calls=%async_computation.2 | async-start | bytes 8388608
  134.5 5.5 %slice-start.1 = ((s8[8388608]{0:T(1024)(128)(4,1)}), s8[4194304]{0:T(1024)(128)(4,1)S(1)}, s32[]{:S(2)}) async-start(s8[8388608]{0:T(1024)(128)(4,1)} %bitcast.14), calls=%async_computation.3 | async-start | bytes 8388608
  135.3 13.5 %collective-permute-start.15 = (bf16[272,512]{1,0:T(8,128)(2,1)S(1)}, bf16[272,512]{1,0:T(8,128)(2,1)S(1)}, u32[]{:S(2)}, u32[]{:S(2)}) collective-permute-start(bf16[272,512]{1,0:T(8,128)(2,1)S(1)} %shard_map.118), channel_id=1, source_target_pairs={{0,8},{1,9},{2,10},{3,11},{4,12},{5,13},{6,14},{7,15},{8,0},{9,1},... | collective-permute-start | bytes 835592 | tf_op jit(solution)/shard_map/ppermute | solution.py:54
  140.8 12.2 %collective-permute-start.16 = (bf16[272,512]{1,0:T(8,128)(2,1)S(1)}, bf16[272,512]{1,0:T(8,128)(2,1)S(1)}, u32[]{:S(2)}, u32[]{:S(2)}) collective-permute-start(bf16[272,512]{1,0:T(8,128)(2,1)S(1)} %shard_map.119), channel_id=1, source_target_pairs={{0,4},{1,5},{2,6},{3,7},{4,8},{5,9},{6,10},{7,11},{8,12},{9,13},{1... | collective-permute-start | bytes 835592 | tf_op jit(solution)/shard_map/ppermute | solution.py:54
  143.8 9.4 %collective-permute-start.17 = (bf16[272,512]{1,0:T(8,128)(2,1)S(1)}, bf16[272,512]{1,0:T(8,128)(2,1)S(1)}, u32[]{:S(2)}, u32[]{:S(2)}) collective-permute-start(bf16[272,512]{1,0:T(8,128)(2,1)S(1)} %shard_map.120), channel_id=1, source_target_pairs={{0,12},{1,13},{2,14},{3,15},{4,0},{5,1},{6,2},{7,3},{8,4},{9,5},{1... | collective-permute-start | bytes 835592 | tf_op jit(solution)/shard_map/ppermute | solution.py:54
Sparse Core Ops, SparseCore 0:
  26.2 47.0 all-gather.2
  75.5 57.0 all-gather.4
